TPU v7x, 32 devices: a whole 2x2x4 slice. The times are simulated.
32 devices in a mesh: items: 16 (over z, x, core), seq: 2 (over y).
Axes of the slice: x: 2, y: 2, z: 4, core: 2. Of those that a mesh axis runs over, the one named last changes fastest.
Arguments:
- tokens: bfloat16 [64, 2, 128, 768], P('items', 'seq'), may hold values from -6 to 6
- visible: int32 [64, 2, 128], P('items', 'seq'), may hold values from 0 to 587, as said below
- lengths: int32 [64], P('items'), may hold values from 59 to 235, as said below
- first_gain: bfloat16 [768], P(('items', 'seq')), may hold values from 0.5 to 1.5
- first_shift: bfloat16 [768], P(('items', 'seq')), may hold values from -1.5 to 1.5
- input_weight: bfloat16 [768, 2304], P(('items', 'seq')), may hold values from -0.21875 to 0.21875
- query_bias: bfloat16 [768], P(('items', 'seq')), may hold values from -1.5 to 1.5
- value_bias: bfloat16 [768], P(('items', 'seq')), may hold values from -1.5 to 1.5
- output_weight: bfloat16 [768, 768], P(('items', 'seq')), may hold values from -1.75 to 1.75
- output_bias: bfloat16 [768], P(('items', 'seq')), may hold values from -1.5 to 1.5
- second_gain: bfloat16 [768], P(('items', 'seq')), may hold values from 0.5 to 1.5
- second_shift: bfloat16 [768], P(('items', 'seq')), may hold values from -1.5 to 1.5
- expand_weight: bfloat16 [768, 3072], P(('items', 'seq')), may hold values from -0.21875 to 0.21875
- expand_bias: bfloat16 [3072], P(('items', 'seq')), may hold values from -1.5 to 1.5
- reduce_weight: bfloat16 [3072, 768], P(('items', 'seq')), may hold values from -0.109375 to 0.109375
- reduce_bias: bfloat16 [768], P(('items', 'seq')), may hold values from -1.5 to 1.5
- cotangent: bfloat16 [64, 2, 128, 768], P('items', 'seq'), may hold values from -6 to 6
Outputs:
- layer_out: bfloat16 [64, 2, 128, 768], P('items', 'seq')
- tokens_grad: float32 [64, 2, 128, 768], P('items', 'seq')
- first_gain_grad: float32 [768], P(('items', 'seq'))
- first_shift_grad: float32 [768], P(('items', 'seq'))
- input_weight_grad: float32 [768, 2304], P(('items', 'seq'))
- query_bias_grad: float32 [768], P(('items', 'seq'))
- value_bias_grad: float32 [768], P(('items', 'seq'))
- output_weight_grad: float32 [768, 768], P(('items', 'seq'))
- output_bias_grad: float32 [768], P(('items', 'seq'))
- second_gain_grad: float32 [768], P(('items', 'seq'))
- second_shift_grad: float32 [768], P(('items', 'seq'))
- expand_weight_grad: float32 [768, 3072], P(('items', 'seq'))
- expand_bias_grad: float32 [3072], P(('items', 'seq'))
- reduce_weight_grad: float32 [3072, 768], P(('items', 'seq'))
- reduce_bias_grad: float32 [768], P(('items', 'seq'))
Inputs may be any that keep to these rules, and one draw needn't show every extreme that they name: `lengths`: the count of visible tokens of each item; some item has exactly 235, another exactly 59. For an item with n visible tokens: its distinct visible patch numbers in ascending order, the first (n + 1) // 2 in block 0 and the other n // 2 in block 1, from slot 0 on; the remaining slots hold 0.
All inputs are finite; a program needn't handle non-finite values.
Results may differ from a plain program's by a relative error of at most 0.0099.
Values may be sent and summed in bfloat16 or wider, within the bound.
A program may use at most 192 MiB of HBM per device.

v0:
```python
import jax
import jax.numpy as jnp
from jax import lax
from jax.sharding import PartitionSpec as P

HD = 64
GRID = 14
MICRO = 2
ITEMS_MB = 2


EPSILON = 1e-06
SCORE_SCALE = 0.125


def layer_norm(rows_in, gain, shift):
    centre = rows_in - jnp.mean(rows_in, axis=-1, keepdims=True)
    spread = jnp.mean(centre * centre, axis=-1, keepdims=True)
    return centre * lax.rsqrt(spread + EPSILON) * gain + shift


def gelu_exact(value_in):
    return jax.nn.gelu(value_in, approximate=False)


def positions(index, model_width):
    channel = jnp.arange(model_width)
    portion = 3 * channel // model_width
    frequency = jnp.power(10000.0, -(channel % 256 // 2).astype(jnp.float32) / 128.0)
    which_frame = index // (GRID * GRID)
    which_row = index % (GRID * GRID) // GRID
    which_column = index % GRID
    coordinate = jnp.where(
        portion == 0,
        which_frame[..., None],
        jnp.where(portion == 1, which_row[..., None], which_column[..., None]),
    )
    angle = coordinate.astype(jnp.float32) * frequency
    return jnp.where(channel % 2 == 0, jnp.sin(angle), jnp.cos(angle))


def contract_rows(left, right):
    return lax.dot_general(
        left, right, (((0,), (0,)), ((), ())), preferred_element_type=jnp.float32
    )


def against(left, right):
    return lax.dot_general(
        left, right, (((1,), (1,)), ((), ())), preferred_element_type=jnp.float32
    )


def row_masks(lengths, block_rows, block_number):
    counts = (lengths + 1 - block_number) // 2
    return jnp.arange(block_rows)[None, :] < counts[:, None]


def micro_batch(gathered, tokens, visible, lengths, cotangent, seq_place):
    (
        first_gain,
        first_shift,
        input_weight,
        query_bias,
        value_bias,
        output_weight,
        output_bias,
        second_gain,
        second_shift,
        expand_weight,
        expand_bias,
        reduce_weight,
        reduce_bias,
    ) = gathered
    item_count, block_rows, model_width = tokens.shape
    head_count = model_width // HD
    total_rows = item_count * block_rows
    (
        first_gain,
        first_shift,
        query_bias,
        value_bias,
        output_bias,
        second_gain,
        second_shift,
        expand_bias,
        reduce_bias,
    ) = (
        vector.astype(jnp.float32)
        for vector in (
            first_gain,
            first_shift,
            query_bias,
            value_bias,
            output_bias,
            second_gain,
            second_shift,
            expand_bias,
            reduce_bias,
        )
    )
    query_live = row_masks(lengths, block_rows, seq_place).reshape(total_rows, 1)
    key_live = jnp.concatenate(
        [row_masks(lengths, block_rows, 0), row_masks(lengths, block_rows, 1)], axis=1
    )
    key_mask = key_live[:, None, None, :]
    entry = tokens.reshape(total_rows, model_width).astype(jnp.float32) + positions(
        visible.reshape(total_rows), model_width
    )
    normed, first_pull = jax.vjp(layer_norm, entry, first_gain, first_shift)
    normed_low = normed.astype(jnp.bfloat16)
    joined_bias = jnp.concatenate([query_bias, jnp.zeros_like(query_bias), value_bias])
    projected = (
        jnp.dot(normed_low, input_weight, preferred_element_type=jnp.float32) + joined_bias
    ).astype(jnp.bfloat16)
    queries = projected[:, :model_width].reshape(item_count, block_rows, head_count, HD)
    keys_here = projected[:, model_width : 2 * model_width].reshape(
        item_count, block_rows, model_width
    )
    values_here = projected[:, 2 * model_width :].reshape(item_count, block_rows, model_width)
    keys_all, values_all = (
        lax.all_gather(keys_here, "seq", axis=1, tiled=True),
        lax.all_gather(values_here, "seq", axis=1, tiled=True),
    )
    keys_all = keys_all.reshape(item_count, 2 * block_rows, head_count, HD)
    values_all = values_all.reshape(item_count, 2 * block_rows, head_count, HD)
    scores = (
        jnp.einsum("cqhd,ckhd->chqk", queries, keys_all, preferred_element_type=jnp.float32)
        * SCORE_SCALE
    )
    scores = jnp.where(key_mask, scores, -1e30)
    row_max = jnp.max(scores, axis=-1, keepdims=True)
    exponent = jnp.exp(scores - row_max)
    row_total = jnp.sum(exponent, axis=-1, keepdims=True)
    attention_low = (exponent / row_total).astype(jnp.bfloat16)
    log_total = row_max + jnp.log(row_total)
    attended = jnp.einsum(
        "chqk,ckhd->cqhd", attention_low, values_all, preferred_element_type=jnp.float32
    )
    attended = attended.reshape(total_rows, model_width).astype(jnp.bfloat16)
    middle = (
        entry + jnp.dot(attended, output_weight, preferred_element_type=jnp.float32) + output_bias
    )
    second, second_pull = jax.vjp(layer_norm, middle, second_gain, second_shift)
    second_low = second.astype(jnp.bfloat16)
    expanded = jnp.dot(second_low, expand_weight, preferred_element_type=jnp.float32) + expand_bias
    activated, gelu_pull = jax.vjp(gelu_exact, expanded)
    activated_low = activated.astype(jnp.bfloat16)
    result = (
        middle
        + jnp.dot(activated_low, reduce_weight, preferred_element_type=jnp.float32)
        + reduce_bias
    )
    layer_out = jnp.where(query_live, result, 0.0).astype(jnp.bfloat16)
    incoming = jnp.where(
        query_live, cotangent.reshape(total_rows, model_width).astype(jnp.float32), 0.0
    )
    incoming_low = incoming.astype(jnp.bfloat16)
    reduce_weight_grad = contract_rows(activated_low, incoming_low)
    reduce_bias_grad = jnp.sum(incoming, axis=0)
    activated_grad = against(incoming_low, reduce_weight)
    expanded_grad = gelu_pull(activated_grad)[0].astype(jnp.bfloat16)
    expand_weight_grad = contract_rows(second_low, expanded_grad)
    expand_bias_grad = jnp.sum(expanded_grad.astype(jnp.float32), axis=0)
    second_grad = against(expanded_grad, expand_weight)
    middle_part, second_gain_grad, second_shift_grad = second_pull(second_grad)
    middle_grad = incoming + middle_part
    branch_grad = middle_grad.astype(jnp.bfloat16)
    output_weight_grad = contract_rows(attended, branch_grad)
    output_bias_grad = jnp.sum(branch_grad.astype(jnp.float32), axis=0)
    attended_grad = against(branch_grad, output_weight).astype(jnp.bfloat16)
    attended_grad = attended_grad.reshape(item_count, block_rows, head_count, HD)
    scores = (
        jnp.einsum("cqhd,ckhd->chqk", queries, keys_all, preferred_element_type=jnp.float32)
        * SCORE_SCALE
    )
    scores = jnp.where(key_mask, scores, -1e30)
    attention_full = jnp.exp(scores - log_total)
    attention_low = attention_full.astype(jnp.bfloat16)
    weight_grad = jnp.einsum(
        "cqhd,ckhd->chqk", attended_grad, values_all, preferred_element_type=jnp.float32
    )
    row_inner = jnp.sum(attention_full * weight_grad, axis=-1, keepdims=True)
    scores_grad = (attention_full * (weight_grad - row_inner)).astype(jnp.bfloat16)
    query_grad = (
        jnp.einsum("chqk,ckhd->cqhd", scores_grad, keys_all, preferred_element_type=jnp.float32)
        * SCORE_SCALE
    )
    key_terms = (
        jnp.einsum("chqk,cqhd->ckhd", scores_grad, queries, preferred_element_type=jnp.float32)
        * SCORE_SCALE
    )
    value_terms = jnp.einsum(
        "chqk,cqhd->ckhd", attention_low, attended_grad, preferred_element_type=jnp.float32
    )
    key_grad, value_grad = (
        lax.psum_scatter(
            key_terms.reshape(item_count, 2 * block_rows, model_width).astype(jnp.bfloat16),
            "seq",
            scatter_dimension=1,
            tiled=True,
        ).astype(jnp.float32),
        lax.psum_scatter(
            value_terms.reshape(item_count, 2 * block_rows, model_width).astype(jnp.bfloat16),
            "seq",
            scatter_dimension=1,
            tiled=True,
        ).astype(jnp.float32),
    )
    projected_grad = jnp.concatenate(
        [
            query_grad.reshape(total_rows, model_width),
            key_grad.reshape(total_rows, model_width),
            value_grad.reshape(total_rows, model_width),
        ],
        axis=1,
    ).astype(jnp.bfloat16)
    input_weight_grad = contract_rows(normed_low, projected_grad)
    projected_sums = jnp.sum(projected_grad.astype(jnp.float32), axis=0)
    query_bias_grad = projected_sums[:model_width]
    value_bias_grad = projected_sums[2 * model_width :]
    normed_grad = against(projected_grad, input_weight)
    entry_part, first_gain_grad, first_shift_grad = first_pull(normed_grad)
    tokens_grad = middle_grad + entry_part
    grads = (
        first_gain_grad,
        first_shift_grad,
        input_weight_grad,
        query_bias_grad,
        value_bias_grad,
        output_weight_grad,
        output_bias_grad,
        second_gain_grad,
        second_shift_grad,
        expand_weight_grad,
        expand_bias_grad,
        reduce_weight_grad,
        reduce_bias_grad,
    )
    return (layer_out, tokens_grad, grads)


def body(
    tokens,
    visible,
    lengths,
    first_gain,
    first_shift,
    input_weight,
    query_bias,
    value_bias,
    output_weight,
    output_bias,
    second_gain,
    second_shift,
    expand_weight,
    expand_bias,
    reduce_weight,
    reduce_bias,
    cotangent,
):
    shards = (
        first_gain,
        first_shift,
        input_weight,
        query_bias,
        value_bias,
        output_weight,
        output_bias,
        second_gain,
        second_shift,
        expand_weight,
        expand_bias,
        reduce_weight,
        reduce_bias,
    )
    seq_place = lax.axis_index("seq")
    block_rows = tokens.shape[2]
    model_width = tokens.shape[3]
    outputs_list = []
    gradients_list = []
    totals = None
    for micro_index in range(MICRO):
        first_item = micro_index * ITEMS_MB
        last_item = first_item + ITEMS_MB
        gathered = (
            lax.all_gather(shards[0], ("items", "seq"), axis=0, tiled=True),
            lax.all_gather(shards[1], ("items", "seq"), axis=0, tiled=True),
            lax.all_gather(shards[2], ("items", "seq"), axis=0, tiled=True),
            lax.all_gather(shards[3], ("items", "seq"), axis=0, tiled=True),
            lax.all_gather(shards[4], ("items", "seq"), axis=0, tiled=True),
            lax.all_gather(shards[5], ("items", "seq"), axis=0, tiled=True),
            lax.all_gather(shards[6], ("items", "seq"), axis=0, tiled=True),
            lax.all_gather(shards[7], ("items", "seq"), axis=0, tiled=True),
            lax.all_gather(shards[8], ("items", "seq"), axis=0, tiled=True),
            lax.all_gather(shards[9], ("items", "seq"), axis=0, tiled=True),
            lax.all_gather(shards[10], ("items", "seq"), axis=0, tiled=True),
            lax.all_gather(shards[11], ("items", "seq"), axis=0, tiled=True),
            lax.all_gather(shards[12], ("items", "seq"), axis=0, tiled=True),
        )
        layer_out, tokens_grad, grads = micro_batch(
            gathered,
            tokens[first_item:last_item, 0],
            visible[first_item:last_item, 0],
            lengths[first_item:last_item],
            cotangent[first_item:last_item, 0],
            seq_place,
        )
        outputs_list.append(layer_out)
        gradients_list.append(tokens_grad)
        shares = (
            lax.psum_scatter(grads[0], ("items", "seq"), scatter_dimension=0, tiled=True),
            lax.psum_scatter(grads[1], ("items", "seq"), scatter_dimension=0, tiled=True),
            lax.psum_scatter(grads[2], ("items", "seq"), scatter_dimension=0, tiled=True),
            lax.psum_scatter(grads[3], ("items", "seq"), scatter_dimension=0, tiled=True),
            lax.psum_scatter(grads[4], ("items", "seq"), scatter_dimension=0, tiled=True),
            lax.psum_scatter(grads[5], ("items", "seq"), scatter_dimension=0, tiled=True),
            lax.psum_scatter(grads[6], ("items", "seq"), scatter_dimension=0, tiled=True),
            lax.psum_scatter(grads[7], ("items", "seq"), scatter_dimension=0, tiled=True),
            lax.psum_scatter(grads[8], ("items", "seq"), scatter_dimension=0, tiled=True),
            lax.psum_scatter(grads[9], ("items", "seq"), scatter_dimension=0, tiled=True),
            lax.psum_scatter(grads[10], ("items", "seq"), scatter_dimension=0, tiled=True),
            lax.psum_scatter(grads[11], ("items", "seq"), scatter_dimension=0, tiled=True),
            lax.psum_scatter(grads[12], ("items", "seq"), scatter_dimension=0, tiled=True),
        )
        totals = (
            shares
            if totals is None
            else tuple((earlier + later for earlier, later in zip(totals, shares)))
        )
    item_count = tokens.shape[0]
    layer_out = jnp.concatenate(outputs_list, axis=0).reshape(
        item_count, 1, block_rows, model_width
    )
    tokens_grad = jnp.concatenate(gradients_list, axis=0).reshape(
        item_count, 1, block_rows, model_width
    )
    return (
        layer_out,
        tokens_grad,
        totals[0],
        totals[1],
        totals[2],
        totals[3],
        totals[4],
        totals[5],
        totals[6],
        totals[7],
        totals[8],
        totals[9],
        totals[10],
        totals[11],
        totals[12],
    )


def solution(mesh):
    in_specs = (
        P("items", "seq", None, None),
        P("items", "seq", None),
        P("items"),
        P(("items", "seq")),
        P(("items", "seq")),
        P(("items", "seq"), None),
        P(("items", "seq")),
        P(("items", "seq")),
        P(("items", "seq"), None),
        P(("items", "seq")),
        P(("items", "seq")),
        P(("items", "seq")),
        P(("items", "seq"), None),
        P(("items", "seq")),
        P(("items", "seq"), None),
        P(("items", "seq")),
        P("items", "seq", None, None),
    )
    out_specs = (
        P("items", "seq", None, None),
        P("items", "seq", None, None),
        P(("items", "seq")),
        P(("items", "seq")),
        P(("items", "seq"), None),
        P(("items", "seq")),
        P(("items", "seq")),
        P(("items", "seq"), None),
        P(("items", "seq")),
        P(("items", "seq")),
        P(("items", "seq")),
        P(("items", "seq"), None),
        P(("items", "seq")),
        P(("items", "seq"), None),
        P(("items", "seq")),
    )
    return jax.shard_map(body, mesh=mesh, in_specs=in_specs, out_specs=out_specs, check_vma=False)
```

profile of v0, /device:TPU:0, one launch (start us, length us, event | category | flops | bytes accessed | tf_op | source)
XLA Modules:
  0.0 953.4 jit_solution(12207761035186075691)
XLA Ops:
  17.6 42.6 %all-reduce.19 = (bf16[768]{0:T(1024)(128)(2,1)S(1)}, bf16[768]{0:T(1024)(128)(2,1)S(1)}, bf16[768]{0:T(1024)(128)(2,1)S(1)}, bf16[768]{0:T(1024)(128)(2,1)S(1)}...) all-reduce(bf16[768]{0:T(1024)(128)(2,1)S(1)} %dynamic-update-slice, ...), channel_id=1, replica_groups=mesh['items'=16,'seq'=2] {'items','seq'}, use_global_device_ids=true, to_apply=%add.4 | all-reduce | flops 9216 | bytes 36864
  61.5 1.3 and_select_fusion.17
  65.2 4.2 fusion.50
  69.4 7.9 multiply_reduce_fusion.13
  78.4 1.3 fusion.89
  80.6 3.0 bitcast_add_fusion.1
  83.8 3.3 fusion
  87.5 10.9 %all_gather.70 = bf16[2,256,768]{2,1,0:T(8,128)(2,1)S(1)} all-gather(bf16[2,128,768]{2,1,0:T(8,128)(2,1)S(1)} %bitcast.284), channel_id=1, replica_groups=mesh['items'=16,'seq'=2] {'seq'}, dimensions={1}, use_global_device_ids=true | all-gather | bytes 1179648 | tf_op jit(solution)/shard_map/all_gather | solution.py:122
  99.5 10.8 %all_gather.69 = bf16[2,256,768]{2,1,0:T(8,128)(2,1)S(1)} all-gather(bf16[2,128,768]{2,1,0:T(8,128)(2,1)S(1)} %bitcast.282), channel_id=1, replica_groups=mesh['items'=16,'seq'=2] {'seq'}, dimensions={1}, use_global_device_ids=true | all-gather | bytes 1179648 | tf_op jit(solution)/shard_map/all_gather | solution.py:123
  111.5 2.0 fusion.113
  115.0 1.6 fusion.44
  117.0 13.1 %all-gather.7.cloned.1.call-done = bf16[768,768]{1,0:T(8,128)(2,1)} async-done(((bf16[24,768]{1,0:T(8,128)(2,1)}), bf16[768,768]{1,0:T(8,128)(2,1)}) %all-gather.7.cloned.1.call-update) | async-done | bytes 1179664 | tf_op jit(solution)/shard_map/all_gather | solution.py:292
  130.2 2.1 fusion.114
  134.7 61.1 %all-gather.9.cloned.1.call-done = bf16[768,3072]{1,0:T(8,128)(2,1)} async-done(((bf16[24,3072]{1,0:T(8,128)(2,1)}), bf16[768,3072]{1,0:T(8,128)(2,1)}) %all-gather.9.cloned.1.call-update) | async-done | bytes 4718608 | tf_op jit(solution)/shard_map/all_gather | solution.py:296
  195.7 5.8 convolution_add_fusion.6
  201.5 59.5 %all-gather.11.cloned.1.call-done = bf16[3072,768]{1,0:T(8,128)(2,1)} async-done(((bf16[96,768]{1,0:T(8,128)(2,1)}), bf16[3072,768]{1,0:T(8,128)(2,1)}) %all-gather.11.cloned.1.call-update) | async-done | bytes 4718608 | tf_op jit(solution)/shard_map/all_gather | solution.py:298
  261.0 12.3 %convert_reduce_fusion.1 = (f32[3072]{0:T(1024)}, bf16[256,3072]{1,0:T(8,128)(2,1)S(1)}, f32[256,3072]{1,0:T(8,128)}) fusion(f32[256,3072]{1,0:T(8,128)} %convolution_add_fusion.6, bf16[256,768]{1,0:T(8,128)(2,1)} %fusion.48, bf16[3072,768]{1,0:T(8,128)(2,1)} %all-gather.11.cloned.1.call-done), kind=kOutput, calls=%fused_computation.14 | convolution fusion | flops 1266152448 | bytes 12988416 | tf_op jit(solution)/shard_map/dot_general | solution.py:49
  273.4 2.1 multiply_reduce_fusion.3
  275.9 1.6 convert_reduce_fusion.5
  280.8 2.4 fusion.26
  283.2 2.3 copy.107
  285.6 2.7 multiply_reduce_fusion.1
  291.0 1.2 copy.105
  293.1 4.3 multiply_reduce_fusion.11
  298.7 3.3 reduce-scatter.11.cloned.1.call-done
  301.9 1.2 copy.109
  303.1 18.5 %reduce-scatter.9.cloned.1.call-done = bf16[2,128,768]{2,1,0:T(8,128)(2,1)} async-done(((bf16[2,256,768]{2,1,0:T(8,128)(2,1)}), bf16[2,128,768]{2,1,0:T(8,128)(2,1)}) %reduce-scatter.9.cloned.1.call-update) | async-done | bytes 393232 | tf_op jit(solution)/shard_map/reduce_scatter | solution.py:197
  321.6 1.2 copy.108
  322.9 7.1 multiply_reduce_fusion.5
  330.0 6.6 fusion.106
  337.2 1.2 fusion.1
  338.8 11.5 %all_gather.80 = bf16[2,256,768]{2,1,0:T(8,128)(2,1)S(1)} all-gather(bf16[2,128,768]{2,1,0:T(8,128)(2,1)S(1)} %bitcast.285), channel_id=1, replica_groups=mesh['items'=16,'seq'=2] {'seq'}, dimensions={1}, use_global_device_ids=true | all-gather | bytes 1179648 | tf_op jit(solution)/shard_map/all_gather | solution.py:122
  350.4 1.2 copy.98
  351.5 10.7 %all_gather.79 = bf16[2,256,768]{2,1,0:T(8,128)(2,1)S(1)} all-gather(bf16[2,128,768]{2,1,0:T(8,128)(2,1)S(1)} %bitcast.283), channel_id=1, replica_groups=mesh['items'=16,'seq'=2] {'seq'}, dimensions={1}, use_global_device_ids=true | all-gather | bytes 1179648 | tf_op jit(solution)/shard_map/all_gather | solution.py:123
  363.3 2.0 fusion.115
  366.9 1.6 fusion.45
  369.9 1.5 convolution_add_fusion.5
  371.8 10.4 %convert_reduce_fusion = (f32[3072]{0:T(1024)}, bf16[256,3072]{1,0:T(8,128)(2,1)S(1)}, f32[256,3072]{1,0:T(8,128)}) fusion(f32[256,3072]{1,0:T(8,128)S(1)} %convolution_add_fusion.5, bf16[256,768]{1,0:T(8,128)(2,1)S(1)} %copy-done.65, bf16[3072,768]{1,0:T(8,128)(2,1)S(1)} %bitcast.301), kind=kOutput, calls=%fused_computation.13 | convolution fusion | flops 1266152448 | bytes 12988416 | tf_op jit(solution)/shard_map/dot_general | solution.py:49
  382.3 2.1 multiply_reduce_fusion.2
  384.9 1.9 convert_reduce_fusion.4
  390.0 2.4 fusion.29
  392.4 2.3 copy.116
  394.8 3.0 multiply_reduce_fusion
  402.1 1.8 convolution_add_fusion.7
  405.5 4.2 fusion.99
  409.7 2.5 reduce-scatter.15.cloned.1.call-done
  412.3 1.2 copy.118
  413.5 19.2 %reduce-scatter.13.cloned.1.call-done = bf16[2,128,768]{2,1,0:T(8,128)(2,1)} async-done(((bf16[2,256,768]{2,1,0:T(8,128)(2,1)}), bf16[2,128,768]{2,1,0:T(8,128)(2,1)}) %reduce-scatter.13.cloned.1.call-update) | async-done | bytes 393232 | tf_op jit(solution)/shard_map/reduce_scatter | solution.py:197
  432.6 1.2 copy.117
  433.9 7.3 convolution_add_fusion
  442.9 2.3 fusion.101
  445.2 5.3 convolution_add_fusion.2
  450.8 3.5 multiply_convert_fusion.3
  454.3 1.4 fusion.117
  458.8 5.1 convolution_add_fusion.1
  466.6 4.6 fusion.38
  474.1 3.9 fusion.39
  479.3 5.2 multiply_reduce_fusion.4
  485.1 40.6 %all-reduce.18 = (f32[768]{0:T(1024)S(1)}, f32[768]{0:T(1024)S(1)}, f32[768]{0:T(1024)S(1)}, f32[768]{0:T(1024)S(1)}, f32[768]{0:T(1024)S(1)}, /*index=5*/f32[76...) all-reduce(f32[768]{0:T(1024)S(1)} %add.474, ...), channel_id=19, replica_groups=mesh['items'=16,'seq'=2] {'items','seq'}, use_global_device_ids=true, to_apply=%region_27.28.clone | all-reduce | flops 9216 | bytes 73728
  531.1 4.7 fusion.108
  536.1 1.2 pad_maximum_fusion
  538.0 125.1 %reduce-scatter.17.cloned.1.call-done = f32[24,2304]{1,0:T(8,128)} async-done(((f32[768,2304]{1,0:T(8,128)}), f32[24,2304]{1,0:T(8,128)}) %reduce-scatter.17.cloned.1.call-update) | async-done | bytes 221200 | tf_op jit(solution)/shard_map/reduce_scatter | solution.py:314
  663.2 141.3 %reduce-scatter.21.cloned.1.call-done = f32[24,3072]{1,0:T(8,128)} async-done(((f32[768,3072]{1,0:T(8,128)}), f32[24,3072]{1,0:T(8,128)}) %reduce-scatter.21.cloned.1.call-update) | async-done | bytes 294928 | tf_op jit(solution)/shard_map/reduce_scatter | solution.py:321
  804.5 141.8 %reduce-scatter.23.cloned.1.call-done = f32[96,768]{1,0:T(8,128)} async-done(((f32[3072,768]{1,0:T(8,128)}), f32[96,768]{1,0:T(8,128)}) %reduce-scatter.23.cloned.1.call-update) | async-done | bytes 294928 | tf_op jit(solution)/shard_map/reduce_scatter | solution.py:323
  (518 shorter events, 64.0 us)
Async XLA Ops:
  7.2 73.4 %copy-start.58 = (bf16[4,1,128,768]{3,2,1,0:T(8,128)(2,1)S(1)}, bf16[4,1,128,768]{3,2,1,0:T(8,128)(2,1)}, u32[]{:S(2)}) copy-start(bf16[4,1,128,768]{3,2,1,0:T(8,128)(2,1)} %param.17) | copy-start | bytes 2359300
  7.2 72.5 %copy-start.8 = (bf16[4,1,128,768]{3,2,1,0:T(8,128)(2,1)S(1)}, bf16[4,1,128,768]{3,2,1,0:T(8,128)(2,1)}, u32[]{:S(2)}) copy-start(bf16[4,1,128,768]{3,2,1,0:T(8,128)(2,1)} %param.33) | copy-start | bytes 2359300
  7.2 76.4 %all-gather.5.cloned.1.call-start = ((), (), s32[]{:S(2)}) async-start(), calls=%async_computation.8 | async-start | bytes 3649536 | tf_op jit(solution)/shard_map/all_gather | solution.py:289
  7.9 122.2 %all-gather.7.cloned.1.call-start = ((), (), s32[]{:S(2)}) async-start(), calls=%async_computation.9 | async-start | bytes 1216512 | tf_op jit(solution)/shard_map/all_gather | solution.py:292
  8.7 187.0 %all-gather.9.cloned.1.call-start = ((), (), s32[]{:S(2)}) async-start(), calls=%async_computation.10 | async-start | bytes 4866048 | tf_op jit(solution)/shard_map/all_gather | solution.py:296
  9.4 251.5 %all-gather.11.cloned.1.call-start = ((), (), s32[]{:S(2)}) async-start(), calls=%async_computation.11 | async-start | bytes 4866048 | tf_op jit(solution)/shard_map/all_gather | solution.py:298
  10.0 291.9 %reduce-scatter.11.cloned.1.call-start = ((), (), s32[]{:S(2)}) async-start(), calls=%async_computation.13 | async-start | bytes 1179648 | tf_op jit(solution)/shard_map/reduce_scatter | solution.py:203
  61.5 22.1 %copy-start.121 = (pred[768]{0:T(1024)(128)(4,1)}, pred[768]{0:T(1024)(128)(4,1)S(1)}, u32[]{:S(2)}) copy-start(pred[768]{0:T(1024)(128)(4,1)S(1)} %broadcast_compare_fusion.1) | copy-start | bytes 2308
  63.5 20.1 %copy-start.90 = (pred[768]{0:T(1024)(128)(4,1)}, pred[768]{0:T(1024)(128)(4,1)S(1)}, u32[]{:S(2)}) copy-start(pred[768]{0:T(1024)(128)(4,1)S(1)} %get-tuple-element.165) | copy-start | bytes 2308
  63.5 20.1 %copy-start.93 = (pred[768]{0:T(1024)(128)(4,1)}, pred[768]{0:T(1024)(128)(4,1)S(1)}, u32[]{:S(2)}) copy-start(pred[768]{0:T(1024)(128)(4,1)S(1)} %get-tuple-element.166) | copy-start | bytes 2308
  63.5 20.1 %copy-start.75 = (f32[768]{0:T(1024)}, f32[768]{0:T(1024)S(1)}, u32[]{:S(2)}) copy-start(f32[768]{0:T(1024)S(1)} %fusion.78) | copy-start | bytes 9220
  63.6 20.1 %copy-start.117 = (f32[2304]{0:T(1024)}, f32[2304]{0:T(1024)S(1)}, u32[]{:S(2)}) copy-start(f32[2304]{0:T(1024)S(1)} %pad_maximum_fusion.4) | copy-start | bytes 27652
  64.4 12.9 %copy-start.142 = (s32[2,1,128]{2,1,0:T(1,128)}, s32[2,1,128]{2,1,0:T(1,128)S(1)}, u32[]{:S(2)}) copy-start(s32[2,1,128]{2,1,0:T(1,128)S(1)} %get-tuple-element.130) | copy-start | bytes 3076
  65.1 12.1 %copy-start.171 = (s32[2,128]{1,0:T(2,128)}, s32[2,128]{1,0:T(2,128)S(1)}, u32[]{:S(2)}) copy-start(s32[2,128]{1,0:T(2,128)S(1)} %get-tuple-element.135) | copy-start | bytes 3076
  65.1 12.1 %copy-start.173 = (s32[2,128]{1,0:T(2,128)}, s32[2,128]{1,0:T(2,128)S(1)}, u32[]{:S(2)}) copy-start(s32[2,128]{1,0:T(2,128)S(1)} %get-tuple-element.136) | copy-start | bytes 3076
  69.4 14.3 %copy-start.176 = (s32[2,128]{1,0:T(2,128)}, s32[2,128]{1,0:T(2,128)S(1)}, u32[]{:S(2)}) copy-start(s32[2,128]{1,0:T(2,128)S(1)} %and_select_fusion.2) | copy-start | bytes 3076
  69.4 14.3 %copy-start.107 = (f32[256]{0:T(256)}, f32[256]{0:T(256)S(1)}, u32[]{:S(2)}) copy-start(f32[256]{0:T(256)S(1)} %get-tuple-element.131) | copy-start | bytes 3076
  87.4 26.0 %copy-start.37 = (bf16[2,128,12,64]{1,0,3,2:T(2,128)(2,1)}, bf16[2,128,12,64]{1,0,3,2:T(2,128)(2,1)S(1)}, u32[]{:S(2)}) copy-start(bf16[2,128,12,64]{1,0,3,2:T(2,128)(2,1)S(1)} %reshape.724) | copy-start | bytes 1179652
  117.0 84.5 %copy-start.35 = (bf16[2,128,12,64]{1,0,3,2:T(2,128)(2,1)}, bf16[2,128,12,64]{1,0,3,2:T(2,128)(2,1)S(1)}, u32[]{:S(2)}) copy-start(bf16[2,128,12,64]{1,0,3,2:T(2,128)(2,1)S(1)} %copy.91) | copy-start | bytes 1179652
  261.0 12.3 %copy-start.13 = (f32[256,768]{1,0:T(8,128)S(1)}, f32[256,768]{1,0:T(8,128)}, u32[]{:S(2)}) copy-start(f32[256,768]{1,0:T(8,128)} %copy-done.12) | copy-start | bytes 2359300
  261.0 12.3 %copy-start.83 = (f32[256]{0:T(256)S(1)}, f32[256]{0:T(256)}, u32[]{:S(2)}) copy-start(f32[256]{0:T(256)} %copy-done.82) | copy-start | bytes 3076
  261.0 12.3 %copy-start.113 = (f32[256]{0:T(256)S(1)}, f32[256]{0:T(256)}, u32[]{:S(2)}) copy-start(f32[256]{0:T(256)} %fusion.92) | copy-start | bytes 3076
  261.0 12.3 %copy-start.178 = (bf16[768,3072]{1,0:T(8,128)(2,1)S(1)}, bf16[768,3072]{1,0:T(8,128)(2,1)}, u32[]{:S(2)}) copy-start(bf16[768,3072]{1,0:T(8,128)(2,1)} %all-gather.9.cloned.1.call-done) | copy-start | bytes 14155780
  285.5 36.1 %reduce-scatter.9.cloned.1.call-start = ((), (), s32[]{:S(2)}) async-start(), calls=%async_computation.12 | async-start | bytes 1179648 | tf_op jit(solution)/shard_map/reduce_scatter | solution.py:197
  292.3 120.0 %reduce-scatter.15.cloned.1.call-start = ((), (), s32[]{:S(2)}) async-start(), calls=%async_computation.15 | async-start | bytes 1179648 | tf_op jit(solution)/shard_map/reduce_scatter | solution.py:203
  293.0 44.3 %copy-start.87 = (f32[256]{0:T(256)}, f32[256]{0:T(256)S(1)}, u32[]{:S(2)}) copy-start(f32[256]{0:T(256)S(1)} %get-tuple-element.133) | copy-start | bytes 3076
  293.0 29.7 %copy-start.59 = (bf16[4,1,128,768]{3,2,1,0:T(8,128)(2,1)S(1)}, bf16[4,1,128,768]{3,2,1,0:T(8,128)(2,1)}, u32[]{:S(2)}) copy-start(bf16[4,1,128,768]{3,2,1,0:T(8,128)(2,1)} %param.17) | copy-start | bytes 2359300
  293.1 29.7 %copy-start.108 = (f32[256]{0:T(256)S(1)}, f32[256]{0:T(256)}, u32[]{:S(2)}) copy-start(f32[256]{0:T(256)} %copy-done.107) | copy-start | bytes 3076
  293.1 29.7 %copy-start.111 = (f32[256]{0:T(256)S(1)}, f32[256]{0:T(256)}, u32[]{:S(2)}) copy-start(f32[256]{0:T(256)} %copy-done.110) | copy-start | bytes 3076
  293.1 29.7 %copy-start.132 = (s32[256]{0:T(256)S(1)}, s32[256]{0:T(256)}, u32[]{:S(2)}) copy-start(s32[256]{0:T(256)} %copy-done.131) | copy-start | bytes 3076
  293.1 29.7 %copy-start.134 = (s32[256]{0:T(256)S(1)}, s32[256]{0:T(256)}, u32[]{:S(2)}) copy-start(s32[256]{0:T(256)} %copy-done.133) | copy-start | bytes 3076
  293.1 29.7 %copy-start.136 = (s32[256]{0:T(256)S(1)}, s32[256]{0:T(256)}, u32[]{:S(2)}) copy-start(s32[256]{0:T(256)} %copy-done.135) | copy-start | bytes 3076
  297.4 25.4 %copy-start.162 = (f32[2,128]{1,0:T(2,128)}, f32[2,128]{1,0:T(2,128)S(1)}, u32[]{:S(2)}) copy-start(f32[2,128]{1,0:T(2,128)S(1)} %multiply_reduce_fusion.11) | copy-start | bytes 3076
  297.4 32.6 %copy-start.137 = (s32[256]{0:T(256)}, s32[256]{0:T(256)S(1)}, u32[]{:S(2)}) copy-start(s32[256]{0:T(256)S(1)} %and_select_fusion.5) | copy-start | bytes 3076
  297.5 39.7 %copy-start.97 = (f32[256]{0:T(256)}, f32[256]{0:T(256)S(1)}, u32[]{:S(2)}) copy-start(f32[256]{0:T(256)S(1)} %bitcast_rsqrt_fusion) | copy-start | bytes 3076
  298.6 31.3 %copy-start.27 = (bf16[96,8,2,128]{3,1,2,0:T(8,128)(2,1)}, bf16[96,8,2,128]{3,1,2,0:T(8,128)(2,1)S(1)}, u32[]{:S(2)}) copy-start(bf16[96,8,2,128]{3,1,2,0:T(8,128)(2,1)S(1)} %copy.172) | copy-start | bytes 1179652
  303.1 26.9 %copy-start.29 = (bf16[256,768]{0,1:T(8,128)(2,1)}, bf16[256,768]{0,1:T(8,128)(2,1)S(1)}, u32[]{:S(2)}) copy-start(bf16[256,768]{0,1:T(8,128)(2,1)S(1)} %copy.109) | copy-start | bytes 1179652
  322.9 14.4 %copy-start.179 = (bf16[768,2304]{1,0:T(8,128)(2,1)S(1)}, bf16[768,2304]{1,0:T(8,128)(2,1)}, u32[]{:S(2)}) copy-start(bf16[768,2304]{1,0:T(8,128)(2,1)} %all-gather.5.cloned.1.call-done) | copy-start | bytes 10616836
  338.8 26.5 %copy-start.39 = (bf16[2,128,12,64]{1,0,3,2:T(2,128)(2,1)}, bf16[2,128,12,64]{1,0,3,2:T(2,128)(2,1)S(1)}, u32[]{:S(2)}) copy-start(bf16[2,128,12,64]{1,0,3,2:T(2,128)(2,1)S(1)} %reshape.729) | copy-start | bytes 1179652
  369.6 14.8 %copy-start.2 = (f32[256,768]{1,0:T(8,128)}, f32[256,768]{1,0:T(8,128)S(1)}, u32[]{:S(2)}) copy-start(f32[256,768]{1,0:T(8,128)S(1)} %get-tuple-element.160) | copy-start | bytes 2359300
  369.6 14.8 %copy-start.85 = (f32[256]{0:T(256)}, f32[256]{0:T(256)S(1)}, u32[]{:S(2)}) copy-start(f32[256]{0:T(256)S(1)} %broadcast_multiply_fusion) | copy-start | bytes 3076
  369.9 14.5 %copy-start.114 = (f32[256]{0:T(256)}, f32[256]{0:T(256)S(1)}, u32[]{:S(2)}) copy-start(f32[256]{0:T(256)S(1)} %fusion.93) | copy-start | bytes 3076
  394.7 37.9 %reduce-scatter.13.cloned.1.call-start = ((), (), s32[]{:S(2)}) async-start(), calls=%async_computation.14 | async-start | bytes 1179648 | tf_op jit(solution)/shard_map/reduce_scatter | solution.py:197
  401.5 136.5 %reduce-scatter.19.cloned.1.call-start = ((), (), s32[]{:S(2)}) async-start(), calls=%async_computation.17 | async-start | bytes 2433024 | tf_op jit(solution)/shard_map/reduce_scatter | solution.py:317
  404.0 259.2 %reduce-scatter.17.cloned.1.call-start = ((), (), s32[]{:S(2)}) async-start(), calls=%async_computation.16 | async-start | bytes 7299072 | tf_op jit(solution)/shard_map/reduce_scatter | solution.py:314
  405.5 28.3 %copy-start.43 = (bf16[96,8,2,128]{3,1,2,0:T(8,128)(2,1)}, bf16[96,8,2,128]{3,1,2,0:T(8,128)(2,1)S(1)}, u32[]{:S(2)}) copy-start(bf16[96,8,2,128]{3,1,2,0:T(8,128)(2,1)S(1)} %copy.171) | copy-start | bytes 1179652
  405.5 28.3 %copy-start.17 = (f32[256,768]{1,0:T(8,128)S(1)}, f32[256,768]{1,0:T(8,128)}, u32[]{:S(2)}) copy-start(f32[256,768]{1,0:T(8,128)} %copy-done.15) | copy-start | bytes 2359300
  405.5 28.3 %copy-start.88 = (f32[256]{0:T(256)S(1)}, f32[256]{0:T(256)}, u32[]{:S(2)}) copy-start(f32[256]{0:T(256)} %copy-done.87) | copy-start | bytes 3076
  405.5 28.3 %copy-start.98 = (f32[256]{0:T(256)S(1)}, f32[256]{0:T(256)}, u32[]{:S(2)}) copy-start(f32[256]{0:T(256)} %copy-done.97) | copy-start | bytes 3076
  413.4 27.8 %copy-start.45 = (bf16[256,768]{0,1:T(8,128)(2,1)}, bf16[256,768]{0,1:T(8,128)(2,1)S(1)}, u32[]{:S(2)}) copy-start(bf16[256,768]{0,1:T(8,128)(2,1)S(1)} %copy.118) | copy-start | bytes 1179652
  441.3 363.2 %reduce-scatter.21.cloned.1.call-start = ((), (), s32[]{:S(2)}) async-start(), calls=%async_computation.18 | async-start | bytes 9732096 | tf_op jit(solution)/shard_map/reduce_scatter | solution.py:321
  450.5 495.8 %reduce-scatter.23.cloned.1.call-start = ((), (), s32[]{:S(2)}) async-start(), calls=%async_computation.19 | async-start | bytes 9732096 | tf_op jit(solution)/shard_map/reduce_scatter | solution.py:323
  479.2 51.8 %copy-start.163 = (f32[2,128]{1,0:T(2,128)S(1)}, f32[2,128]{1,0:T(2,128)}, u32[]{:S(2)}) copy-start(f32[2,128]{1,0:T(2,128)} %copy-done.162) | copy-start | bytes 3076
  479.2 51.8 %copy-start.61 = (bf16[4,1,128,768]{3,2,1,0:T(8,128)(2,1)S(1)}, bf16[4,1,128,768]{3,2,1,0:T(8,128)(2,1)}, u32[]{:S(2)}) copy-start(bf16[4,1,128,768]{3,2,1,0:T(8,128)(2,1)} %param.17) | copy-start | bytes 2359300
  479.2 51.8 %copy-start.96 = (pred[768]{0:T(1024)(128)(4,1)S(1)}, pred[768]{0:T(1024)(128)(4,1)}, u32[]{:S(2)}) copy-start(pred[768]{0:T(1024)(128)(4,1)} %copy-done.93) | copy-start | bytes 2308
  479.2 51.8 %copy-start.100 = (f32[256]{0:T(256)S(1)}, f32[256]{0:T(256)}, u32[]{:S(2)}) copy-start(f32[256]{0:T(256)} %copy-done.97) | copy-start | bytes 3076
  479.2 51.8 %copy-start.124 = (pred[768]{0:T(1024)(128)(4,1)S(1)}, pred[768]{0:T(1024)(128)(4,1)}, u32[]{:S(2)}) copy-start(pred[768]{0:T(1024)(128)(4,1)} %copy-done.121) | copy-start | bytes 2308
  479.2 51.8 %copy-start.127 = (s32[256]{0:T(256)S(1)}, s32[256]{0:T(256)}, u32[]{:S(2)}) copy-start(s32[256]{0:T(256)} %get-tuple-element.137) | copy-start | bytes 3076
  479.2 51.8 %copy-start.130 = (s32[256]{0:T(256)S(1)}, s32[256]{0:T(256)}, u32[]{:S(2)}) copy-start(s32[256]{0:T(256)} %get-tuple-element.138) | copy-start | bytes 3076
  479.2 51.8 %copy-start.139 = (s32[256]{0:T(256)S(1)}, s32[256]{0:T(256)}, u32[]{:S(2)}) copy-start(s32[256]{0:T(256)} %copy-done.137) | copy-start | bytes 3076
  484.4 51.4 %copy-start.24 = (f32[256,768]{1,0:T(8,128)S(1)}, f32[256,768]{1,0:T(8,128)}, u32[]{:S(2)}) copy-start(f32[256,768]{1,0:T(8,128)} %copy-done.23) | copy-start | bytes 2359300
  484.4 51.4 %copy-start.145 = (f32[256]{0:T(256)S(1)}, f32[256]{0:T(256)}, u32[]{:S(2)}) copy-start(f32[256]{0:T(256)} %copy-done.144) | copy-start | bytes 3076
  484.4 51.4 %copy-start.155 = (pred[256]{0:T(512)(128)(4,1)S(1)}, pred[256]{0:T(512)(128)(4,1)}, u32[]{:S(2)}) copy-start(pred[256]{0:T(512)(128)(4,1)} %get-tuple-element.142) | copy-start | bytes 772
  484.4 51.6 %copy-start.62 = (f32[256,768]{1,0:T(8,128)S(1)}, f32[256,768]{1,0:T(8,128)}, u32[]{:S(2)}) copy-start(f32[256,768]{1,0:T(8,128)} %get-tuple-element.119) | copy-start | bytes 2359300
  (133 other events, 454.9 us)
Sparse Core Ops, SparseCore 0:
  11.0 63.0 all-gather.4
  77.0 53.1 all-gather.6
  133.1 62.5 all-gather.8
  198.5 62.4 all-gather.10
  285.6 16.2 reduce-scatter.10
  304.1 17.4 reduce-scatter.8
  394.8 17.3 reduce-scatter.14
  415.2 17.4 reduce-scatter.12
  438.5 99.4 reduce-scatter.18
  545.1 118.0 reduce-scatter.16
  669.6 134.7 reduce-scatter.20
  811.8 134.4 reduce-scatter.22
where the time goes:
time: 964 us; the launch traced here: 953 us
  waiting for transfers between devices  589 us (61%)
  blocking collectives  127 us (13%)
  matrix products  111 us (12%)
  other arithmetic  61 us (6%)
  local copies, waits for them, and re-layouts  47.8 us (5%)
  between operations  17.1 us (2%)
    reduce_scatter x1, waiting for transfers between devices, body(): lax.psum_scatter(grads[11], ('items', 'seq'), scatter_dimension=0, tiled=...  142 us
    reduce_scatter x1, waiting for transfers between devices, body(): lax.psum_scatter(grads[9], ('items', 'seq'), scatter_dimension=0, tiled=T...  141 us
    reduce_scatter x1, waiting for transfers between devices, body(): lax.psum_scatter(grads[2], ('items', 'seq'), scatter_dimension=0, tiled=T...  125 us
    unnamed x2, blocking collectives  83.2 us
    all_gather x1, waiting for transfers between devices, body(): lax.all_gather(shards[9], ('items', 'seq'), axis=0, tiled=True)  61.1 us
    all_gather x1, waiting for transfers between devices, body(): lax.all_gather(shards[11], ('items', 'seq'), axis=0, tiled=True)  59.5 us
    dot_general x8, matrix products, against(): lax.dot_general(left, right, (((1,), (1,)), ((), ())), preferred_element_...  40.2 us
    reduce_scatter x2, waiting for transfers between devices, micro_batch(): lax.psum_scatter(key_terms.reshape(item_count, 2 * block_rows, model_widt...  37.7 us
  transfers between devices with their start and end apart: 12, of which 11 were waited for; matrix products, arithmetic and copies ran while one was open for 14% of the time, Pallas kernels for 0%

commit v1 on v0

--- a/solution.py
+++ b/solution.py
@@ -1,6 +1,11 @@
+import functools
+
 import jax
 import jax.numpy as jnp
+import numpy as np
 from jax import lax
+from jax.experimental import pallas as pl
+from jax.experimental.pallas import tpu as pltpu
 from jax.sharding import PartitionSpec as P
 
 HD = 64
@@ -240,7 +245,7 @@
     return (layer_out, tokens_grad, grads)
 
 
-def body(
+def general_body(
     tokens,
     visible,
     lengths,
@@ -354,6 +359,911 @@
     )
 
 
+Z_SIZE = 4
+F32 = jnp.float32
+BF16 = jnp.bfloat16
+MESH = pl.DeviceIdType.MESH
+RELAY_X = 3
+CHUNK = 24
+W_I, W_O, W_E, W_R, VEC = TENSORS = range(5)
+AG_SEMS = 19
+RS_SEMS = 13
+VECTORS = 8
+
+
+def nn(left, right):
+    return lax.dot_general(left, right, (((1,), (0,)), ((), ())), preferred_element_type=F32)
+
+
+def nt(left, right):
+    return lax.dot_general(left, right, (((1,), (1,)), ((), ())), preferred_element_type=F32)
+
+
+def tn(left, right):
+    return lax.dot_general(left, right, (((0,), (0,)), ((), ())), preferred_element_type=F32)
+
+
+def lanes(start, size):
+    return pl.ds(pl.multiple_of(start, 128), size)
+
+
+def rows_at(start, size):
+    return pl.ds(pl.multiple_of(start, 128), size)
+
+
+class Place:
+    def __init__(self):
+        item = lax.axis_index("items")
+        self.y = lax.axis_index("seq")
+        self.z = item // 4
+        self.x = (item // 2) % 2
+        self.c = item % 2
+
+    def device(self, z, x, c, y):
+        return ((z * 2 + x) * 2 + c, y)
+
+    def to_z(self, k):
+        return self.device(lax.rem(self.z + k, Z_SIZE), self.x, self.c, self.y)
+
+    @property
+    def to_x(self):
+        return self.device(self.z, 1 - self.x, self.c, self.y)
+
+    @property
+    def to_y(self):
+        return self.device(self.z, self.x, self.c, 1 - self.y)
+
+    @property
+    def to_c(self):
+        return self.device(self.z, self.x, 1 - self.c, self.y)
+
+    def column(self, flip_x, flip_c, flip_y):
+        x = 1 - self.x if flip_x else self.x
+        c = 1 - self.c if flip_c else self.c
+        y = 1 - self.y if flip_y else self.y
+        return x * 4 + c * 2 + y
+
+    def quarter(self, flip_x, flip_y):
+        x = 1 - self.x if flip_x else self.x
+        y = 1 - self.y if flip_y else self.y
+        return x * 2 + y
+
+
+def remote(src, dst, send, recv, device):
+    return pltpu.make_async_remote_copy(
+        src_ref=src, dst_ref=dst, send_sem=send, recv_sem=recv, device_id=device, device_id_type=MESH
+    )
+
+
+class Gather:
+    def __init__(self, here, buf, send, recv):
+        self.here, self.buf, self.send, self.recv = here, buf, send, recv
+        self.open = []
+
+    def copy(self, slot, index, device):
+        ref = self.buf.at[slot]
+        return remote(ref, ref, self.send.at[index], self.recv.at[index], device)
+
+    def push(self, slot, index, device):
+        made = self.copy(slot, index, device)
+        made.start()
+        self.open.append(made)
+
+    def pull(self, slot, index):
+        self.copy(slot, index, self.here.to_x).wait_recv()
+
+    def behind(self, k):
+        return lax.rem(self.here.z + (Z_SIZE - k), Z_SIZE)
+
+    def begin(self):
+        here = self.here
+        own = (here.z, here.column(0, 0, 0))
+        for k in (1, 3, 2):
+            self.push(own, k - 1, here.to_z(k))
+        self.push(own, 3, here.to_x)
+        self.push(own, 7, here.to_y)
+
+    def pass_on(self, k):
+        here = self.here
+        slot = (self.behind(k), here.column(0, 0, 0))
+        self.pull(slot, k - 1)
+        self.push(slot, 3 + k, here.to_x)
+        self.push(slot, 7 + k, here.to_y)
+
+    def own_to_core(self):
+        here = self.here
+        self.push((slice(None), here.column(0, 0, 0)), 15, here.to_c)
+
+    def relay(self, k):
+        here = self.here
+        from_x = (self.behind(k), here.column(1, 0, 0))
+        from_y = (self.behind(k), here.column(0, 0, 1))
+        self.pull(from_x, 3 + k)
+        self.pull(from_y, 7 + k)
+        if k < RELAY_X:
+            self.push(from_y, 11 + k, here.to_x)
+        else:
+            self.push(from_x, 11 + k, here.to_y)
+
+    def sides_to_core(self):
+        here = self.here
+        self.push((slice(None), here.column(1, 0, 0)), 16, here.to_c)
+        self.push((slice(None), here.column(0, 0, 1)), 17, here.to_c)
+
+    def corner(self):
+        here = self.here
+        for k in range(4):
+            self.pull((self.behind(k), here.column(1, 0, 1)), 11 + k)
+        self.push((slice(None), here.column(1, 0, 1)), 18, here.to_c)
+
+    def from_core(self):
+        here = self.here
+        for index, (fx, fy) in ((15, (0, 0)), (16, (1, 0)), (17, (0, 1)), (18, (1, 1))):
+            self.pull((slice(None), here.column(fx, 1, fy)), index)
+
+    def drain(self):
+        for made in self.open:
+            made.wait_send()
+        self.open = []
+
+
+QUARTERS = ((1, 1), (1, 0), (0, 1), (0, 0))
+
+
+class Reduce:
+    def __init__(self, here, part, core, relay, sides, ends, send, recv):
+        self.here, self.part, self.core, self.sides_in, self.ends = here, part, core, sides, ends
+        self.relay_in = relay
+        self.send, self.recv = send, recv
+        self.open = []
+
+    def push(self, src, dst, index, device):
+        made = remote(src, dst, self.send.at[index], self.recv.at[index], device)
+        made.start()
+        self.open.append(made)
+
+    def pull(self, dst, index):
+        remote(dst, dst, self.send.at[index], self.recv.at[index], self.here.to_x).wait_recv()
+
+    def add(self, column, first, last, *others):
+        part = self.part
+
+        def one(z, carry):
+            total = part[z, column].astype(F32)
+            for ref, index in others:
+                total = total + ref[z, index].astype(F32)
+            part[z, column] = total.astype(part.dtype)
+            return carry
+
+        lax.fori_loop(first, last, one, 0)
+
+    def core_send(self, spare=None):
+        here = self.here
+        if spare is not None:
+            pl.semaphore_wait(spare, 1)
+        for index, (fx, fy) in enumerate(QUARTERS):
+            self.push(
+                self.part.at[:, here.column(fx, 1, fy)],
+                self.core.at[:, here.quarter(fx, fy)],
+                index,
+                here.to_c,
+            )
+
+    def core_add(self):
+        here = self.here
+        for index, (fx, fy) in enumerate(QUARTERS):
+            quarter = here.quarter(fx, fy)
+            self.pull(self.core.at[:, quarter], index)
+            self.add(here.column(fx, 0, fy), 0, 4, (self.core, quarter))
+            if index == 0:
+                corner = here.column(1, 0, 1)
+                src, dst = self.part, self.relay_in
+                self.push(src.at[:RELAY_X, corner], dst.at[:RELAY_X], 4, here.to_x)
+                self.push(src.at[RELAY_X:, corner], dst.at[RELAY_X:], 5, here.to_y)
+            if index == 1:
+                column = here.column(1, 0, 0)
+                dst = self.sides_in.at[:RELAY_X, 0]
+                self.push(self.part.at[:RELAY_X, column], dst, 6, here.to_x)
+            if index == 2:
+                column = here.column(0, 0, 1)
+                dst = self.sides_in.at[RELAY_X:, 1]
+                self.push(self.part.at[RELAY_X:, column], dst, 8, here.to_y)
+
+    def relay(self):
+        here, part = self.here, self.part
+        to_x, to_y = here.column(1, 0, 0), here.column(0, 0, 1)
+
+        def pair(z, column):
+            total = part[z, column].astype(F32) + self.relay_in[z].astype(F32)
+            part[z, column] = total.astype(part.dtype)
+
+        self.pull(self.relay_in.at[RELAY_X:], 5)
+        for z in range(RELAY_X, 4):
+            pair(z, to_x)
+        self.push(part.at[RELAY_X:, to_x], self.sides_in.at[RELAY_X:, 0], 7, here.to_x)
+        self.pull(self.relay_in.at[:RELAY_X], 4)
+
+        def one(z, carry):
+            pair(z, to_y)
+            return carry
+
+        lax.fori_loop(0, RELAY_X, one, 0)
+        self.push(part.at[:RELAY_X, to_y], self.sides_in.at[:RELAY_X, 1], 9, here.to_y)
+
+    def sides(self):
+        here = self.here
+        for index, where in ((6, (slice(0, RELAY_X), 0)), (8, (slice(RELAY_X, 4), 1)),
+                             (7, (slice(RELAY_X, 4), 0)), (9, (slice(0, RELAY_X), 1))):
+            self.pull(self.sides_in.at[where], index)
+        own = here.column(0, 0, 0)
+        self.add(own, 0, 4, (self.sides_in, 0), (self.sides_in, 1))
+        for k in (1, 3, 2):
+            away = lax.rem(here.z + k, Z_SIZE)
+            self.push(self.part.at[away, own], self.ends.at[k - 1], 9 + k, here.to_z(k))
+
+    def finish(self):
+        here = self.here
+        for k in (1, 3, 2):
+            self.pull(self.ends.at[k - 1], 9 + k)
+        total = self.part[here.z, here.column(0, 0, 0)].astype(F32)
+        for k in range(3):
+            total = total + self.ends[k].astype(F32)
+        return total
+
+    def drain(self):
+        for made in self.open:
+            made.wait_send()
+        self.open = []
+
+
+def normalise(rows_in):
+    centre = rows_in - jnp.mean(rows_in, axis=-1, keepdims=True)
+    spread = jnp.mean(centre * centre, axis=-1, keepdims=True)
+    inverse = lax.rsqrt(spread + EPSILON)
+    return centre * inverse, inverse
+
+
+def normalise_back(grad, unit, inverse):
+    return inverse * (
+        grad
+        - jnp.mean(grad, axis=-1, keepdims=True)
+        - unit * jnp.mean(grad * unit, axis=-1, keepdims=True)
+    )
+
+
+def spread_matrix(slot):
+    lane = lax.broadcasted_iota(jnp.int32, (128, 768), 0)
+    place = lax.broadcasted_iota(jnp.int32, (128, 768), 1)
+    if slot is None:
+        inside = lax.rem(place, 4 * CHUNK)
+        wanted = 32 * (inside // CHUNK) + lax.rem(inside, CHUNK)
+    else:
+        wanted = 32 * slot + lax.rem(place, CHUNK)
+    return jnp.where(lane == wanted, 1.0, 0.0).astype(BF16)
+
+
+def owner_mask(each, first):
+    device = lax.broadcasted_iota(jnp.int32, (32, 768), 0)
+    place = lax.broadcasted_iota(jnp.int32, (32, 768), 1)
+    return device == first + place // each
+
+
+def collect(group, matrix, each, first):
+    moved = nn(group.astype(BF16), matrix)
+    return jnp.sum(jnp.where(owner_mask(each, first), moved, 0.0), axis=0, keepdims=True)
+
+
+def deal(row, matrix, each, first):
+    placed = jnp.where(owner_mask(each, first), row, 0.0)
+    high = placed.astype(BF16)
+    rest = placed - high.astype(F32)
+    middle = rest.astype(BF16)
+    low = (rest - middle.astype(F32)).astype(BF16)
+    return nt(high, matrix) + nt(middle, matrix) + nt(low, matrix)
+
+
+def one_hot(value):
+    slot = lax.broadcasted_iota(jnp.int32, (16, 128), 0).astype(F32)
+    ones = jnp.where(slot == value, 1.0, 0.0).astype(BF16)
+    return jnp.concatenate([ones, ones, ones], axis=0)
+
+
+def live_rows(count, block, number):
+    slot = lax.broadcasted_iota(jnp.int32, (number, 1), 0)
+    return slot < (count + 1 - block) // 2
+
+
+def live_bias(count):
+    slot = lax.broadcasted_iota(jnp.int32, (256, 1), 0)
+    block = slot // 128
+    return jnp.where(slot - 128 * block < (count + 1 - block) // 2, 0.0, -1e30)
+
+
+def half_mask(head):
+    return lax.broadcasted_iota(jnp.int32, (1, 128), 1) // HD == head
+
+
+def fused_kernel(
+    lengths, tokens, cotangent, seen, shard_I, shard_O, shard_E, shard_R, shard_V, table,
+    layer_out, tokens_grad, grad_I, grad_O, grad_E, grad_R, grad_V, *refs,
+):
+    s = Store(refs)
+    here = Place()
+    z, x, c, y = here.z, here.x, here.c, here.y
+    own = here.column(0, 0, 0)
+
+    barrier = pltpu.get_barrier_semaphore()
+    partners = [here.to_z(1), here.to_z(2), here.to_z(3), here.to_x, here.to_y, here.to_c]
+    for device in partners:
+        pl.semaphore_signal(barrier, inc=1, device_id=device, device_id_type=MESH)
+
+    for name, shard in ((W_I, shard_I), (W_O, shard_O), (W_E, shard_E)):
+        whole = shard[...].astype(F32)
+        half = whole.shape[1] // 2
+        unit = jnp.concatenate([whole[:, :half], whole[:, half:]], axis=0)
+        s.G[name][z, own] = unit.astype(BF16)
+    s.G[W_R][z, own] = shard_R[...]
+    s.G[VEC][z, own] = shard_V[...]
+    s.SEEN[:, y] = seen[pl.ds(2 * y, 2)]
+    pl.semaphore_wait(barrier, len(partners))
+
+    gather = {
+        name: Gather(here, s.G[name], s.GS[name], s.GQ[name]) for name in TENSORS
+    }
+    swap_s, swap_r = s.SWS, s.SWR
+    mine, other = pl.ds(2 * y, 2), pl.ds(2 * (1 - y), 2)
+    swaps = [
+        remote(tokens.at[other], s.TOK.at[:, y], swap_s.at[0], swap_r.at[0], here.to_y),
+        remote(seen.at[other], s.SEEN.at[:, y], swap_s.at[1], swap_r.at[1], here.to_y),
+        remote(cotangent.at[other], s.INC.at[:, y], swap_s.at[2], swap_r.at[2], here.to_y),
+    ]
+    came = [
+        remote(s.TOK.at[:, 1 - y], s.TOK.at[:, 1 - y], swap_s.at[0], swap_r.at[0], here.to_y),
+        remote(s.SEEN.at[:, 1 - y], s.SEEN.at[:, 1 - y], swap_s.at[1], swap_r.at[1], here.to_y),
+        remote(s.INC.at[:, 1 - y], s.INC.at[:, 1 - y], swap_s.at[2], swap_r.at[2], here.to_y),
+    ]
+    local = [
+        pltpu.make_async_copy(tokens.at[mine], s.TOK.at[:, y], s.LOC.at[0]),
+        pltpu.make_async_copy(cotangent.at[mine], s.INC.at[:, y], s.LOC.at[1]),
+    ]
+    gather[VEC].begin()
+    gather[W_I].begin()
+    swaps[1].start()
+    swaps[0].start()
+    local[0].start()
+    local[1].start()
+    gather[W_O].begin()
+    gather[W_E].begin()
+    gather[W_R].begin()
+    swaps[2].start()
+
+    def step_z(name):
+        for k in (1, 3, 2):
+            gather[name].pass_on(k)
+        gather[name].own_to_core()
+
+    def step_relay(name):
+        for k in range(4):
+            gather[name].relay(k)
+        gather[name].sides_to_core()
+
+    def step_corner(name):
+        gather[name].corner()
+
+    def step_last(name):
+        gather[name].from_core()
+
+    for name in (VEC, W_I, W_O):
+        step_z(name)
+    for name in (VEC, W_I, W_O):
+        step_relay(name)
+    step_z(W_E)
+    for name in (VEC, W_I):
+        step_corner(name)
+    step_last(VEC)
+
+    vec = s.ROWS
+    for number in range(VECTORS):
+        group = s.G[VEC][:, :, number // 4, :].reshape(32, 128)
+        vec[pl.ds(number, 1), :] = collect(group, spread_matrix(number % 4), CHUNK, 0)
+    group = s.G[VEC][:, :, 2, :].reshape(32, 128)
+    for part in range(4):
+        cols = slice(768 * part, 768 * part + 768)
+        s.EB[:, cols] = collect(group, spread_matrix(None), 4 * CHUNK, 8 * part)
+
+    def vector(number):
+        return vec[pl.ds(number, 1), :]
+
+    s.PB[:, 0:768] = vector(2)
+    s.PB[:, 768:1536] = jnp.zeros((1, 768), F32)
+    s.PB[:, 1536:2304] = vector(3)
+    sums = s.SUMS
+    sums[...] = jnp.zeros_like(sums)
+    s.EBG[...] = jnp.zeros_like(s.EBG)
+
+    for copy in (swaps[0], swaps[1]):
+        copy.wait_send()
+    local[0].wait()
+    came[1].wait_recv()
+    came[0].wait_recv()
+
+    def first_norm(block, carry):
+        it, half = block // 2, block % 2
+        rows = rows_at(128 * block, 128)
+        patch = s.SEEN[it, half][0:1, :].astype(F32)
+        frame = jnp.floor((patch + 0.5) * (1.0 / (GRID * GRID)))
+        inside = patch - frame * (GRID * GRID)
+        line = jnp.floor((inside + 0.5) * (1.0 / GRID))
+        across = inside - line * GRID
+        place = jnp.concatenate([tn(one_hot(v), table[...]) for v in (frame, line, across)], axis=1)
+        entry = s.TOK[it, half].astype(F32) + place
+        s.ENT[rows, :] = entry
+        unit, _ = normalise(entry)
+        normed = (unit * vector(0) + vector(1)).astype(BF16)
+        s.XB[rows, :] = normed
+        s.NRMT[:, lanes(128 * block, 128)] = normed.T
+        return carry
+
+    lax.fori_loop(0, 4, first_norm, 0)
+
+    def lay_out(name, target, half):
+        buf = s.G[name]
+
+        def one(i, carry):
+            zz, pair = i // 4, 2 * (i % 4)
+            even = buf[zz, pair].astype(F32)
+            odd = buf[zz, pair + 1].astype(F32)
+            rows = pl.ds(pl.multiple_of(48 * i, 16), 48)
+            target[rows, :half] = jnp.concatenate([even[:24], odd[:24]], axis=0).astype(BF16)
+            target[rows, half:] = jnp.concatenate([even[24:], odd[24:]], axis=0).astype(BF16)
+            return carry
+
+        lax.fori_loop(0, 16, one, 0)
+
+    step_last(W_I)
+    lay_out(W_I, s.WI, 1152)
+
+    def project(n, carry):
+        cols = lanes(256 * n, 256)
+        s.PRJ[:, cols] = (nn(s.XB[...], s.WI[:, cols]) + s.PB[:, cols]).astype(BF16)
+        return carry
+
+    lax.fori_loop(0, 9, project, 0)
+
+    step_relay(W_E)
+    step_corner(W_O)
+    step_z(W_R)
+    step_last(W_O)
+    lay_out(W_O, s.WO, 384)
+
+    def attend(step, carry):
+        it, pair = step // 6, step % 6
+        rows = rows_at(256 * it, 256)
+        cols = lanes(128 * pair, 128)
+        q = s.PRJ[rows, cols]
+        k = s.PRJ[rows, lanes(768 + 128 * pair, 128)]
+        v = s.PRJ[rows, lanes(1536 + 128 * pair, 128)]
+        bias = live_bias(lengths[2 * y + it])
+        total = jnp.zeros((128, 256), F32)
+        for head in range(2):
+            mask = half_mask(head)
+            scores = nt(jnp.where(mask, k, 0), q) * SCORE_SCALE + bias
+            exponent = jnp.exp(scores - jnp.max(scores, axis=0, keepdims=True))
+            attention = exponent * (1.0 / jnp.sum(exponent, axis=0, keepdims=True))
+            low = attention.astype(BF16)
+            s.ATN[2 * step + head] = low
+            total = total + tn(jnp.where(mask, v, 0), low)
+        s.ATTT[cols, rows] = total.astype(BF16)
+        s.XB[rows, cols] = total.T.astype(BF16)
+        return carry
+
+    lax.fori_loop(0, 6, attend, 0)
+    step_corner(W_E)
+    step_relay(W_R)
+    lax.fori_loop(6, 12, attend, 0)
+
+    def second_norm(it, carry):
+        rows = rows_at(256 * it, 256)
+        middle = s.ENT[rows, :] + nn(s.XB[rows, :], s.WO[...]) + vector(4)
+        s.MID[rows, :] = middle
+        unit, _ = normalise(middle)
+        second = (unit * vector(5) + vector(6)).astype(BF16)
+        s.XB[rows, :] = second
+        s.SECT[:, rows] = second.T
+        return carry
+
+    lax.fori_loop(0, 2, second_norm, 0)
+    step_last(W_E)
+    lay_out(W_E, s.WE, 1536)
+    step_corner(W_R)
+
+    def expand(step, carry):
+        n, it = step // 2, step % 2
+        cols = lanes(256 * n, 256)
+        rows = rows_at(256 * it, 256)
+        expanded = nn(s.XB[rows, :], s.WE[:, cols]) + s.EB[:, cols]
+        normal = 0.5 * (1.0 + lax.erf(expanded * 0.7071067811865476))
+        density = jnp.exp(-0.5 * expanded * expanded) * 0.3989422804014327
+        s.ACT[rows, cols] = (expanded * normal).astype(BF16)
+        s.GP[rows, cols] = (normal + expanded * density).astype(BF16)
+        return carry
+
+    lax.fori_loop(0, 24, expand, 0)
+
+    swaps[2].wait_send()
+    local[1].wait()
+    came[2].wait_recv()
+
+    def take_in(block, carry):
+        it, half = block // 2, block % 2
+        live = live_rows(lengths[2 * y + it], half, 128)
+        incoming = jnp.where(live, s.INC[it, half].astype(F32), 0.0)
+        s.INC[it, half] = incoming.astype(BF16)
+        sums[7:8, :] += jnp.sum(incoming, axis=0, keepdims=True)
+        return carry
+
+    lax.fori_loop(0, 4, take_in, 0)
+
+    reduce = {
+        name: Reduce(
+            here, s.P[name], s.RC[name], s.R1[name], s.R2[name], s.RZ[name],
+            s.RS[name], s.RQ[name],
+        )
+        for name in TENSORS
+    }
+
+    def reduce_weight_grad(f, carry):
+        zz, xx = f // 2, f % 2
+        moved = s.ACT[:, lanes(384 * f, 384)].T
+        part = nn(moved, s.INC[...].reshape(512, 768))
+        s.P[W_R][zz, pl.ds(4 * xx, 4)] = part.reshape(4, 96, 768).astype(BF16)
+        return carry
+
+    lax.fori_loop(0, 8, reduce_weight_grad, 0)
+    reduce[W_R].core_send()
+
+    step_last(W_R)
+
+    def expanded_grad(step, carry):
+        zz, it = step // 2, step % 2
+        rows = rows_at(256 * it, 256)
+        cols = lanes(768 * zz, 768)
+        weight = s.G[W_R][zz].reshape(768, 768)
+        incoming = s.INC[it].reshape(256, 768)
+        grad = (nt(incoming, weight) * s.GP[rows, cols].astype(F32)).astype(BF16)
+        s.GP[rows, cols] = grad
+        s.EBG[:, cols] += jnp.sum(grad.astype(F32), axis=0, keepdims=True)
+        return carry
+
+    lax.fori_loop(0, 8, expanded_grad, 0)
+    reduce[W_R].core_add()
+
+    def weight_grad(name, moved, grad, half, wide):
+        part = s.P[name]
+
+        def one(step, carry):
+            n, m = step // 2, step % 2
+            left = grad[:, lanes(wide * n, wide)]
+            right = grad[:, lanes(half + wide * n, wide)]
+            block = nn(moved[rows_at(384 * m, 384), :], jnp.concatenate([left, right], axis=1))
+            for j in range(8):
+                for side in range(2):
+                    rows = slice(48 * j + 24 * side, 48 * j + 24 * side + 24)
+                    unit = jnp.concatenate([block[rows, :wide], block[rows, wide:]], axis=0)
+                    part[2 * m + j // 4, 2 * (j % 4) + side, :, lanes(wide * n, wide)] = unit.astype(BF16)
+            return carry
+
+        lax.fori_loop(0, 2 * half // wide, one, 0)
+
+    gather[W_E].drain()
+    weight_grad(W_E, s.SECT, s.GP, 1536, 256)
+    reduce[W_E].core_send()
+
+    def finish_rows(it, carry):
+        rows = rows_at(256 * it, 256)
+        out = s.MID[rows, :] + vector(7)
+        for zz in range(4):
+            out = out + nn(s.ACT[rows, 768 * zz : 768 * zz + 768], s.G[W_R][zz].reshape(768, 768))
+        for half in range(2):
+            live = live_rows(lengths[2 * y + it], half, 128)
+            s.TOK[it, half] = jnp.where(live, out[128 * half : 128 * half + 128], 0.0).astype(BF16)
+        return carry
+
+    lax.fori_loop(0, 2, finish_rows, 0)
+    out_there = remote(
+        s.TOK.at[:, 1 - y], layer_out.at[mine], swap_s.at[3], swap_r.at[3], here.to_y
+    )
+    out_came = remote(s.TOK.at[:, y], layer_out.at[other], swap_s.at[3], swap_r.at[3], here.to_y)
+    out_here = pltpu.make_async_copy(s.TOK.at[:, y], layer_out.at[mine], s.LOC.at[2])
+    out_there.start()
+    out_here.start()
+
+    reduce[W_R].relay()
+
+    def middle_back(it, carry):
+        rows = rows_at(256 * it, 256)
+        grad = nt(s.GP[rows, :], s.WE[...])
+        unit, inverse = normalise(s.MID[rows, :])
+        sums[5:6, :] += jnp.sum(grad * unit, axis=0, keepdims=True)
+        sums[6:7, :] += jnp.sum(grad, axis=0, keepdims=True)
+        incoming = s.INC[it].reshape(256, 768).astype(F32)
+        middle_grad = incoming + normalise_back(grad * vector(5), unit, inverse)
+        s.MID[rows, :] = middle_grad
+        branch = middle_grad.astype(BF16)
+        s.XB[rows, :] = branch
+        sums[4:5, :] += jnp.sum(branch.astype(F32), axis=0, keepdims=True)
+        return carry
+
+    lax.fori_loop(0, 2, middle_back, 0)
+    reduce[W_E].core_add()
+    pl.semaphore_signal(s.SPARE, inc=1, device_id=here.to_c, device_id_type=MESH)
+    gather[W_O].drain()
+    weight_grad(W_O, s.ATTT, s.XB, 384, 128)
+    reduce[W_O].core_send()
+
+    def attended_back(it, carry):
+        rows = rows_at(256 * it, 256)
+        s.XB[rows, :] = nt(s.XB[rows, :], s.WO[...]).astype(BF16)
+        return carry
+
+    lax.fori_loop(0, 2, attended_back, 0)
+    reduce[W_R].sides()
+    reduce[W_E].relay()
+
+    def attend_back(step, carry):
+        it, pair = step // 6, step % 6
+        rows = rows_at(256 * it, 256)
+        cols = lanes(128 * pair, 128)
+        k_cols, v_cols = lanes(768 + 128 * pair, 128), lanes(1536 + 128 * pair, 128)
+        q = s.PRJ[rows, cols]
+        k = s.PRJ[rows, k_cols]
+        v = s.PRJ[rows, v_cols]
+        grad = s.XB[rows, cols]
+        query_grad = jnp.zeros((128, 256), F32)
+        key_grad = jnp.zeros((256, 128), F32)
+        value_grad = jnp.zeros((256, 128), F32)
+        for head in range(2):
+            mask = half_mask(head)
+            mine_grad = jnp.where(mask, grad, 0)
+            weight_back = nt(v, mine_grad)
+            low = s.ATN[2 * step + head]
+            attention = low.astype(F32)
+            inner = jnp.sum(attention * weight_back, axis=0, keepdims=True)
+            scores_grad = (attention * (weight_back - inner)).astype(BF16)
+            query_grad = query_grad + tn(jnp.where(mask, k, 0), scores_grad)
+            key_grad = key_grad + nn(scores_grad, jnp.where(mask, q, 0))
+            value_grad = value_grad + nn(low, mine_grad)
+        query_low = (query_grad * SCORE_SCALE).T.astype(BF16)
+        value_low = value_grad.astype(BF16)
+        s.PRJ[rows, cols] = query_low
+        s.PRJ[rows, k_cols] = (key_grad * SCORE_SCALE).astype(BF16)
+        s.PRJ[rows, v_cols] = value_low
+        sums[2:3, cols] += jnp.sum(query_low.astype(F32), axis=0, keepdims=True)
+        sums[3:4, cols] += jnp.sum(value_low.astype(F32), axis=0, keepdims=True)
+        return carry
+
+    lax.fori_loop(0, 6, attend_back, 0)
+    reduce[W_O].core_add()
+    reduce[W_E].sides()
+    lax.fori_loop(6, 12, attend_back, 0)
+    gather[W_I].drain()
+    weight_grad(W_I, s.NRMT, s.PRJ, 1152, 128)
+    reduce[W_I].core_send(s.SPARE)
+    reduce[W_O].relay()
+
+    def entry_back(step, carry):
+        it = step % 2
+        half = jnp.where(step < 2, 1 - y, y)
+        rows = rows_at(256 * it + 128 * half, 128)
+        grad = nt(s.PRJ[rows, :], s.WI[...])
+        unit, inverse = normalise(s.ENT[rows, :])
+        sums[0:1, :] += jnp.sum(grad * unit, axis=0, keepdims=True)
+        sums[1:2, :] += jnp.sum(grad, axis=0, keepdims=True)
+        out = s.MID[rows, :] + normalise_back(grad * vector(0), unit, inverse)
+        s.ENT[rows, :] = out
+        s.INC[it, half] = out.astype(BF16)
+        return carry
+
+    lax.fori_loop(0, 2, entry_back, 0)
+    grad_there = remote(s.INC.at[:, 1 - y], s.TGR, swap_s.at[4], swap_r.at[4], here.to_y)
+    grad_there.start()
+    lax.fori_loop(2, 4, entry_back, 0)
+    grad_here = [
+        pltpu.make_async_copy(
+            s.ENT.at[rows_at(256 * it + 128 * y, 128)], tokens_grad.at[2 * y + it], s.LOC.at[3 + it]
+        )
+        for it in range(2)
+    ]
+    for copy in grad_here:
+        copy.start()
+    reduce[W_I].core_add()
+    reduce[W_O].sides()
+
+    for number in range(VECTORS):
+        dealt = deal(sums[number : number + 1, :], spread_matrix(number % 4), CHUNK, 0)
+        if number % 4 == 0:
+            group = dealt
+        else:
+            group = group + dealt
+        if number % 4 == 3:
+            s.P[VEC][:, :, number // 4, :] = group.reshape(4, 8, 128)
+    group = jnp.zeros((32, 128), F32)
+    for part in range(4):
+        row = s.EBG[:, 768 * part : 768 * part + 768]
+        group = group + deal(row, spread_matrix(None), 4 * CHUNK, 8 * part)
+    s.P[VEC][:, :, 2, :] = group.reshape(4, 8, 128)
+    for row in range(3, 8):
+        s.P[VEC][:, :, row, :] = jnp.zeros((4, 8, 128), F32)
+    reduce[VEC].core_send()
+    reduce[W_I].relay()
+    reduce[VEC].core_add()
+    reduce[VEC].relay()
+    grad_R[...] = reduce[W_R].finish()
+
+    def place_grad(name, ref, half):
+        total = reduce[name].finish()
+        ref[:, :half] = total[:24]
+        ref[:, half:] = total[24:]
+
+    place_grad(W_E, grad_E, 1536)
+    reduce[W_I].sides()
+    reduce[VEC].sides()
+    place_grad(W_O, grad_O, 384)
+    grad_there.wait_send()
+    remote(s.INC.at[:, 1 - y], s.TGR, swap_s.at[4], swap_r.at[4], here.to_y).wait_recv()
+    for copy in grad_here:
+        copy.wait()
+    grad_rest = []
+    for it in range(2):
+        rows = rows_at(256 * it + 128 * (1 - y), 128)
+        s.ENT[rows, :] = s.TGR[it].astype(F32)
+        copy = pltpu.make_async_copy(
+            s.ENT.at[rows], tokens_grad.at[2 * (1 - y) + it], s.LOC.at[5 + it]
+        )
+        copy.start()
+        grad_rest.append(copy)
+    place_grad(W_I, grad_I, 1152)
+    grad_V[...] = reduce[VEC].finish()
+    for copy in grad_rest:
+        copy.wait()
+    out_there.wait_send()
+    out_here.wait()
+    out_came.wait_recv()
+    gather[VEC].drain()
+    gather[W_R].drain()
+    for name in TENSORS:
+        reduce[name].drain()
+
+
+UNITS = ((48, 1152), (48, 384), (48, 1536), (96, 768), (8, 128))
+
+
+def scratch_list():
+    dma, vmem = pltpu.SemaphoreType.DMA, pltpu.VMEM
+    shapes = dict(
+        SWS=dma((5,)),
+        SWR=dma((5,)),
+        LOC=dma((7,)),
+        SPARE=pltpu.SemaphoreType.REGULAR,
+        TOK=vmem((2, 2, 128, 768), BF16),
+        INC=vmem((2, 2, 128, 768), BF16),
+        SEEN=vmem((2, 2, 8, 128), jnp.int32),
+        ROWS=vmem((8, 768), F32),
+        EB=vmem((1, 3072), F32),
+        PB=vmem((1, 2304), F32),
+        SUMS=vmem((8, 768), F32),
+        EBG=vmem((1, 3072), F32),
+        WI=vmem((768, 2304), BF16),
+        WO=vmem((768, 768), BF16),
+        WE=vmem((768, 3072), BF16),
+        ENT=vmem((512, 768), F32),
+        MID=vmem((512, 768), F32),
+        XB=vmem((512, 768), BF16),
+        NRMT=vmem((768, 512), BF16),
+        ATTT=vmem((768, 512), BF16),
+        SECT=vmem((768, 512), BF16),
+        PRJ=vmem((512, 2304), BF16),
+        ATN=vmem((24, 256, 256), BF16),
+        ACT=vmem((512, 3072), BF16),
+        GP=vmem((512, 3072), BF16),
+        TGR=vmem((2, 128, 768), BF16),
+    )
+    many = dict(G=[], GS=[], GQ=[], P=[], RC=[], R1=[], R2=[], RZ=[], RS=[], RQ=[])
+    for name in TENSORS:
+        kind = F32 if name == VEC else BF16
+        unit = UNITS[name]
+        many["G"].append(vmem((4, 8, *unit), kind))
+        many["GS"].append(dma((AG_SEMS,)))
+        many["GQ"].append(dma((AG_SEMS,)))
+        if name in (W_R, VEC):
+            many["P"].append(vmem((4, 8, *unit), kind))
+        if name != W_I:
+            many["RC"].append(vmem((4, 4, *unit), kind))
+        many["R1"].append(vmem((4, *unit), kind))
+        many["R2"].append(vmem((4, 2, *unit), kind))
+        many["RZ"].append(vmem((3, *unit), kind))
+        many["RS"].append(dma((RS_SEMS,)))
+        many["RQ"].append(dma((RS_SEMS,)))
+    return shapes, many
+
+
+class Store:
+    def __init__(self, refs):
+        shapes, many = scratch_list()
+        refs = list(refs)
+        for name in shapes:
+            setattr(self, name, refs.pop(0))
+        for name, listed in many.items():
+            setattr(self, name, [refs.pop(0) for _ in listed])
+        self.P = self.G[:3] + self.P
+        self.RC = [self.RC[1].at[:, :, :, :1152]] + self.RC
+
+
+def position_table():
+    step = np.arange(16, dtype=np.float64)[:, None]
+    channel = np.arange(256)
+    angle = step * np.power(10000.0, -(channel // 2) / 128.0)
+    whole = np.where(channel % 2 == 0, np.sin(angle), np.cos(angle)).astype(np.float32)
+    high = whole.astype(jnp.bfloat16)
+    rest = whole - high.astype(np.float32)
+    middle = rest.astype(jnp.bfloat16)
+    low = (rest - middle.astype(np.float32)).astype(jnp.bfloat16)
+    return np.concatenate([high, middle, low], axis=0)
+
+
+def fused_body(
+    tokens, visible, lengths, first_gain, first_shift, input_weight, query_bias, value_bias,
+    output_weight, output_bias, second_gain, second_shift, expand_weight, expand_bias,
+    reduce_weight, reduce_bias, cotangent,
+):
+    chunks = jnp.concatenate(
+        [
+            jnp.stack(
+                [first_gain, first_shift, query_bias, value_bias, output_bias, second_gain, second_shift, reduce_bias]
+            ),
+            expand_bias.reshape(4, CHUNK),
+        ],
+        axis=0,
+    ).astype(F32)
+    shard_V = jnp.pad(chunks, ((0, 20), (0, 32 - CHUNK))).reshape(8, 128)
+    seen = jnp.broadcast_to(visible, (4, 8, 128))
+    hbm = pl.BlockSpec(memory_space=pl.ANY)
+    vmem = pl.BlockSpec(memory_space=pltpu.VMEM)
+    smem = pl.BlockSpec(memory_space=pltpu.SMEM)
+    shapes, many = scratch_list()
+    results = [
+        jax.ShapeDtypeStruct((4, 128, 768), BF16),
+        jax.ShapeDtypeStruct((4, 128, 768), F32),
+        jax.ShapeDtypeStruct(input_weight.shape, F32),
+        jax.ShapeDtypeStruct(output_weight.shape, F32),
+        jax.ShapeDtypeStruct(expand_weight.shape, F32),
+        jax.ShapeDtypeStruct(reduce_weight.shape, F32),
+        jax.ShapeDtypeStruct((8, 128), F32),
+    ]
+    layer_out, tokens_grad, grad_I, grad_O, grad_E, grad_R, grad_V = pl.pallas_call(
+        fused_kernel,
+        name="layer",
+        out_shape=results,
+        in_specs=[smem, hbm, hbm, vmem, vmem, vmem, vmem, vmem, vmem, vmem],
+        out_specs=[hbm, hbm, vmem, vmem, vmem, vmem, vmem],
+        scratch_shapes=[*shapes.values(), *(shape for listed in many.values() for shape in listed)],
+        compiler_params=pltpu.CompilerParams(
+            collective_id=0, has_side_effects=True, vmem_limit_bytes=VMEM_BYTES
+        ),
+    )(
+        lengths, tokens[:, 0], cotangent[:, 0], seen, input_weight, output_weight, expand_weight,
+        reduce_weight, shard_V, jnp.asarray(position_table()),
+    )
+    dealt = grad_V.reshape(32, 32)[:12, :CHUNK]
+    return (
+        layer_out[:, None], tokens_grad[:, None], dealt[0], dealt[1], grad_I, dealt[2], dealt[3], grad_O,
+        dealt[4], dealt[5], dealt[6], grad_E, dealt[8:12].reshape(4 * CHUNK), grad_R, dealt[7],
+    )
+
+
+VMEM_BYTES = 67000000
+
+
 def solution(mesh):
     in_specs = (
         P("items", "seq", None, None),
@@ -391,4 +1301,6 @@
         P(("items", "seq"), None),
         P(("items", "seq")),
     )
-    return jax.shard_map(body, mesh=mesh, in_specs=in_specs, out_specs=out_specs, check_vma=False)
+    sizes = (mesh.shape["items"], mesh.shape["seq"])
+    chosen = fused_body if sizes == (Z_SIZE * 4, 2) else general_body
+    return jax.shard_map(chosen, mesh=mesh, in_specs=in_specs, out_specs=out_specs, check_vma=False)

time: 964 us -> 207 us (0.21); the launches traced: 953 us -> 207 us
  waiting for transfers between devices: 589 us -> 0 us
  Pallas kernels: 0 us -> 195 us
  blocking collectives: 127 us -> 0 us
  matrix products: 111 us -> 0 us
  other arithmetic: 61 us -> 0.01 us
  local copies, waits for them, and re-layouts: 47.8 us -> 11.5 us
  between operations: 17.1 us -> 0.68 us
    reduce_scatter x8 -> x0, waiting for transfers between devices: 452 us -> none  [the longest x1 142 us: body(): lax.psum_scatter(grads[11], ('items', 'seq'), scatter_dimension=0, tiled=...]
    pallas_call x0 -> x1, Pallas kernels: none -> 195 us  [fused_body(): pl.pallas_call(fused_kernel, name='layer', out_shape=results, in_specs=[s...]
    all_gather x4 -> x0, waiting for transfers between devices: 134 us -> none  [the longest x1 61.1 us: body(): lax.all_gather(shards[9], ('items', 'seq'), axis=0, tiled=True)]
    dot_general x36 -> x0, matrix products: 111 us -> none  [the longest x8 40.2 us: against(): lax.dot_general(left, right, (((1,), (1,)), ((), ())), preferred_element_...]
    unnamed x2 -> x0, blocking collectives: 83.2 us -> none
    all_gather x4 -> x0, blocking collectives: 43.9 us -> none  [the longest x2 22.4 us: micro_batch(): lax.all_gather(keys_here, 'seq', axis=1, tiled=True)]
    reduce_sum x16 -> x0, other arithmetic: 35.9 us -> none  [the longest x5 16.1 us: layer_norm(): centre = rows_in - jnp.mean(rows_in, axis=-1, keepdims=True)]
    unnamed x399 -> x16, local copies, waits for them, and re-layouts: 25.2 us -> 5.97 us
  transfers between devices with their start and end apart: 12 -> 0, of which waited for: 11 -> 0; matrix products, arithmetic and copies ran while one was open for 14% -> 0% of each run, Pallas kernels for 0% -> 0%
where the time goes in v1:
time: 207 us
  Pallas kernels  195 us (94%)
  local copies, waits for them, and re-layouts  11.5 us (6%)
    pallas_call x1, Pallas kernels, fused_body(): pl.pallas_call(fused_kernel, name='layer', out_shape=results, in_specs=[s...  195 us
    unnamed x16, local copies, waits for them, and re-layouts  5.97 us

profile of v1, /device:TPU:0, one launch (start us, length us, event | category | flops | bytes accessed | tf_op | source)
XLA Modules:
  0.0 207.2 jit_solution(12084446517082749627)
XLA Ops:
  0.6 0.7 reshape.44
  1.4 0.8 concatenate.3
  2.2 0.7 reshape.50.shard_V
  2.9 1.3 broadcast_in_dim.14.seen
  4.2 195.0 %layer.1 = (bf16[4,128,768]{2,1,0:T(8,128)(2,1)}, f32[4,128,768]{2,1,0:T(8,128)}, f32[24,2304]{1,0:T(8,128)}, f32[24,768]{1,0:T(8,128)}, f32[24,3072]{1,0:T(8,12...) custom-call(s32[4]{0:T(128)} %lengths.1, bf16[4,128,768]{2,1,0:T(8,128)(2,1)} %bitcast.34, bf16[4,128,768]{2,1,0:T(8,128)(2,1)} %bitcast.35, ...), custom_call_target="tpu_custom_call" | custom-call | tf_op jit(solution)/shard_map/layer/pallas_call | solution.py:1243
  199.2 0.0 copy-start
  199.2 0.9 reshape.47
  200.0 0.5 slice_bitcast_fusion
  200.6 0.6 reshape.48
  201.2 2.1 copy.41
  203.2 0.0 copy-done
  203.2 0.0 copy-start.3
  203.2 0.0 copy-start.4
  203.2 0.0 copy-start.2
  203.2 0.0 copy-start.1
  203.3 1.1 copy.42
  204.4 0.0 copy-done.3
  204.4 0.7 copy.43
  205.1 0.0 copy-done.4
  205.1 0.6 copy.44
  205.7 0.0 copy-done.2
  205.7 0.7 copy.45
  206.4 0.0 copy-done.1
  206.4 0.7 copy.46
  (2 shorter events, 0.0 us)
Async XLA Ops:
  199.2 4.1 %copy-start = (f32[4,128,768]{2,1,0:T(8,128)S(1)}, f32[4,128,768]{2,1,0:T(8,128)}, u32[]{:S(2)}) copy-start(f32[4,128,768]{2,1,0:T(8,128)} %get-tuple-element.23) | copy-start | bytes 4718596
  203.2 1.2 copy-start.3
  203.2 1.9 copy-start.4
  203.2 2.5 %copy-start.2 = (f32[24,3072]{1,0:T(8,128)S(1)}, f32[24,3072]{1,0:T(8,128)}, u32[]{:S(2)}) copy-start(f32[24,3072]{1,0:T(8,128)} %get-tuple-element.78) | copy-start | bytes 884740
  203.2 3.2 %copy-start.1 = (f32[96,768]{1,0:T(8,128)S(1)}, f32[96,768]{1,0:T(8,128)}, u32[]{:S(2)}) copy-start(f32[96,768]{1,0:T(8,128)} %get-tuple-element.80) | copy-start | bytes 884740

commit v2 on v0

--- a/solution.py
+++ b/solution.py
@@ -1,6 +1,11 @@
+import functools
+
 import jax
 import jax.numpy as jnp
+import numpy as np
 from jax import lax
+from jax.experimental import pallas as pl
+from jax.experimental.pallas import tpu as pltpu
 from jax.sharding import PartitionSpec as P
 
 HD = 64
@@ -240,7 +245,7 @@
     return (layer_out, tokens_grad, grads)
 
 
-def body(
+def general_body(
     tokens,
     visible,
     lengths,
@@ -354,6 +359,1151 @@
     )
 
 
+Z_SIZE = 4
+F32 = jnp.float32
+BF16 = jnp.bfloat16
+MESH = pl.DeviceIdType.MESH
+CHUNK = 24
+W_I, W_O, W_E, W_R, W_Q, VEC = TENSORS = range(6)
+GATHER_X = (3, 3, 3, 3, None, 2)
+D_IA, D_IB, D_O, D_EA, D_EB, D_R, D_Q, D_V = SUMS = range(8)
+REDUCE_X = (3, 3, 3, 3, 3, 2, None, 2)
+SEMS = 20
+VECTORS = 8
+
+
+def nn(left, right):
+    return lax.dot_general(left, right, (((1,), (0,)), ((), ())), preferred_element_type=F32)
+
+
+def nt(left, right):
+    return lax.dot_general(left, right, (((1,), (1,)), ((), ())), preferred_element_type=F32)
+
+
+def tn(left, right):
+    return lax.dot_general(left, right, (((0,), (0,)), ((), ())), preferred_element_type=F32)
+
+
+def lanes(start, size):
+    return pl.ds(pl.multiple_of(start, 128), size)
+
+
+def rows_at(start, size):
+    return pl.ds(pl.multiple_of(start, 128), size)
+
+
+class Place:
+    def __init__(self):
+        item = lax.axis_index("items")
+        self.y = lax.axis_index("seq")
+        self.z = item // 4
+        self.x = (item // 2) % 2
+        self.c = item % 2
+
+    def device(self, z, x, c, y):
+        return ((z * 2 + x) * 2 + c, y)
+
+    def to_z(self, k):
+        return self.device(lax.rem(self.z + k, Z_SIZE), self.x, self.c, self.y)
+
+    @property
+    def to_x(self):
+        return self.device(self.z, 1 - self.x, self.c, self.y)
+
+    @property
+    def to_y(self):
+        return self.device(self.z, self.x, self.c, 1 - self.y)
+
+    @property
+    def to_c(self):
+        return self.device(self.z, self.x, 1 - self.c, self.y)
+
+    def column(self, flip_x, flip_c, flip_y):
+        x = 1 - self.x if flip_x else self.x
+        c = 1 - self.c if flip_c else self.c
+        y = 1 - self.y if flip_y else self.y
+        return x * 4 + c * 2 + y
+
+    def quarter(self, flip_x, flip_y):
+        x = 1 - self.x if flip_x else self.x
+        y = 1 - self.y if flip_y else self.y
+        return x * 2 + y
+
+
+def remote(src, dst, send, recv, device):
+    return pltpu.make_async_remote_copy(
+        src_ref=src, dst_ref=dst, send_sem=send, recv_sem=recv, device_id=device, device_id_type=MESH
+    )
+
+
+class Gather:
+    def __init__(self, here, buf, send, recv, share):
+        self.here, self.buf, self.send, self.recv = here, buf, send, recv
+        self.share = share
+        self.open = []
+
+    def copy(self, slot, index, device):
+        ref = self.buf.at[slot]
+        return remote(ref, ref, self.send.at[index], self.recv.at[index], device)
+
+    def push(self, slot, index, device):
+        made = self.copy(slot, index, device)
+        made.start()
+        self.open.append(made)
+
+    def pull(self, slot, index):
+        self.copy(slot, index, self.here.to_x).wait_recv()
+
+    def behind(self, k):
+        return lax.rem(self.here.z + (Z_SIZE - k), Z_SIZE)
+
+    def own(self):
+        return (self.here.z, self.here.column(0, 0, 0))
+
+    def begin_z(self):
+        for k in (1, 3, 2):
+            self.push(self.own(), k - 1, self.here.to_z(k))
+
+    def begin_x(self):
+        self.push(self.own(), 3, self.here.to_x)
+
+    def begin_y(self):
+        self.push(self.own(), 7, self.here.to_y)
+
+    def pass_on(self, k):
+        here = self.here
+        slot = (self.behind(k), here.column(0, 0, 0))
+        self.pull(slot, k - 1)
+        self.push(slot, 3 + k, here.to_x)
+        self.push(slot, 7 + k, here.to_y)
+
+    def own_to_core(self):
+        here = self.here
+        self.push((slice(None), here.column(0, 0, 0)), 15, here.to_c)
+
+    def relay(self, k):
+        here = self.here
+        from_x = (self.behind(k), here.column(1, 0, 0))
+        from_y = (self.behind(k), here.column(0, 0, 1))
+        self.pull(from_x, 3 + k)
+        self.pull(from_y, 7 + k)
+        if k < self.share:
+            self.push(from_y, 11 + k, here.to_x)
+        else:
+            self.push(from_x, 11 + k, here.to_y)
+
+    def sides_to_core(self):
+        here = self.here
+        self.push((slice(None), here.column(1, 0, 0)), 16, here.to_c)
+        self.push((slice(None), here.column(0, 0, 1)), 17, here.to_c)
+
+    def corner(self):
+        here = self.here
+        for k in range(4):
+            self.pull((self.behind(k), here.column(1, 0, 1)), 11 + k)
+        self.push((slice(None), here.column(1, 0, 1)), 18, here.to_c)
+
+    def from_core(self):
+        here = self.here
+        for index, (fx, fy) in ((15, (0, 0)), (16, (1, 0)), (17, (0, 1)), (18, (1, 1))):
+            self.pull((slice(None), here.column(fx, 1, fy)), index)
+
+    def drain(self):
+        for made in self.open:
+            made.wait_send()
+        self.open = []
+
+
+class PlaneGather(Gather):
+    def halves(self):
+        wide = self.buf.shape[-1] // 2
+        return slice(0, wide), slice(wide, 2 * wide)
+
+    def begin_x(self):
+        self.push(self.own(), 0, self.here.to_x)
+
+    def begin_y(self):
+        self.push(self.own(), 1, self.here.to_y)
+
+    def along_z(self, column, first):
+        for k in (1, 3, 2):
+            self.push((self.here.z, column), first + k - 1, self.here.to_z(k))
+
+    def own_along_z(self):
+        self.along_z(self.here.column(0, 0, 0), 4)
+
+    def relay(self):
+        here = self.here
+        left, right = self.halves()
+        from_x, from_y = here.column(1, 0, 0), here.column(0, 0, 1)
+        self.pull((here.z, from_x), 0)
+        self.push((here.z, from_x, slice(None), right), 3, here.to_y)
+        self.pull((here.z, from_y), 1)
+        self.push((here.z, from_y, slice(None), left), 2, here.to_x)
+        self.along_z(from_x, 7)
+        self.along_z(from_y, 10)
+
+    def corner(self):
+        here = self.here
+        left, right = self.halves()
+        corner = here.column(1, 0, 1)
+        self.pull((here.z, corner, slice(None), left), 2)
+        self.pull((here.z, corner, slice(None), right), 3)
+        self.along_z(corner, 13)
+
+    def to_core(self, part):
+        here = self.here
+        flips = ((0, 0), (1, 0), (0, 1), (1, 1))[part]
+        column = here.column(flips[0], 0, flips[1])
+        for k in (1, 3, 2):
+            self.pull((self.behind(k), column), 4 + 3 * part + k - 1)
+        self.push((slice(None), column), 16 + part, here.to_c)
+
+    def from_core(self):
+        here = self.here
+        for index, (fx, fy) in enumerate(((0, 0), (1, 0), (0, 1), (1, 1))):
+            self.pull((slice(None), here.column(fx, 1, fy)), 16 + index)
+
+
+QUARTERS = ((1, 1), (1, 0), (0, 1), (0, 0))
+
+
+class Reduce:
+    def __init__(self, here, part, core, relay, sides, ends, send, recv, share):
+        self.here, self.part, self.core, self.sides_in, self.ends = here, part, core, sides, ends
+        self.share = share
+        self.relay_in = relay
+        self.send, self.recv = send, recv
+        self.open = []
+
+    def push(self, src, dst, index, device):
+        made = remote(src, dst, self.send.at[index], self.recv.at[index], device)
+        made.start()
+        self.open.append(made)
+
+    def pull(self, dst, index):
+        remote(dst, dst, self.send.at[index], self.recv.at[index], self.here.to_x).wait_recv()
+
+    def add(self, column, first, last, *others):
+        part = self.part
+
+        def one(z, carry):
+            total = part[z, column].astype(F32)
+            for ref, index in others:
+                total = total + ref[z, index].astype(F32)
+            part[z, column] = total.astype(part.dtype)
+            return carry
+
+        lax.fori_loop(first, last, one, 0)
+
+    def core_send(self, spare=None):
+        here = self.here
+        if spare is not None:
+            pl.semaphore_wait(spare, 1)
+        for index, (fx, fy) in enumerate(QUARTERS):
+            self.push(
+                self.part.at[:, here.column(fx, 1, fy)],
+                self.core.at[:, here.quarter(fx, fy)],
+                index,
+                here.to_c,
+            )
+
+    def core_add(self, index):
+        here, share = self.here, self.share
+        fx, fy = QUARTERS[index]
+        quarter, column = here.quarter(fx, fy), here.column(fx, 0, fy)
+        self.pull(self.core.at[:, quarter], index)
+        self.add(column, 0, 4, (self.core, quarter))
+        part = self.part
+        if index == 0:
+            self.push(part.at[:share, column], self.relay_in.at[:share], 4, here.to_x)
+            self.push(part.at[share:, column], self.relay_in.at[share:], 5, here.to_y)
+        if index == 1:
+            self.push(part.at[:share, column], self.sides_in.at[:share, 0], 6, here.to_x)
+        if index == 2:
+            self.push(part.at[share:, column], self.sides_in.at[share:, 1], 8, here.to_y)
+
+    def relay(self):
+        here, part, share = self.here, self.part, self.share
+        to_x, to_y = here.column(1, 0, 0), here.column(0, 0, 1)
+
+        def pair(z, column):
+            total = part[z, column].astype(F32) + self.relay_in[z].astype(F32)
+            part[z, column] = total.astype(part.dtype)
+
+        self.pull(self.relay_in.at[share:], 5)
+        for z in range(share, 4):
+            pair(z, to_x)
+        self.push(part.at[share:, to_x], self.sides_in.at[share:, 0], 7, here.to_x)
+        self.pull(self.relay_in.at[:share], 4)
+
+        def one(z, carry):
+            pair(z, to_y)
+            return carry
+
+        lax.fori_loop(0, share, one, 0)
+        self.push(part.at[:share, to_y], self.sides_in.at[:share, 1], 9, here.to_y)
+
+    def sides(self):
+        here, share = self.here, self.share
+        for index, where in ((6, (slice(0, share), 0)), (8, (slice(share, 4), 1)),
+                             (7, (slice(share, 4), 0)), (9, (slice(0, share), 1))):
+            self.pull(self.sides_in.at[where], index)
+        own = here.column(0, 0, 0)
+        self.add(own, 0, 4, (self.sides_in, 0), (self.sides_in, 1))
+        for k in (1, 3, 2):
+            away = lax.rem(here.z + k, Z_SIZE)
+            self.push(self.part.at[away, own], self.ends.at[k - 1], 9 + k, here.to_z(k))
+
+    def finish(self):
+        here = self.here
+        for k in (1, 3, 2):
+            self.pull(self.ends.at[k - 1], 9 + k)
+        total = self.part[here.z, here.column(0, 0, 0)].astype(F32)
+        for k in range(3):
+            total = total + self.ends[k].astype(F32)
+        return total
+
+    def drain(self):
+        for made in self.open:
+            made.wait_send()
+        self.open = []
+
+
+class PlaneReduce(Reduce):
+    def core_add(self, index):
+        here = self.here
+        fx, fy = QUARTERS[index]
+        quarter, column = here.quarter(fx, fy), here.column(fx, 0, fy)
+        self.pull(self.core.at[:, quarter], index)
+        self.add(column, 0, 4, (self.core, quarter))
+        for k in (1, 3, 2):
+            away = lax.rem(here.z + k, Z_SIZE)
+            self.push(
+                self.part.at[away, column], self.ends.at[k - 1, index], 4 + 3 * index + k - 1, here.to_z(k)
+            )
+
+    def relay(self):
+        here, part, z = self.here, self.part, self.here.z
+        wide = part.shape[-1] // 2
+        for index, (fx, fy) in enumerate(QUARTERS):
+            column = here.column(fx, 0, fy)
+            for k in (1, 3, 2):
+                self.pull(self.ends.at[k - 1, index], 4 + 3 * index + k - 1)
+            total = part[z, column].astype(F32)
+            for k in range(3):
+                total = total + self.ends[k, index].astype(F32)
+            part[z, column] = total.astype(part.dtype)
+            if index == 0:
+                src, dst = part.at[z, column], self.relay_in
+                self.push(src.at[:, :wide], dst.at[:, :wide], 16, here.to_x)
+                self.push(src.at[:, wide:], dst.at[:, wide:], 17, here.to_y)
+
+    def sides(self):
+        here, part, z = self.here, self.part, self.here.z
+        wide = part.shape[-1] // 2
+        for index, cols, fx, fy, to in (
+            (17, slice(wide, 2 * wide), 1, 0, here.to_x), (16, slice(0, wide), 0, 1, here.to_y)
+        ):
+            column = here.column(fx, 0, fy)
+            self.pull(self.relay_in.at[:, cols], index)
+            total = part[z, column, :, cols].astype(F32) + self.relay_in[:, cols].astype(F32)
+            part[z, column, :, cols] = total.astype(part.dtype)
+            self.push(part.at[z, column], self.sides_in.at[fy], 18 + fy, to)
+
+    def finish(self):
+        here = self.here
+        total = self.part[here.z, here.column(0, 0, 0)].astype(F32)
+        for index in range(2):
+            self.pull(self.sides_in.at[index], 18 + index)
+            total = total + self.sides_in[index].astype(F32)
+        return total
+
+
+def normalise(rows_in):
+    centre = rows_in - jnp.mean(rows_in, axis=-1, keepdims=True)
+    spread = jnp.mean(centre * centre, axis=-1, keepdims=True)
+    inverse = lax.rsqrt(spread + EPSILON)
+    return centre * inverse, inverse
+
+
+def normalise_back(grad, unit, inverse):
+    return inverse * (
+        grad
+        - jnp.mean(grad, axis=-1, keepdims=True)
+        - unit * jnp.mean(grad * unit, axis=-1, keepdims=True)
+    )
+
+
+def spread_matrix(slot):
+    lane = lax.broadcasted_iota(jnp.int32, (128, 768), 0)
+    place = lax.broadcasted_iota(jnp.int32, (128, 768), 1)
+    if slot is None:
+        inside = lax.rem(place, 4 * CHUNK)
+        wanted = 32 * (inside // CHUNK) + lax.rem(inside, CHUNK)
+    else:
+        wanted = 32 * slot + lax.rem(place, CHUNK)
+    return jnp.where(lane == wanted, 1.0, 0.0).astype(BF16)
+
+
+def owner_mask(each, first):
+    device = lax.broadcasted_iota(jnp.int32, (32, 768), 0)
+    place = lax.broadcasted_iota(jnp.int32, (32, 768), 1)
+    return device == first + place // each
+
+
+def collect(group, matrix, each, first):
+    moved = nn(group.astype(BF16), matrix)
+    return jnp.sum(jnp.where(owner_mask(each, first), moved, 0.0), axis=0, keepdims=True)
+
+
+def deal(row, matrix, each, first):
+    placed = jnp.where(owner_mask(each, first), row, 0.0)
+    high = placed.astype(BF16)
+    rest = placed - high.astype(F32)
+    middle = rest.astype(BF16)
+    low = (rest - middle.astype(F32)).astype(BF16)
+    return nt(high, matrix) + nt(middle, matrix) + nt(low, matrix)
+
+
+def one_hot(value):
+    slot = lax.broadcasted_iota(jnp.int32, (16, 128), 0).astype(F32)
+    ones = jnp.where(slot == value, 1.0, 0.0).astype(BF16)
+    return jnp.concatenate([ones, ones, ones], axis=0)
+
+
+def live_rows(count, block, number):
+    slot = lax.broadcasted_iota(jnp.int32, (number, 1), 0)
+    return slot < (count + 1 - block) // 2
+
+
+def live_bias(count):
+    slot = lax.broadcasted_iota(jnp.int32, (256, 1), 0)
+    block = slot // 128
+    return jnp.where(slot - 128 * block < (count + 1 - block) // 2, 0.0, -1e30)
+
+
+def half_mask(head):
+    return lax.broadcasted_iota(jnp.int32, (1, 128), 1) // HD == head
+
+
+def fused_kernel(
+    lengths, tokens, cotangent, seen, shard_I, shard_O, shard_E, shard_R, shard_V, table,
+    layer_out, tokens_grad, grad_I, grad_O, grad_E, grad_R, grad_V, *refs,
+):
+    s = Store(refs)
+    here = Place()
+    z, x, c, y = here.z, here.x, here.c, here.y
+    own = here.column(0, 0, 0)
+    mine, other = pl.ds(2 * y, 2), pl.ds(2 * (1 - y), 2)
+    sums = s.SUMS
+
+    gather = [
+        (PlaneGather if name == W_Q else Gather)(here, s.G[name], s.GS[name], s.GQ[name], GATHER_X[name])
+        for name in TENSORS
+    ]
+    reduce = []
+    for number, (name, cols, landing) in enumerate(PIECES):
+        kind = PlaneReduce if name == W_Q else Reduce
+        part, *bufs = [s.P[name], s.R1[name], s.R2[name], s.RZ[name]]
+        core = s.RC[landing]
+        if cols is not None:
+            part, *bufs = [ref.at[(*(slice(None),) * (len(ref.shape) - 1), cols)] for ref in (part, *bufs)]
+            core = core.at[:, :, :, : cols.stop - cols.start]
+        reduce.append(kind(here, part, core, *bufs, s.RS[number], s.RQ[number], REDUCE_X[number]))
+
+    def swap(src, dst, came, index):
+        made = remote(src, dst, s.SWS.at[index], s.SWR.at[index], here.to_y)
+        return made, remote(came, came, s.SWS.at[index], s.SWR.at[index], here.to_y)
+
+    tok_out, tok_in = swap(tokens.at[other], s.TOK.at[:, y], s.TOK.at[:, 1 - y], 0)
+    seen_out, seen_in = swap(s.AWAY, s.SEEN.at[:, y], s.SEEN.at[:, 1 - y], 1)
+    cot_out, cot_in = swap(cotangent.at[other], s.INC.at[:, y], s.INC.at[:, 1 - y], 2)
+    lay_out, lay_in = swap(s.TOK.at[:, 1 - y], layer_out.at[mine], layer_out.at[other], 3)
+    grad_out, grad_in = swap(s.INC.at[:, 1 - y], s.TGR, s.TGR, 4)
+    tok_copy = pltpu.make_async_copy(tokens.at[mine], s.TOK.at[:, y], s.LOC.at[0])
+    cot_copy = pltpu.make_async_copy(cotangent.at[mine], s.INC.at[:, y], s.LOC.at[1])
+    out_copy = pltpu.make_async_copy(s.TOK.at[:, y], layer_out.at[mine], s.LOC.at[2])
+    near_copies = [
+        pltpu.make_async_copy(
+            s.ENT.at[rows_at(256 * it + 128 * y, 128)], tokens_grad.at[2 * y + it], s.LOC.at[3 + it]
+        )
+        for it in range(2)
+    ]
+    far_copies = [
+        pltpu.make_async_copy(
+            s.ENT.at[rows_at(256 * it + 128 * (1 - y), 128)], tokens_grad.at[2 * (1 - y) + it], s.LOC.at[5 + it]
+        )
+        for it in range(2)
+    ]
+
+    def vector(number):
+        return s.ROWS[pl.ds(number, 1), :]
+
+    def start():
+        barrier = pltpu.get_barrier_semaphore()
+        partners = [here.to_z(1), here.to_z(2), here.to_z(3), here.to_x, here.to_y, here.to_c]
+        for device in partners:
+            pl.semaphore_signal(barrier, inc=1, device_id=device, device_id_type=MESH)
+        tok_copy.start()
+        cot_copy.start()
+        for name, shard in ((W_I, shard_I), (W_O, shard_O), (W_E, shard_E)):
+            whole = shard[...].astype(F32)
+            half = whole.shape[1] // 2
+            unit = jnp.concatenate([whole[:, :half], whole[:, half:]], axis=0)
+            s.G[name][z, own] = unit.astype(BF16)
+        s.G[W_R][z, own] = shard_R[0:48, :]
+        s.G[W_Q][z, own] = shard_R[48:96, :]
+        s.G[VEC][z, own] = shard_V[...]
+        for it in range(2):
+            s.SEEN[it, y] = jnp.broadcast_to(seen[2 * y + it], (8, 128))
+            s.AWAY[it] = jnp.broadcast_to(seen[2 * (1 - y) + it], (8, 128))
+        pl.semaphore_wait(barrier, len(partners))
+
+    def vectors():
+        for number in range(VECTORS):
+            group = s.G[VEC][:, :, number // 4, :].reshape(32, 128)
+            s.ROWS[pl.ds(number, 1), :] = collect(group, spread_matrix(number % 4), CHUNK, 0)
+        group = s.G[VEC][:, :, 2, :].reshape(32, 128)
+        for part in range(4):
+            cols = slice(768 * part, 768 * part + 768)
+            s.EB[:, cols] = collect(group, spread_matrix(None), 4 * CHUNK, 8 * part)
+        s.PB[:, 0:768] = vector(2)
+        s.PB[:, 768:1536] = jnp.zeros((1, 768), F32)
+        s.PB[:, 1536:2304] = vector(3)
+        sums[...] = jnp.zeros_like(sums)
+        s.EBG[...] = jnp.zeros_like(s.EBG)
+
+    def first_norm():
+        def one(block, carry):
+            it, half = block // 2, block % 2
+            rows = rows_at(128 * block, 128)
+            patch = s.SEEN[it, half][0:1, :].astype(F32)
+            frame = jnp.floor((patch + 0.5) * (1.0 / (GRID * GRID)))
+            inside = patch - frame * (GRID * GRID)
+            line = jnp.floor((inside + 0.5) * (1.0 / GRID))
+            across = inside - line * GRID
+            place = jnp.concatenate([tn(one_hot(v), table[...]) for v in (frame, line, across)], axis=1)
+            entry = s.TOK[it, half].astype(F32) + place
+            s.ENT[rows, :] = entry
+            unit, _ = normalise(entry)
+            normed = (unit * vector(0) + vector(1)).astype(BF16)
+            s.XB[rows, :] = normed
+            s.NRMT[:, lanes(128 * block, 128)] = normed.T
+            return carry
+
+        lax.fori_loop(0, 4, one, 0)
+
+    def spread_rows(name, target):
+        buf = s.G[name]
+        half = target.shape[1] // 2
+
+        def one(i, carry):
+            zz, pair = i // 4, 2 * (i % 4)
+            even = buf[zz, pair].astype(F32)
+            odd = buf[zz, pair + 1].astype(F32)
+            rows = pl.ds(pl.multiple_of(48 * i, 16), 48)
+            target[rows, :half] = jnp.concatenate([even[:24], odd[:24]], axis=0).astype(BF16)
+            target[rows, half:] = jnp.concatenate([even[24:], odd[24:]], axis=0).astype(BF16)
+            return carry
+
+        lax.fori_loop(0, 16, one, 0)
+
+    def project():
+        def one(n, carry):
+            cols = lanes(256 * n, 256)
+            s.PRJ[:, cols] = (nn(s.XB[...], s.WI[:, cols]) + s.PB[:, cols]).astype(BF16)
+            return carry
+
+        lax.fori_loop(0, 9, one, 0)
+
+    def attend(first, last):
+        def one(step, carry):
+            it, pair = step // 6, step % 6
+            rows = rows_at(256 * it, 256)
+            cols = lanes(128 * pair, 128)
+            q = s.PRJ[rows, cols]
+            k = s.PRJ[rows, lanes(768 + 128 * pair, 128)]
+            v = s.PRJ[rows, lanes(1536 + 128 * pair, 128)]
+            bias = live_bias(lengths[2 * y + it])
+            total = jnp.zeros((128, 256), F32)
+            for head in range(2):
+                mask = half_mask(head)
+                scores = nt(jnp.where(mask, k, 0), q) * SCORE_SCALE + bias
+                exponent = jnp.exp(scores - jnp.max(scores, axis=0, keepdims=True))
+                attention = exponent * (1.0 / jnp.sum(exponent, axis=0, keepdims=True))
+                low = attention.astype(BF16)
+                s.ATN[2 * step + head] = low
+                total = total + tn(jnp.where(mask, v, 0), low)
+            s.ATTT[cols, rows] = total.astype(BF16)
+            s.XB[rows, cols] = total.T.astype(BF16)
+            return carry
+
+        lax.fori_loop(first, last, one, 0)
+
+    def second_norm():
+        def one(it, carry):
+            rows = rows_at(256 * it, 256)
+            middle = s.ENT[rows, :] + nn(s.XB[rows, :], s.WO[...]) + vector(4)
+            s.MID[rows, :] = middle
+            unit, _ = normalise(middle)
+            second = (unit * vector(5) + vector(6)).astype(BF16)
+            s.XB[rows, :] = second
+            s.SECT[:, rows] = second.T
+            return carry
+
+        lax.fori_loop(0, 2, one, 0)
+
+    def expand(first, last):
+        def one(step, carry):
+            n, it = step // 2, step % 2
+            cols = lanes(256 * n, 256)
+            rows = rows_at(256 * it, 256)
+            expanded = nn(s.XB[rows, :], s.WE[:, cols]) + s.EB[:, cols]
+            normal = 0.5 * (1.0 + lax.erf(expanded * 0.7071067811865476))
+            density = jnp.exp(-0.5 * expanded * expanded) * 0.3989422804014327
+            s.ACT[rows, cols] = (expanded * normal).astype(BF16)
+            s.GP[rows, cols] = (normal + expanded * density).astype(BF16)
+            return carry
+
+        lax.fori_loop(first, last, one, 0)
+
+    def take_in():
+        def one(block, carry):
+            it, half = block // 2, block % 2
+            live = live_rows(lengths[2 * y + it], half, 128)
+            incoming = jnp.where(live, s.INC[it, half].astype(F32), 0.0)
+            s.INC[it, half] = incoming.astype(BF16)
+            sums[7:8, :] += jnp.sum(incoming, axis=0, keepdims=True)
+            return carry
+
+        lax.fori_loop(0, 4, one, 0)
+
+    def reduce_weight_grad():
+        def one(f, carry):
+            zz, xx = f // 2, f % 2
+            moved = s.ACT[:, lanes(384 * f, 384)].T
+            part = nn(moved, s.INC[...].reshape(512, 768))
+            units = part.reshape(4, 96, 768).astype(BF16)
+            s.P[W_R][zz, pl.ds(4 * xx, 4)] = units[:, :48]
+            s.P[W_Q][zz, pl.ds(4 * xx, 4)] = units[:, 48:]
+            return carry
+
+        lax.fori_loop(0, 8, one, 0)
+
+    def reduce_rows(zz):
+        return jnp.concatenate([s.G[W_R][zz], s.G[W_Q][zz]], axis=1).reshape(768, 768)
+
+    def expanded_grad(first, last):
+        def one(step, carry):
+            zz, it = step // 2, step % 2
+            rows = rows_at(256 * it, 256)
+            cols = lanes(768 * zz, 768)
+            incoming = s.INC[it].reshape(256, 768)
+            grad = (nt(incoming, reduce_rows(zz)) * s.GP[rows, cols].astype(F32)).astype(BF16)
+            s.GP[rows, cols] = grad
+            s.EBG[:, cols] += jnp.sum(grad.astype(F32), axis=0, keepdims=True)
+            return carry
+
+        lax.fori_loop(first, last, one, 0)
+
+    def weight_grad(name, moved, grad, first, last):
+        part, wide = s.P[name], 384
+        half = UNITS[name][1]
+
+        def one(step, carry):
+            n, m = step // 2, step % 2
+            left = grad[:, lanes(wide * n, wide)]
+            right = grad[:, lanes(half + wide * n, wide)]
+            block = nn(moved[rows_at(384 * m, 384), :], jnp.concatenate([left, right], axis=1))
+            for j in range(8):
+                for side in range(2):
+                    rows = slice(48 * j + 24 * side, 48 * j + 24 * side + 24)
+                    unit = jnp.concatenate([block[rows, :wide], block[rows, wide:]], axis=0)
+                    part[2 * m + j // 4, 2 * (j % 4) + side, :, lanes(wide * n, wide)] = unit.astype(BF16)
+            return carry
+
+        if first == 0:
+            gather[name].drain()
+        lax.fori_loop(2 * first, 2 * last, one, 0)
+
+    def finish_rows():
+        def one(it, carry):
+            rows = rows_at(256 * it, 256)
+            out = s.MID[rows, :] + vector(7)
+            for zz in range(4):
+                out = out + nn(s.ACT[rows, 768 * zz : 768 * zz + 768], reduce_rows(zz))
+            for half in range(2):
+                live = live_rows(lengths[2 * y + it], half, 128)
+                s.TOK[it, half] = jnp.where(live, out[128 * half : 128 * half + 128], 0.0).astype(BF16)
+            return carry
+
+        tok_out.wait_send()
+        lax.fori_loop(0, 2, one, 0)
+        out_copy.start()
+
+    def middle_back():
+        def one(it, carry):
+            rows = rows_at(256 * it, 256)
+            grad = nt(s.GP[rows, :], s.WE[...])
+            unit, inverse = normalise(s.MID[rows, :])
+            sums[5:6, :] += jnp.sum(grad * unit, axis=0, keepdims=True)
+            sums[6:7, :] += jnp.sum(grad, axis=0, keepdims=True)
+            incoming = s.INC[it].reshape(256, 768).astype(F32)
+            middle_grad = incoming + normalise_back(grad * vector(5), unit, inverse)
+            s.MID[rows, :] = middle_grad
+            branch = middle_grad.astype(BF16)
+            s.XB[rows, :] = branch
+            sums[4:5, :] += jnp.sum(branch.astype(F32), axis=0, keepdims=True)
+            return carry
+
+        lax.fori_loop(0, 2, one, 0)
+
+    def attended_back():
+        def one(it, carry):
+            rows = rows_at(256 * it, 256)
+            s.XB[rows, :] = nt(s.XB[rows, :], s.WO[...]).astype(BF16)
+            return carry
+
+        lax.fori_loop(0, 2, one, 0)
+
+    def attend_back(first, last):
+        def one(step, carry):
+            it, pair = step // 6, step % 6
+            rows = rows_at(256 * it, 256)
+            cols = lanes(128 * pair, 128)
+            k_cols, v_cols = lanes(768 + 128 * pair, 128), lanes(1536 + 128 * pair, 128)
+            q = s.PRJ[rows, cols]
+            k = s.PRJ[rows, k_cols]
+            v = s.PRJ[rows, v_cols]
+            grad = s.XB[rows, cols]
+            query_grad = jnp.zeros((128, 256), F32)
+            key_grad = jnp.zeros((256, 128), F32)
+            value_grad = jnp.zeros((256, 128), F32)
+            for head in range(2):
+                mask = half_mask(head)
+                mine_grad = jnp.where(mask, grad, 0)
+                weight_back = nt(v, mine_grad)
+                low = s.ATN[2 * step + head]
+                attention = low.astype(F32)
+                inner = jnp.sum(attention * weight_back, axis=0, keepdims=True)
+                scores_grad = (attention * (weight_back - inner)).astype(BF16)
+                query_grad = query_grad + tn(jnp.where(mask, k, 0), scores_grad)
+                key_grad = key_grad + nn(scores_grad, jnp.where(mask, q, 0))
+                value_grad = value_grad + nn(low, mine_grad)
+            query_low = (query_grad * SCORE_SCALE).T.astype(BF16)
+            value_low = value_grad.astype(BF16)
+            s.PRJ[rows, cols] = query_low
+            s.PRJ[rows, k_cols] = (key_grad * SCORE_SCALE).astype(BF16)
+            s.PRJ[rows, v_cols] = value_low
+            sums[2:3, cols] += jnp.sum(query_low.astype(F32), axis=0, keepdims=True)
+            sums[3:4, cols] += jnp.sum(value_low.astype(F32), axis=0, keepdims=True)
+            return carry
+
+        lax.fori_loop(first, last, one, 0)
+
+    def entry_back(half):
+        rows = [rows_at(256 * it + 128 * half, 128) for it in range(2)]
+
+        def both(ref):
+            return jnp.concatenate([ref[r, :] for r in rows], axis=0)
+
+        grad = nt(both(s.PRJ), s.WI[...])
+        unit, inverse = normalise(both(s.ENT))
+        sums[0:1, :] += jnp.sum(grad * unit, axis=0, keepdims=True)
+        sums[1:2, :] += jnp.sum(grad, axis=0, keepdims=True)
+        return rows, both(s.MID) + normalise_back(grad * vector(0), unit, inverse)
+
+    def entry_back_far():
+        _, out = entry_back(1 - y)
+        cot_out.wait_send()
+        for it in range(2):
+            s.INC[it, 1 - y] = out[128 * it : 128 * it + 128].astype(BF16)
+
+    def entry_back_near():
+        rows, out = entry_back(y)
+        for it in range(2):
+            s.ENT[rows[it], :] = out[128 * it : 128 * it + 128]
+        for copy in near_copies:
+            copy.start()
+
+    def deal_sums():
+        group = None
+        for number in range(VECTORS):
+            dealt = deal(sums[number : number + 1, :], spread_matrix(number % 4), CHUNK, 0)
+            group = dealt if number % 4 == 0 else group + dealt
+            if number % 4 == 3:
+                s.P[VEC][:, :, number // 4, :] = group.reshape(4, 8, 128)
+        group = jnp.zeros((32, 128), F32)
+        for part in range(4):
+            row = s.EBG[:, 768 * part : 768 * part + 768]
+            group = group + deal(row, spread_matrix(None), 4 * CHUNK, 8 * part)
+        s.P[VEC][:, :, 2, :] = group.reshape(4, 8, 128)
+        for row in range(3, 8):
+            s.P[VEC][:, :, row, :] = jnp.zeros((4, 8, 128), F32)
+
+    def give_spare(index):
+        pl.semaphore_signal(s.SPARE.at[index], inc=1, device_id=here.to_c, device_id_type=MESH)
+
+    def place_grad(number, ref):
+        cols = PIECES[number][1]
+        half = ref.shape[1] // 2
+        if cols is None:
+            cols = slice(0, half)
+        total = reduce[number].finish()
+        ref[:, cols] = total[:24]
+        ref[:, half + cols.start : half + cols.stop] = total[24:]
+
+    def take_grad():
+        grad_in.wait_recv()
+        for it in range(2):
+            s.ENT[rows_at(256 * it + 128 * (1 - y), 128), :] = s.TGR[it].astype(F32)
+        for copy in far_copies:
+            copy.start()
+
+    def end():
+        for made in (seen_out, lay_out, grad_out):
+            made.wait_send()
+        out_copy.wait()
+        for copy in near_copies + far_copies:
+            copy.wait()
+        for one in (*gather, *reduce):
+            one.drain()
+
+    start()
+    gather[W_O].begin_x()
+    gather[W_E].begin_y()
+    gather[VEC].begin_x()
+    gather[W_Q].begin_y()
+    gather[W_O].begin_y()
+    gather[W_O].begin_z()
+    gather[VEC].begin_y()
+    gather[W_I].begin_x()
+    gather[W_E].begin_x()
+    gather[VEC].begin_z()
+    gather[W_I].begin_z()
+    gather[VEC].pass_on(3)
+    gather[W_O].pass_on(2)
+    gather[W_Q].begin_x()
+    gather[W_I].begin_y()
+    gather[W_O].pass_on(1)
+    gather[W_O].relay(2)
+    gather[VEC].pass_on(1)
+    gather[VEC].pass_on(2)
+    gather[W_E].begin_z()
+    gather[W_O].pass_on(3)
+    gather[W_I].pass_on(1)
+    gather[W_I].pass_on(3)
+    gather[W_O].relay(3)
+    gather[VEC].relay(3)
+    gather[W_I].pass_on(2)
+    gather[W_I].relay(3)
+    gather[W_O].relay(0)
+    gather[W_I].relay(1)
+    gather[VEC].relay(2)
+    gather[W_I].relay(0)
+    gather[VEC].relay(1)
+    gather[VEC].relay(0)
+    seen_out.start()
+    tok_out.start()
+    gather[W_O].relay(1)
+    gather[W_I].relay(2)
+    gather[W_I].sides_to_core()
+    gather[W_O].own_to_core()
+    gather[VEC].sides_to_core()
+    gather[VEC].own_to_core()
+    gather[W_Q].own_along_z()
+    gather[W_E].pass_on(3)
+    gather[W_O].sides_to_core()
+    gather[W_R].begin_z()
+    gather[VEC].corner()
+    seen_in.wait_recv()
+    gather[W_O].corner()
+    gather[W_O].from_core()
+    gather[W_I].own_to_core()
+    gather[W_E].pass_on(2)
+    gather[VEC].from_core()
+    gather[W_E].pass_on(1)
+    gather[W_I].corner()
+    gather[W_I].from_core()
+    gather[W_E].relay(0)
+    tok_copy.wait()
+    tok_in.wait_recv()
+    gather[W_Q].relay()
+    vectors()
+    first_norm()
+    gather[W_E].relay(3)
+    spread_rows(W_I, s.WI)
+    project()
+    gather[W_E].relay(2)
+    spread_rows(W_O, s.WO)
+    attend(0, 6)
+    gather[W_E].relay(1)
+    gather[W_R].begin_y()
+    gather[W_R].begin_x()
+    gather[W_E].own_to_core()
+    gather[W_R].pass_on(3)
+    gather[W_R].pass_on(1)
+    gather[W_Q].corner()
+    gather[W_E].sides_to_core()
+    gather[W_Q].to_core(0)
+    gather[W_R].pass_on(2)
+    cot_out.start()
+    attend(6, 12)
+    gather[W_E].corner()
+    gather[W_R].own_to_core()
+    second_norm()
+    gather[W_R].relay(0)
+    gather[W_Q].to_core(1)
+    gather[W_E].from_core()
+    spread_rows(W_E, s.WE)
+    expand(0, 12)
+    gather[W_R].relay(3)
+    gather[W_R].relay(2)
+    gather[W_R].relay(1)
+    expand(12, 24)
+    gather[W_Q].to_core(3)
+    cot_copy.wait()
+    cot_in.wait_recv()
+    gather[W_R].sides_to_core()
+    gather[W_Q].to_core(2)
+    take_in()
+    gather[W_R].corner()
+    reduce_weight_grad()
+    gather[W_R].from_core()
+    gather[W_Q].from_core()
+    reduce[D_R].core_send()
+    expanded_grad(0, 4)
+    reduce[D_R].core_add(0)
+    reduce[D_Q].core_send()
+    reduce[D_R].core_add(1)
+    expanded_grad(4, 8)
+    reduce[D_R].core_add(2)
+    reduce[D_R].core_add(3)
+    give_spare(0)
+    reduce[D_Q].core_add(0)
+    weight_grad(W_E, s.SECT, s.GP, 0, 2)
+    reduce[D_R].relay()
+    reduce[D_EA].core_send(s.SPARE.at[0])
+    finish_rows()
+    reduce[D_EA].core_add(0)
+    reduce[D_Q].core_add(1)
+    lay_out.start()
+    weight_grad(W_E, s.SECT, s.GP, 2, 4)
+    reduce[D_Q].core_add(2)
+    reduce[D_EA].core_add(1)
+    reduce[D_Q].core_add(3)
+    give_spare(1)
+    reduce[D_R].sides()
+    reduce[D_EB].core_send(s.SPARE.at[1])
+    middle_back()
+    reduce[D_EB].core_add(0)
+    weight_grad(W_O, s.ATTT, s.XB, 0, 1)
+    reduce[D_EA].core_add(2)
+    reduce[D_EA].relay()
+    reduce[D_EB].core_add(1)
+    reduce[D_EA].core_add(3)
+    give_spare(2)
+    reduce[D_EB].core_add(2)
+    attended_back()
+    reduce[D_O].core_send()
+    attend_back(0, 6)
+    reduce[D_O].core_add(0)
+    attend_back(6, 12)
+    reduce[D_O].core_add(1)
+    reduce[D_EB].relay()
+    weight_grad(W_I, s.NRMT, s.PRJ, 0, 2)
+    reduce[D_IA].core_send(s.SPARE.at[2])
+    weight_grad(W_I, s.NRMT, s.PRJ, 2, 3)
+    reduce[D_IA].core_add(0)
+    reduce[D_EB].core_add(3)
+    give_spare(3)
+    reduce[D_EB].sides()
+    reduce[D_IB].core_send(s.SPARE.at[3])
+    reduce[D_O].core_add(2)
+    reduce[D_O].relay()
+    reduce[D_O].core_add(3)
+    reduce[D_EA].sides()
+    reduce[D_Q].relay()
+    reduce[D_IB].core_add(0)
+    reduce[D_IA].core_add(1)
+    reduce[D_IA].core_add(2)
+    entry_back_far()
+    reduce[D_IA].relay()
+    entry_back_near()
+    deal_sums()
+    reduce[D_Q].sides()
+    reduce[D_V].core_send()
+    lay_in.wait_recv()
+    reduce[D_O].sides()
+    reduce[D_IA].core_add(3)
+    reduce[D_V].core_add(0)
+    reduce[D_IB].core_add(1)
+    reduce[D_IB].core_add(2)
+    reduce[D_IB].relay()
+    reduce[D_IA].sides()
+    reduce[D_V].core_add(1)
+    reduce[D_V].core_add(2)
+    place_grad(D_EA, grad_E)
+    reduce[D_V].core_add(3)
+    reduce[D_V].relay()
+    reduce[D_IB].core_add(3)
+    grad_out.start()
+    grad_R[48:96, :] = reduce[D_Q].finish()
+    reduce[D_V].sides()
+    grad_R[0:48, :] = reduce[D_R].finish()
+    place_grad(D_O, grad_O)
+    place_grad(D_EB, grad_E)
+    reduce[D_IB].sides()
+    grad_V[...] = reduce[D_V].finish()
+    place_grad(D_IA, grad_I)
+    place_grad(D_IB, grad_I)
+    take_grad()
+    end()
+
+
+UNITS = ((48, 1152), (48, 384), (48, 1536), (48, 768), (48, 768), (8, 128))
+
+
+PIECES = (
+    (W_I, slice(0, 768), 1),
+    (W_I, slice(768, 1152), 2),
+    (W_O, None, 0),
+    (W_E, slice(0, 768), 1),
+    (W_E, slice(768, 1536), 2),
+    (W_R, None, 1),
+    (W_Q, None, 2),
+    (VEC, None, 3),
+)
+
+
+def scratch_list():
+    dma, vmem = pltpu.SemaphoreType.DMA, pltpu.VMEM
+    shapes = dict(
+        SWS=dma((5,)),
+        SWR=dma((5,)),
+        LOC=dma((7,)),
+        SPARE=pltpu.SemaphoreType.REGULAR((4,)),
+        TOK=vmem((2, 2, 128, 768), BF16),
+        INC=vmem((2, 2, 128, 768), BF16),
+        SEEN=vmem((2, 2, 8, 128), jnp.int32),
+        AWAY=vmem((2, 8, 128), jnp.int32),
+        ROWS=vmem((8, 768), F32),
+        EB=vmem((1, 3072), F32),
+        PB=vmem((1, 2304), F32),
+        SUMS=vmem((8, 768), F32),
+        EBG=vmem((1, 3072), F32),
+        WI=vmem((768, 2304), BF16),
+        WO=vmem((768, 768), BF16),
+        WE=vmem((768, 3072), BF16),
+        ENT=vmem((512, 768), F32),
+        MID=vmem((512, 768), F32),
+        XB=vmem((512, 768), BF16),
+        NRMT=vmem((768, 512), BF16),
+        ATTT=vmem((768, 512), BF16),
+        SECT=vmem((768, 512), BF16),
+        PRJ=vmem((512, 2304), BF16),
+        ATN=vmem((24, 256, 256), BF16),
+        ACT=vmem((512, 3072), BF16),
+        GP=vmem((512, 3072), BF16),
+        TGR=vmem((2, 128, 768), BF16),
+    )
+    many = dict(G=[], GS=[], GQ=[], P=[], RC=[], R1=[], R2=[], RZ=[], RS=[], RQ=[])
+    for name in TENSORS:
+        kind = F32 if name == VEC else BF16
+        unit = UNITS[name]
+        plane = name == W_Q
+        many["G"].append(vmem((4, 8, *unit), kind))
+        many["GS"].append(dma((SEMS,)))
+        many["GQ"].append(dma((SEMS,)))
+        if name in (W_R, W_Q, VEC):
+            many["P"].append(vmem((4, 8, *unit), kind))
+        if name not in (W_I, W_E):
+            many["RC"].append(vmem((4, 4, *unit), kind))
+        many["R1"].append(vmem(unit if plane else (4, *unit), kind))
+        many["R2"].append(vmem((2, *unit) if plane else (4, 2, *unit), kind))
+        many["RZ"].append(vmem((3, 4, *unit) if plane else (3, *unit), kind))
+    for _ in SUMS:
+        many["RS"].append(dma((SEMS,)))
+        many["RQ"].append(dma((SEMS,)))
+    return shapes, many
+
+
+class Store:
+    def __init__(self, refs):
+        shapes, many = scratch_list()
+        refs = list(refs)
+        for name in shapes:
+            setattr(self, name, refs.pop(0))
+        for name, listed in many.items():
+            setattr(self, name, [refs.pop(0) for _ in listed])
+        self.P = self.G[:3] + self.P
+
+
+def position_table():
+    step = np.arange(16, dtype=np.float64)[:, None]
+    channel = np.arange(256)
+    angle = step * np.power(10000.0, -(channel // 2) / 128.0)
+    whole = np.where(channel % 2 == 0, np.sin(angle), np.cos(angle)).astype(np.float32)
+    high = whole.astype(jnp.bfloat16)
+    rest = whole - high.astype(np.float32)
+    middle = rest.astype(jnp.bfloat16)
+    low = (rest - middle.astype(np.float32)).astype(jnp.bfloat16)
+    return np.concatenate([high, middle, low], axis=0)
+
+
+def fused_body(
+    tokens, visible, lengths, first_gain, first_shift, input_weight, query_bias, value_bias,
+    output_weight, output_bias, second_gain, second_shift, expand_weight, expand_bias,
+    reduce_weight, reduce_bias, cotangent,
+):
+    chunks = jnp.concatenate(
+        [
+            jnp.stack(
+                [first_gain, first_shift, query_bias, value_bias, output_bias, second_gain, second_shift, reduce_bias]
+            ),
+            expand_bias.reshape(4, CHUNK),
+        ],
+        axis=0,
+    ).astype(F32)
+    shard_V = jnp.pad(chunks, ((0, 20), (0, 32 - CHUNK))).reshape(8, 128)
+    hbm = pl.BlockSpec(memory_space=pl.ANY)
+    vmem = pl.BlockSpec(memory_space=pltpu.VMEM)
+    smem = pl.BlockSpec(memory_space=pltpu.SMEM)
+    shapes, many = scratch_list()
+    results = [
+        jax.ShapeDtypeStruct((4, 128, 768), BF16),
+        jax.ShapeDtypeStruct((4, 128, 768), F32),
+        jax.ShapeDtypeStruct(input_weight.shape, F32),
+        jax.ShapeDtypeStruct(output_weight.shape, F32),
+        jax.ShapeDtypeStruct(expand_weight.shape, F32),
+        jax.ShapeDtypeStruct(reduce_weight.shape, F32),
+        jax.ShapeDtypeStruct((8, 128), F32),
+    ]
+    layer_out, tokens_grad, grad_I, grad_O, grad_E, grad_R, grad_V = pl.pallas_call(
+        fused_kernel,
+        name="layer",
+        out_shape=results,
+        in_specs=[smem, hbm, hbm, vmem, vmem, vmem, vmem, vmem, vmem, vmem],
+        out_specs=[hbm, hbm, vmem, vmem, vmem, vmem, vmem],
+        scratch_shapes=[*shapes.values(), *(shape for listed in many.values() for shape in listed)],
+        compiler_params=pltpu.CompilerParams(
+            collective_id=0, has_side_effects=True, vmem_limit_bytes=VMEM_BYTES
+        ),
+    )(
+        lengths, tokens[:, 0], cotangent[:, 0], visible, input_weight, output_weight, expand_weight,
+        reduce_weight, shard_V, jnp.asarray(position_table()),
+    )
+    dealt = grad_V.reshape(32, 32)[:12, :CHUNK]
+    return (
+        layer_out[:, None], tokens_grad[:, None], dealt[0], dealt[1], grad_I, dealt[2], dealt[3], grad_O,
+        dealt[4], dealt[5], dealt[6], grad_E, dealt[8:12].reshape(4 * CHUNK), grad_R, dealt[7],
+    )
+
+
+VMEM_BYTES = 67000000
+
+
 def solution(mesh):
     in_specs = (
         P("items", "seq", None, None),
@@ -391,4 +1541,6 @@
         P(("items", "seq"), None),
         P(("items", "seq")),
     )
-    return jax.shard_map(body, mesh=mesh, in_specs=in_specs, out_specs=out_specs, check_vma=False)
+    sizes = (mesh.shape["items"], mesh.shape["seq"])
+    chosen = fused_body if sizes == (Z_SIZE * 4, 2) else general_body
+    return jax.shard_map(chosen, mesh=mesh, in_specs=in_specs, out_specs=out_specs, check_vma=False)

time: 964 us -> 159 us (0.16); the launches traced: 953 us -> 159 us
  waiting for transfers between devices: 589 us -> 0 us
  Pallas kernels: 0 us -> 148 us
  blocking collectives: 127 us -> 0 us
  matrix products: 111 us -> 0 us
  other arithmetic: 61 us -> 0.01 us
  local copies, waits for them, and re-layouts: 47.8 us -> 10.2 us
  between operations: 17.1 us -> 0.68 us
    reduce_scatter x8 -> x0, waiting for transfers between devices: 452 us -> none  [the longest x1 142 us: body(): lax.psum_scatter(grads[11], ('items', 'seq'), scatter_dimension=0, tiled=...]
    pallas_call x0 -> x1, Pallas kernels: none -> 148 us  [fused_body(): pl.pallas_call(fused_kernel, name='layer', out_shape=results, in_specs=[s...]
    all_gather x4 -> x0, waiting for transfers between devices: 134 us -> none  [the longest x1 61.1 us: body(): lax.all_gather(shards[9], ('items', 'seq'), axis=0, tiled=True)]
    dot_general x36 -> x0, matrix products: 111 us -> none  [the longest x8 40.2 us: against(): lax.dot_general(left, right, (((1,), (1,)), ((), ())), preferred_element_...]
    unnamed x2 -> x0, blocking collectives: 83.2 us -> none
    all_gather x4 -> x0, blocking collectives: 43.9 us -> none  [the longest x2 22.4 us: micro_batch(): lax.all_gather(keys_here, 'seq', axis=1, tiled=True)]
    reduce_sum x16 -> x0, other arithmetic: 35.9 us -> none  [the longest x5 16.1 us: layer_norm(): centre = rows_in - jnp.mean(rows_in, axis=-1, keepdims=True)]
    unnamed x399 -> x16, local copies, waits for them, and re-layouts: 25.2 us -> 5.97 us
  transfers between devices with their start and end apart: 12 -> 0, of which waited for: 11 -> 0; matrix products, arithmetic and copies ran while one was open for 14% -> 0% of each run, Pallas kernels for 0% -> 0%
where the time goes in v2:
time: 159 us
  Pallas kernels  148 us (93%)
  local copies, waits for them, and re-layouts  10.2 us (6%)
    pallas_call x1, Pallas kernels, fused_body(): pl.pallas_call(fused_kernel, name='layer', out_shape=results, in_specs=[s...  148 us
    unnamed x16, local copies, waits for them, and re-layouts  5.97 us

profile of v2, /device:TPU:0, one launch (start us, length us, event | category | flops | bytes accessed | tf_op | source)
XLA Modules:
  0.0 159.1 jit_solution(1719161092238512202)
XLA Ops:
  0.6 0.7 reshape.44
  1.4 0.8 concatenate.3
  2.2 0.7 reshape.50.shard_V
  2.9 148.3 %layer.1 = (bf16[4,128,768]{2,1,0:T(8,128)(2,1)}, f32[4,128,768]{2,1,0:T(8,128)}, f32[24,2304]{1,0:T(8,128)}, f32[24,768]{1,0:T(8,128)}, f32[24,3072]{1,0:T(8,12...) custom-call(s32[4]{0:T(128)} %lengths.1, bf16[4,128,768]{2,1,0:T(8,128)(2,1)} %bitcast.34, bf16[4,128,768]{2,1,0:T(8,128)(2,1)} %bitcast.35, ...), custom_call_target="tpu_custom_call" | custom-call | tf_op jit(solution)/shard_map/layer/pallas_call | solution.py:1483
  151.1 0.0 copy-start
  151.1 0.9 reshape.47
  152.0 0.5 slice_bitcast_fusion
  152.6 0.6 reshape.48
  153.1 2.1 %copy.41 = bf16[4,1,128,768]{3,2,1,0:T(8,128)(2,1)} copy(bf16[4,1,128,768]{3,2,1,0:T(8,128)(2,1)} %bitcast.33) | data formatting | bytes 1572864
  155.2 0.0 copy-done
  155.2 0.0 copy-start.3
  155.2 0.0 copy-start.4
  155.2 0.0 copy-start.2
  155.2 0.0 copy-start.1
  155.2 1.1 copy.42
  156.4 0.0 copy-done.3
  156.4 0.7 copy.43
  157.1 0.0 copy-done.4
  157.1 0.6 copy.44
  157.7 0.0 copy-done.2
  157.7 0.7 copy.45
  158.4 0.0 copy-done.1
  158.4 0.7 copy.46
  (2 shorter events, 0.0 us)
Async XLA Ops:
  151.1 4.1 %copy-start = (f32[4,128,768]{2,1,0:T(8,128)S(1)}, f32[4,128,768]{2,1,0:T(8,128)}, u32[]{:S(2)}) copy-start(f32[4,128,768]{2,1,0:T(8,128)} %get-tuple-element.23) | copy-start | bytes 4718596
  155.2 1.2 copy-start.3
  155.2 1.9 %copy-start.4 = (f32[24,768]{1,0:T(8,128)S(1)}, f32[24,768]{1,0:T(8,128)}, u32[]{:S(2)}) copy-start(f32[24,768]{1,0:T(8,128)} %get-tuple-element.74) | copy-start | bytes 221188
  155.2 2.5 %copy-start.2 = (f32[24,3072]{1,0:T(8,128)S(1)}, f32[24,3072]{1,0:T(8,128)}, u32[]{:S(2)}) copy-start(f32[24,3072]{1,0:T(8,128)} %get-tuple-element.78) | copy-start | bytes 884740
  155.2 3.2 %copy-start.1 = (f32[96,768]{1,0:T(8,128)S(1)}, f32[96,768]{1,0:T(8,128)}, u32[]{:S(2)}) copy-start(f32[96,768]{1,0:T(8,128)} %get-tuple-element.80) | copy-start | bytes 884740

commit v3 on v2

--- a/solution.py
+++ b/solution.py
@@ -788,7 +788,8 @@
 
 
 def fused_kernel(
-    lengths, tokens, cotangent, seen, shard_I, shard_O, shard_E, shard_R, shard_V, table,
+    lengths, tokens, cotangent, seen, shard_I, shard_O, shard_E, shard_R, table,
+    v0, v1, v2, v3, v4, v5, v6, v7, v8,
     layer_out, tokens_grad, grad_I, grad_O, grad_E, grad_R, grad_V, *refs,
 ):
     s = Store(refs)
@@ -854,7 +855,24 @@
             s.G[name][z, own] = unit.astype(BF16)
         s.G[W_R][z, own] = shard_R[0:48, :]
         s.G[W_Q][z, own] = shard_R[48:96, :]
-        s.G[VEC][z, own] = shard_V[...]
+        s.STAGE[...] = jnp.zeros_like(s.STAGE)
+        for number, ref in enumerate((v0, v1, v2, v3, v4, v5, v6, v7)):
+            s.STAGE[number : number + 1, 0:CHUNK] = ref[...].astype(F32)
+        s.STAGE[8:9, 0 : 4 * CHUNK] = v8[...].astype(F32)
+        s.G[VEC][z, own] = jnp.zeros((8, 128), F32)
+        for row in range(2):
+            joined = s.STAGE[4 * row : 4 * row + 1, :]
+            for slot in range(1, 4):
+                joined = joined + pltpu.roll(s.STAGE[4 * row + slot : 4 * row + slot + 1, :], 32 * slot, 1)
+            s.G[VEC][z, own, row : row + 1, :] = joined
+        long_row = s.STAGE[8:9, :]
+        lane = lax.broadcasted_iota(jnp.int32, (1, 128), 1)
+        joined = jnp.zeros((1, 128), F32)
+        for slot in range(4):
+            moved = pltpu.roll(long_row, 8 * slot, 1) if slot else long_row
+            inside = jnp.logical_and(lane >= 32 * slot, lane < 32 * slot + CHUNK)
+            joined = jnp.where(inside, moved, joined)
+        s.G[VEC][z, own, 2:3, :] = joined
         for it in range(2):
             s.SEEN[it, y] = jnp.broadcast_to(seen[2 * y + it], (8, 128))
             s.AWAY[it] = jnp.broadcast_to(seen[2 * (1 - y) + it], (8, 128))
@@ -892,7 +910,7 @@
             s.NRMT[:, lanes(128 * block, 128)] = normed.T
             return carry
 
-        lax.fori_loop(0, 4, one, 0)
+        lax.fori_loop(0, 4, one, 0, unroll=4)
 
     def spread_rows(name, target):
         buf = s.G[name]
@@ -911,11 +929,11 @@
 
     def project():
         def one(n, carry):
-            cols = lanes(256 * n, 256)
+            cols = lanes(1152 * n, 1152)
             s.PRJ[:, cols] = (nn(s.XB[...], s.WI[:, cols]) + s.PB[:, cols]).astype(BF16)
             return carry
 
-        lax.fori_loop(0, 9, one, 0)
+        lax.fori_loop(0, 2, one, 0)
 
     def attend(first, last):
         def one(step, carry):
@@ -939,7 +957,7 @@
             s.XB[rows, cols] = total.T.astype(BF16)
             return carry
 
-        lax.fori_loop(first, last, one, 0)
+        lax.fori_loop(first, last, one, 0, unroll=3)
 
     def second_norm():
         def one(it, carry):
@@ -952,12 +970,12 @@
             s.SECT[:, rows] = second.T
             return carry
 
-        lax.fori_loop(0, 2, one, 0)
+        lax.fori_loop(0, 2, one, 0, unroll=2)
 
     def expand(first, last):
         def one(step, carry):
             n, it = step // 2, step % 2
-            cols = lanes(256 * n, 256)
+            cols = lanes(768 * n, 768)
             rows = rows_at(256 * it, 256)
             expanded = nn(s.XB[rows, :], s.WE[:, cols]) + s.EB[:, cols]
             normal = 0.5 * (1.0 + lax.erf(expanded * 0.7071067811865476))
@@ -989,7 +1007,7 @@
             s.P[W_Q][zz, pl.ds(4 * xx, 4)] = units[:, 48:]
             return carry
 
-        lax.fori_loop(0, 8, one, 0)
+        lax.fori_loop(0, 8, one, 0, unroll=2)
 
     def reduce_rows(zz):
         return jnp.concatenate([s.G[W_R][zz], s.G[W_Q][zz]], axis=1).reshape(768, 768)
@@ -1005,7 +1023,7 @@
             s.EBG[:, cols] += jnp.sum(grad.astype(F32), axis=0, keepdims=True)
             return carry
 
-        lax.fori_loop(first, last, one, 0)
+        lax.fori_loop(first, last, one, 0, unroll=4)
 
     def weight_grad(name, moved, grad, first, last):
         part, wide = s.P[name], 384
@@ -1025,7 +1043,7 @@
 
         if first == 0:
             gather[name].drain()
-        lax.fori_loop(2 * first, 2 * last, one, 0)
+        lax.fori_loop(2 * first, 2 * last, one, 0, unroll=2)
 
     def finish_rows():
         def one(it, carry):
@@ -1065,7 +1083,7 @@
             s.XB[rows, :] = nt(s.XB[rows, :], s.WO[...]).astype(BF16)
             return carry
 
-        lax.fori_loop(0, 2, one, 0)
+        lax.fori_loop(0, 2, one, 0, unroll=2)
 
     def attend_back(first, last):
         def one(step, carry):
@@ -1100,7 +1118,7 @@
             sums[3:4, cols] += jnp.sum(value_low.astype(F32), axis=0, keepdims=True)
             return carry
 
-        lax.fori_loop(first, last, one, 0)
+        lax.fori_loop(first, last, one, 0, unroll=6)
 
     def entry_back(half):
         rows = [rows_at(256 * it + 128 * half, 128) for it in range(2)]
@@ -1171,193 +1189,193 @@
             one.drain()
 
     start()
+    tok_out.start()
+    gather[VEC].begin_x()
     gather[W_O].begin_x()
-    gather[W_E].begin_y()
-    gather[VEC].begin_x()
-    gather[W_Q].begin_y()
+    gather[VEC].begin_z()
+    gather[VEC].begin_y()
     gather[W_O].begin_y()
+    seen_out.start()
+    gather[W_E].begin_x()
+    gather[W_I].begin_y()
+    gather[W_Q].begin_x()
+    gather[W_I].begin_x()
+    gather[W_I].begin_z()
+    gather[W_I].pass_on(1)
+    gather[VEC].relay(0)
     gather[W_O].begin_z()
-    gather[VEC].begin_y()
-    gather[W_I].begin_x()
-    gather[W_E].begin_x()
-    gather[VEC].begin_z()
-    gather[W_I].begin_z()
+    gather[VEC].pass_on(1)
+    gather[W_E].begin_z()
+    gather[W_I].pass_on(3)
+    gather[VEC].pass_on(2)
+    gather[W_I].pass_on(2)
+    seen_in.wait_recv()
     gather[VEC].pass_on(3)
-    gather[W_O].pass_on(2)
-    gather[W_Q].begin_x()
-    gather[W_I].begin_y()
-    gather[W_O].pass_on(1)
-    gather[W_O].relay(2)
-    gather[VEC].pass_on(1)
-    gather[VEC].pass_on(2)
-    gather[W_E].begin_z()
-    gather[W_O].pass_on(3)
-    gather[W_I].pass_on(1)
-    gather[W_I].pass_on(3)
-    gather[W_O].relay(3)
-    gather[VEC].relay(3)
-    gather[W_I].pass_on(2)
-    gather[W_I].relay(3)
-    gather[W_O].relay(0)
-    gather[W_I].relay(1)
-    gather[VEC].relay(2)
     gather[W_I].relay(0)
     gather[VEC].relay(1)
-    gather[VEC].relay(0)
-    seen_out.start()
-    tok_out.start()
-    gather[W_O].relay(1)
-    gather[W_I].relay(2)
-    gather[W_I].sides_to_core()
-    gather[W_O].own_to_core()
-    gather[VEC].sides_to_core()
+    gather[W_Q].own_along_z()
+    gather[W_E].begin_y()
     gather[VEC].own_to_core()
-    gather[W_Q].own_along_z()
-    gather[W_E].pass_on(3)
-    gather[W_O].sides_to_core()
-    gather[W_R].begin_z()
-    gather[VEC].corner()
-    seen_in.wait_recv()
-    gather[W_O].corner()
-    gather[W_O].from_core()
-    gather[W_I].own_to_core()
-    gather[W_E].pass_on(2)
-    gather[VEC].from_core()
-    gather[W_E].pass_on(1)
-    gather[W_I].corner()
-    gather[W_I].from_core()
-    gather[W_E].relay(0)
+    gather[W_I].relay(1)
+    gather[W_I].relay(3)
+    gather[W_Q].begin_y()
+    gather[W_O].pass_on(1)
     tok_copy.wait()
     tok_in.wait_recv()
+    gather[W_I].relay(2)
+    gather[VEC].relay(3)
+    gather[VEC].relay(2)
+    gather[W_O].pass_on(3)
+    gather[W_O].pass_on(2)
+    gather[W_R].begin_z()
+    gather[W_I].sides_to_core()
+    gather[W_E].relay(0)
+    gather[W_E].pass_on(3)
+    gather[W_E].pass_on(1)
+    gather[VEC].sides_to_core()
+    gather[W_O].relay(3)
+    gather[W_E].pass_on(2)
+    gather[W_I].corner()
+    gather[VEC].corner()
+    gather[W_I].own_to_core()
+    gather[W_E].own_to_core()
+    gather[W_E].relay(3)
+    gather[W_O].relay(2)
+    gather[VEC].from_core()
+    vectors()
+    gather[W_O].relay(1)
+    gather[W_O].relay(0)
+    gather[W_I].from_core()
+    gather[W_O].own_to_core()
+    gather[W_R].begin_y()
+    gather[W_O].sides_to_core()
+    spread_rows(W_I, s.WI)
+    first_norm()
     gather[W_Q].relay()
-    vectors()
-    first_norm()
-    gather[W_E].relay(3)
-    spread_rows(W_I, s.WI)
+    gather[W_E].relay(1)
     project()
+    attend(0, 6)
     gather[W_E].relay(2)
+    gather[W_E].sides_to_core()
+    gather[W_R].begin_x()
+    gather[W_R].pass_on(2)
+    gather[W_O].corner()
+    gather[W_R].pass_on(1)
+    attend(6, 12)
+    gather[W_Q].corner()
+    gather[W_R].pass_on(3)
+    cot_out.start()
+    gather[W_E].corner()
+    gather[W_Q].to_core(0)
+    gather[W_O].from_core()
     spread_rows(W_O, s.WO)
-    attend(0, 6)
-    gather[W_E].relay(1)
-    gather[W_R].begin_y()
-    gather[W_R].begin_x()
-    gather[W_E].own_to_core()
-    gather[W_R].pass_on(3)
-    gather[W_R].pass_on(1)
-    gather[W_Q].corner()
-    gather[W_E].sides_to_core()
-    gather[W_Q].to_core(0)
-    gather[W_R].pass_on(2)
-    cot_out.start()
-    attend(6, 12)
-    gather[W_E].corner()
-    gather[W_R].own_to_core()
+    gather[W_Q].to_core(1)
     second_norm()
     gather[W_R].relay(0)
-    gather[W_Q].to_core(1)
     gather[W_E].from_core()
     spread_rows(W_E, s.WE)
-    expand(0, 12)
+    expand(0, 4)
+    gather[W_R].relay(2)
+    expand(4, 8)
     gather[W_R].relay(3)
-    gather[W_R].relay(2)
     gather[W_R].relay(1)
-    expand(12, 24)
-    gather[W_Q].to_core(3)
+    gather[W_Q].to_core(2)
     cot_copy.wait()
     cot_in.wait_recv()
     gather[W_R].sides_to_core()
-    gather[W_Q].to_core(2)
+    gather[W_R].own_to_core()
+    gather[W_Q].to_core(3)
     take_in()
     gather[W_R].corner()
     reduce_weight_grad()
+    reduce[D_R].core_send()
+    gather[W_Q].from_core()
     gather[W_R].from_core()
-    gather[W_Q].from_core()
-    reduce[D_R].core_send()
     expanded_grad(0, 4)
     reduce[D_R].core_add(0)
     reduce[D_Q].core_send()
+    expanded_grad(4, 8)
     reduce[D_R].core_add(1)
-    expanded_grad(4, 8)
     reduce[D_R].core_add(2)
     reduce[D_R].core_add(3)
     give_spare(0)
     reduce[D_Q].core_add(0)
     weight_grad(W_E, s.SECT, s.GP, 0, 2)
+    reduce[D_Q].core_add(1)
+    reduce[D_EA].core_send(s.SPARE.at[0])
     reduce[D_R].relay()
-    reduce[D_EA].core_send(s.SPARE.at[0])
+    reduce[D_Q].core_add(2)
     finish_rows()
     reduce[D_EA].core_add(0)
-    reduce[D_Q].core_add(1)
+    weight_grad(W_E, s.SECT, s.GP, 2, 4)
     lay_out.start()
-    weight_grad(W_E, s.SECT, s.GP, 2, 4)
-    reduce[D_Q].core_add(2)
     reduce[D_EA].core_add(1)
+    middle_back()
     reduce[D_Q].core_add(3)
     give_spare(1)
-    reduce[D_R].sides()
     reduce[D_EB].core_send(s.SPARE.at[1])
-    middle_back()
-    reduce[D_EB].core_add(0)
     weight_grad(W_O, s.ATTT, s.XB, 0, 1)
     reduce[D_EA].core_add(2)
+    attended_back()
     reduce[D_EA].relay()
+    reduce[D_EB].core_add(0)
+    reduce[D_R].sides()
+    attend_back(0, 6)
     reduce[D_EB].core_add(1)
+    attend_back(6, 12)
+    weight_grad(W_I, s.NRMT, s.PRJ, 0, 2)
+    reduce[D_EB].core_add(2)
+    weight_grad(W_I, s.NRMT, s.PRJ, 2, 3)
+    reduce[D_EB].relay()
     reduce[D_EA].core_add(3)
     give_spare(2)
-    reduce[D_EB].core_add(2)
-    attended_back()
-    reduce[D_O].core_send()
-    attend_back(0, 6)
-    reduce[D_O].core_add(0)
-    attend_back(6, 12)
-    reduce[D_O].core_add(1)
-    reduce[D_EB].relay()
-    weight_grad(W_I, s.NRMT, s.PRJ, 0, 2)
     reduce[D_IA].core_send(s.SPARE.at[2])
-    weight_grad(W_I, s.NRMT, s.PRJ, 2, 3)
-    reduce[D_IA].core_add(0)
+    reduce[D_EA].sides()
     reduce[D_EB].core_add(3)
     give_spare(3)
-    reduce[D_EB].sides()
+    reduce[D_IA].core_add(0)
     reduce[D_IB].core_send(s.SPARE.at[3])
-    reduce[D_O].core_add(2)
-    reduce[D_O].relay()
-    reduce[D_O].core_add(3)
-    reduce[D_EA].sides()
-    reduce[D_Q].relay()
-    reduce[D_IB].core_add(0)
+    reduce[D_O].core_send()
+    entry_back_far()
+    reduce[D_O].core_add(0)
     reduce[D_IA].core_add(1)
     reduce[D_IA].core_add(2)
-    entry_back_far()
+    entry_back_near()
     reduce[D_IA].relay()
-    entry_back_near()
     deal_sums()
+    reduce[D_EB].sides()
+    reduce[D_IB].core_add(0)
+    reduce[D_Q].relay()
+    reduce[D_V].core_send()
+    place_grad(D_EA, grad_E)
+    reduce[D_V].core_add(0)
+    reduce[D_V].core_add(1)
+    reduce[D_O].core_add(1)
+    reduce[D_O].core_add(2)
+    lay_in.wait_recv()
+    reduce[D_O].relay()
+    reduce[D_IA].core_add(3)
+    reduce[D_IB].core_add(1)
+    reduce[D_IA].sides()
+    reduce[D_IB].core_add(2)
+    reduce[D_V].core_add(2)
+    grad_R[0:48, :] = reduce[D_R].finish()
+    reduce[D_O].core_add(3)
+    reduce[D_IB].relay()
+    reduce[D_IB].core_add(3)
+    reduce[D_V].core_add(3)
+    place_grad(D_EB, grad_E)
+    reduce[D_V].relay()
     reduce[D_Q].sides()
-    reduce[D_V].core_send()
-    lay_in.wait_recv()
+    grad_out.start()
     reduce[D_O].sides()
-    reduce[D_IA].core_add(3)
-    reduce[D_V].core_add(0)
-    reduce[D_IB].core_add(1)
-    reduce[D_IB].core_add(2)
-    reduce[D_IB].relay()
-    reduce[D_IA].sides()
-    reduce[D_V].core_add(1)
-    reduce[D_V].core_add(2)
-    place_grad(D_EA, grad_E)
-    reduce[D_V].core_add(3)
-    reduce[D_V].relay()
-    reduce[D_IB].core_add(3)
-    grad_out.start()
+    reduce[D_IB].sides()
     grad_R[48:96, :] = reduce[D_Q].finish()
+    place_grad(D_O, grad_O)
     reduce[D_V].sides()
-    grad_R[0:48, :] = reduce[D_R].finish()
-    place_grad(D_O, grad_O)
-    place_grad(D_EB, grad_E)
-    reduce[D_IB].sides()
+    place_grad(D_IB, grad_I)
+    place_grad(D_IA, grad_I)
     grad_V[...] = reduce[D_V].finish()
-    place_grad(D_IA, grad_I)
-    place_grad(D_IB, grad_I)
     take_grad()
     end()
 
@@ -1389,6 +1407,7 @@
         SEEN=vmem((2, 2, 8, 128), jnp.int32),
         AWAY=vmem((2, 8, 128), jnp.int32),
         ROWS=vmem((8, 768), F32),
+        STAGE=vmem((16, 128), F32),
         EB=vmem((1, 3072), F32),
         PB=vmem((1, 2304), F32),
         SUMS=vmem((8, 768), F32),
@@ -1452,21 +1471,42 @@
     return np.concatenate([high, middle, low], axis=0)
 
 
+def hand_over(*refs):
+    given, vectors_in, results, rows = refs[:6], refs[6], refs[7:13], refs[13:22]
+    holds, sems = refs[22:28], refs[28]
+    steps = []
+    for src, hold, dst in zip(given, holds, results):
+        parts = src.shape[0] if len(src.shape) == 3 else 1
+        for part in range(parts):
+            where = part if parts > 1 else slice(None)
+            number = len(steps)
+            steps.append((
+                pltpu.make_async_copy(src.at[where], hold.at[where], sems.at[0, number]),
+                pltpu.make_async_copy(hold.at[where], dst.at[where], sems.at[1, number]),
+            ))
+    for first, _ in steps:
+        first.start()
+    for number in range(VECTORS):
+        slot = number % 4
+        rows[number][...] = vectors_in[number // 4 : number // 4 + 1, 32 * slot : 32 * slot + CHUNK]
+    row = vectors_in[2:3, :]
+    lane = lax.broadcasted_iota(jnp.int32, (1, 128), 1)
+    joined = row
+    for slot in range(1, 4):
+        joined = jnp.where(lane >= CHUNK * slot, pltpu.roll(row, 128 - 8 * slot, 1), joined)
+    rows[8][...] = joined[:, : 4 * CHUNK]
+    for first, second in steps:
+        first.wait()
+        second.start()
+    for _, second in steps:
+        second.wait()
+
+
 def fused_body(
     tokens, visible, lengths, first_gain, first_shift, input_weight, query_bias, value_bias,
     output_weight, output_bias, second_gain, second_shift, expand_weight, expand_bias,
     reduce_weight, reduce_bias, cotangent,
 ):
-    chunks = jnp.concatenate(
-        [
-            jnp.stack(
-                [first_gain, first_shift, query_bias, value_bias, output_bias, second_gain, second_shift, reduce_bias]
-            ),
-            expand_bias.reshape(4, CHUNK),
-        ],
-        axis=0,
-    ).astype(F32)
-    shard_V = jnp.pad(chunks, ((0, 20), (0, 32 - CHUNK))).reshape(8, 128)
     hbm = pl.BlockSpec(memory_space=pl.ANY)
     vmem = pl.BlockSpec(memory_space=pltpu.VMEM)
     smem = pl.BlockSpec(memory_space=pltpu.SMEM)
@@ -1484,7 +1524,7 @@
         fused_kernel,
         name="layer",
         out_shape=results,
-        in_specs=[smem, hbm, hbm, vmem, vmem, vmem, vmem, vmem, vmem, vmem],
+        in_specs=[smem, hbm, hbm] + [vmem] * 15,
         out_specs=[hbm, hbm, vmem, vmem, vmem, vmem, vmem],
         scratch_shapes=[*shapes.values(), *(shape for listed in many.values() for shape in listed)],
         compiler_params=pltpu.CompilerParams(
@@ -1492,12 +1532,29 @@
         ),
     )(
         lengths, tokens[:, 0], cotangent[:, 0], visible, input_weight, output_weight, expand_weight,
-        reduce_weight, shard_V, jnp.asarray(position_table()),
-    )
-    dealt = grad_V.reshape(32, 32)[:12, :CHUNK]
+        reduce_weight, jnp.asarray(position_table()),
+        *(
+            vector.reshape(1, -1)
+            for vector in (
+                first_gain, first_shift, query_bias, value_bias, output_bias, second_gain, second_shift,
+                reduce_bias, expand_bias,
+            )
+        ),
+    )
+    parts = (layer_out, tokens_grad, grad_I, grad_O, grad_E, grad_R)
+    row, long_row = jax.ShapeDtypeStruct((1, CHUNK), F32), jax.ShapeDtypeStruct((1, 4 * CHUNK), F32)
+    layer_out, tokens_grad, grad_I, grad_O, grad_E, grad_R, *rows = pl.pallas_call(
+        hand_over,
+        name="hand_over",
+        out_shape=[jax.ShapeDtypeStruct(part.shape, part.dtype) for part in parts] + [row] * VECTORS + [long_row],
+        in_specs=[hbm] * 6 + [vmem],
+        out_specs=[hbm] * 6 + [vmem] * 9,
+        scratch_shapes=[pltpu.VMEM(part.shape, part.dtype) for part in parts] + [pltpu.SemaphoreType.DMA((2, 12))],
+    )(*parts, grad_V)
+    dealt = [row.reshape(-1) for row in rows]
     return (
         layer_out[:, None], tokens_grad[:, None], dealt[0], dealt[1], grad_I, dealt[2], dealt[3], grad_O,
-        dealt[4], dealt[5], dealt[6], grad_E, dealt[8:12].reshape(4 * CHUNK), grad_R, dealt[7],
+        dealt[4], dealt[5], dealt[6], grad_E, dealt[8], grad_R, dealt[7],
     )
 
 

time: 159 us -> 150 us (0.943)
  local copies, waits for them, and re-layouts: 10.2 us -> 0 us
    unnamed x16 -> x0, local copies, waits for them, and re-layouts: 5.97 us -> none
    pallas_call x0 -> x1, Pallas kernels: none -> 4.39 us  [fused_body(): pl.pallas_call(hand_over, name='hand_over', out_shape=[jax.ShapeDtypeStru...]
    pallas_call x1, Pallas kernels: 148 us -> 145 us  [fused_body(): pl.pallas_call(fused_kernel, name='layer', out_shape=results, in_specs=[s...]
    reshape x4 -> x0, local copies, waits for them, and re-layouts: 2.85 us -> none  [the longest x1 0.85 us: fused_body(): dealt = grad_V.reshape(32, 32)[:12, :CHUNK]]
where the time goes in v3:
time: 150 us
  Pallas kernels  149 us (99%)
    pallas_call x1, Pallas kernels, fused_body(): pl.pallas_call(fused_kernel, name='layer', out_shape=results, in_specs=[s...  145 us
    pallas_call x1, Pallas kernels, fused_body(): pl.pallas_call(hand_over, name='hand_over', out_shape=[jax.ShapeDtypeStru...  4.39 us

profile of v3, /device:TPU:0, one launch (start us, length us, event | category | flops | bytes accessed | tf_op | source)
XLA Modules:
  0.0 150.2 jit_solution(10782854116634295277)
XLA Ops:
  0.7 144.9 %layer.1 = (bf16[4,128,768]{2,1,0:T(8,128)(2,1)}, f32[4,128,768]{2,1,0:T(8,128)}, f32[24,2304]{1,0:T(8,128)}, f32[24,768]{1,0:T(8,128)}, f32[24,3072]{1,0:T(8,12...) custom-call(s32[4]{0:T(128)} %lengths.1, bf16[4,128,768]{2,1,0:T(8,128)(2,1)} %bitcast.26, bf16[4,128,768]{2,1,0:T(8,128)(2,1)} %bitcast.27, ...), custom_call_target="tpu_custom_call" | custom-call | tf_op jit(solution)/shard_map/layer/pallas_call | solution.py:1523
  145.6 4.4 %hand_over.1 = (bf16[4,128,768]{2,1,0:T(8,128)(2,1)}, f32[4,128,768]{2,1,0:T(8,128)}, f32[24,2304]{1,0:T(8,128)}, f32[24,768]{1,0:T(8,128)}, f32[24,3072]{1,0:T(...) custom-call(bf16[4,128,768]{2,1,0:T(8,128)(2,1)} %get-tuple-element., ...), custom_call_target="tpu_custom_call" | custom-call | tf_op jit(solution)/shard_map/hand_over/pallas_call | solution.py:1546

commit v4 on v3

--- a/solution.py
+++ b/solution.py
@@ -367,8 +367,9 @@
 W_I, W_O, W_E, W_R, W_Q, VEC = TENSORS = range(6)
 GATHER_X = (3, 3, 3, 3, None, 2)
 D_IA, D_IB, D_O, D_EA, D_EB, D_R, D_Q, D_V = SUMS = range(8)
-REDUCE_X = (3, 3, 3, 3, 3, 2, None, 2)
-SEMS = 20
+REDUCE_X = (3, 3, 3, 3, 3, 3, None, 2)
+SEMS = 24
+R_ROWS, Q_ROWS = 32, 64
 VECTORS = 8
 
 
@@ -407,6 +408,20 @@
         return self.device(lax.rem(self.z + k, Z_SIZE), self.x, self.c, self.y)
 
     @property
+    def inner(self):
+        return jnp.logical_or(self.z == 1, self.z == 2)
+
+    @property
+    def outer(self):
+        return jnp.logical_or(self.z == 0, self.z == 3)
+
+    def near(self, k):
+        return None if k == 2 else self.z != (0 if k == 3 else 3)
+
+    def at_z(self, z):
+        return self.device(z, self.x, self.c, self.y)
+
+    @property
     def to_x(self):
         return self.device(self.z, 1 - self.x, self.c, self.y)
 
@@ -436,20 +451,37 @@
     )
 
 
+def under(condition, action):
+    if condition is None:
+        action()
+    else:
+        pl.when(condition)(action)
+
+
 class Gather:
     def __init__(self, here, buf, send, recv, share):
         self.here, self.buf, self.send, self.recv = here, buf, send, recv
         self.share = share
         self.open = []
 
-    def copy(self, slot, index, device):
+    def copy(self, slot, index, device, recv=None):
         ref = self.buf.at[slot]
-        return remote(ref, ref, self.send.at[index], self.recv.at[index], device)
-
-    def push(self, slot, index, device):
-        made = self.copy(slot, index, device)
-        made.start()
-        self.open.append(made)
+        recv = index if recv is None else recv
+        return remote(ref, ref, self.send.at[index], self.recv.at[recv], device)
+
+    def push(self, slot, index, device, when=None, recv=None):
+        made = self.copy(slot, index, device, recv)
+        under(when, made.start)
+        self.open.append((made, when))
+
+    def along(self, slot, first):
+        for k in (1, 3, 2):
+            self.push(slot, first + k - 1, self.here.to_z(k), self.here.near(k))
+
+    def hand_on(self, slot, first, index):
+        up = self.here.z == 2
+        device = self.here.at_z(jnp.where(up, 3, 0))
+        self.push(slot, index, device, self.here.inner, first + jnp.where(up, 2, 0))
 
     def pull(self, slot, index):
         self.copy(slot, index, self.here.to_x).wait_recv()
@@ -461,8 +493,7 @@
         return (self.here.z, self.here.column(0, 0, 0))
 
     def begin_z(self):
-        for k in (1, 3, 2):
-            self.push(self.own(), k - 1, self.here.to_z(k))
+        self.along(self.own(), 0)
 
     def begin_x(self):
         self.push(self.own(), 3, self.here.to_x)
@@ -474,6 +505,8 @@
         here = self.here
         slot = (self.behind(k), here.column(0, 0, 0))
         self.pull(slot, k - 1)
+        if k == 2:
+            self.hand_on(slot, 0, 19)
         self.push(slot, 3 + k, here.to_x)
         self.push(slot, 7 + k, here.to_y)
 
@@ -509,8 +542,8 @@
             self.pull((slice(None), here.column(fx, 1, fy)), index)
 
     def drain(self):
-        for made in self.open:
-            made.wait_send()
+        for made, when in self.open:
+            under(when, made.wait_send)
         self.open = []
 
 
@@ -526,8 +559,7 @@
         self.push(self.own(), 1, self.here.to_y)
 
     def along_z(self, column, first):
-        for k in (1, 3, 2):
-            self.push((self.here.z, column), first + k - 1, self.here.to_z(k))
+        self.along((self.here.z, column), first)
 
     def own_along_z(self):
         self.along_z(self.here.column(0, 0, 0), 4)
@@ -551,11 +583,17 @@
         self.pull((here.z, corner, slice(None), right), 3)
         self.along_z(corner, 13)
 
+    def pass_z(self, part):
+        flips = ((0, 0), (1, 0), (0, 1), (1, 1))[part]
+        slot = (self.behind(2), self.here.column(flips[0], 0, flips[1]))
+        self.pull(slot, 5 + 3 * part)
+        self.hand_on(slot, 4 + 3 * part, 20 + part)
+
     def to_core(self, part):
         here = self.here
         flips = ((0, 0), (1, 0), (0, 1), (1, 1))[part]
         column = here.column(flips[0], 0, flips[1])
-        for k in (1, 3, 2):
+        for k in (1, 3):
             self.pull((self.behind(k), column), 4 + 3 * part + k - 1)
         self.push((slice(None), column), 16 + part, here.to_c)
 
@@ -569,17 +607,54 @@
 
 
 class Reduce:
-    def __init__(self, here, part, core, relay, sides, ends, send, recv, share):
+    def __init__(self, here, part, core, relay, sides, ends, middle, send, recv, share):
         self.here, self.part, self.core, self.sides_in, self.ends = here, part, core, sides, ends
+        self.middle = middle
         self.share = share
         self.relay_in = relay
         self.send, self.recv = send, recv
         self.open = []
 
-    def push(self, src, dst, index, device):
+    def push(self, src, dst, index, device, when=None):
         made = remote(src, dst, self.send.at[index], self.recv.at[index], device)
-        made.start()
-        self.open.append(made)
+        under(when, made.start)
+        self.open.append((made, when))
+
+    def across(self, column, ends, middle, first, index):
+        here, z = self.here, self.here.z
+        for k in (1, 3):
+            away = lax.rem(z + k, Z_SIZE)
+            self.push(self.part.at[away, column], ends[k - 1], first + k - 1, here.to_z(k), here.near(k))
+        inner = here.at_z(jnp.where(z == 0, 1, 2))
+        self.push(self.part.at[3 - z, column], middle, index, inner, here.outer)
+        away = lax.rem(z + 2, Z_SIZE)
+        self.push(self.part.at[away, column], ends[1], first + 1, here.to_z(2), here.outer)
+
+    def add_middle(self, column, ends, middle, first, index):
+        here = self.here
+        away = lax.rem(here.z + 2, Z_SIZE)
+
+        def add():
+            self.pull(middle, index)
+            total = self.part[away, column].astype(F32) + middle[...].astype(F32)
+            self.part[away, column] = total.astype(self.part.dtype)
+
+        pl.when(here.inner)(add)
+        self.push(self.part.at[away, column], ends[1], first + 1, here.to_z(2), here.inner)
+
+    def take_ends(self, ends, first):
+        self.pull(ends[1], first + 1)
+        for k, missing in ((1, 0), (3, 3)):
+            ref = ends[k - 1]
+
+            def clear(ref=ref):
+                ref[...] = jnp.zeros(ref.shape, ref.dtype)
+
+            pl.when(self.here.z != missing)(functools.partial(self.pull, ref, first + k - 1))
+            pl.when(self.here.z == missing)(clear)
+
+    def three_ends(self):
+        return [self.ends.at[k] for k in range(3)]
 
     def pull(self, dst, index):
         remote(dst, dst, self.send.at[index], self.recv.at[index], self.here.to_x).wait_recv()
@@ -596,11 +671,12 @@
 
         lax.fori_loop(first, last, one, 0)
 
-    def core_send(self, spare=None):
+    def core_send(self, spare=None, first=0, last=4):
         here = self.here
         if spare is not None:
             pl.semaphore_wait(spare, 1)
-        for index, (fx, fy) in enumerate(QUARTERS):
+        for index in range(first, last):
+            fx, fy = QUARTERS[index]
             self.push(
                 self.part.at[:, here.column(fx, 1, fy)],
                 self.core.at[:, here.quarter(fx, fy)],
@@ -651,22 +727,22 @@
             self.pull(self.sides_in.at[where], index)
         own = here.column(0, 0, 0)
         self.add(own, 0, 4, (self.sides_in, 0), (self.sides_in, 1))
-        for k in (1, 3, 2):
-            away = lax.rem(here.z + k, Z_SIZE)
-            self.push(self.part.at[away, own], self.ends.at[k - 1], 9 + k, here.to_z(k))
+        self.across(own, self.three_ends(), self.middle, 10, 13)
+
+    def pass_z(self):
+        self.add_middle(self.here.column(0, 0, 0), self.three_ends(), self.middle, 10, 13)
 
     def finish(self):
         here = self.here
-        for k in (1, 3, 2):
-            self.pull(self.ends.at[k - 1], 9 + k)
+        self.take_ends(self.three_ends(), 10)
         total = self.part[here.z, here.column(0, 0, 0)].astype(F32)
         for k in range(3):
             total = total + self.ends[k].astype(F32)
         return total
 
     def drain(self):
-        for made in self.open:
-            made.wait_send()
+        for made, when in self.open:
+            under(when, made.wait_send)
         self.open = []
 
 
@@ -677,19 +753,22 @@
         quarter, column = here.quarter(fx, fy), here.column(fx, 0, fy)
         self.pull(self.core.at[:, quarter], index)
         self.add(column, 0, 4, (self.core, quarter))
-        for k in (1, 3, 2):
-            away = lax.rem(here.z + k, Z_SIZE)
-            self.push(
-                self.part.at[away, column], self.ends.at[k - 1, index], 4 + 3 * index + k - 1, here.to_z(k)
-            )
+        self.across(column, self.column_ends(index), self.middle.at[index], 4 + 3 * index, 20 + index)
+
+    def column_ends(self, index):
+        return [self.ends.at[k, index] for k in range(3)]
+
+    def pass_z(self, index):
+        fx, fy = QUARTERS[index]
+        column = self.here.column(fx, 0, fy)
+        self.add_middle(column, self.column_ends(index), self.middle.at[index], 4 + 3 * index, 20 + index)
 
     def relay(self):
         here, part, z = self.here, self.part, self.here.z
         wide = part.shape[-1] // 2
         for index, (fx, fy) in enumerate(QUARTERS):
             column = here.column(fx, 0, fy)
-            for k in (1, 3, 2):
-                self.pull(self.ends.at[k - 1, index], 4 + 3 * index + k - 1)
+            self.take_ends(self.column_ends(index), 4 + 3 * index)
             total = part[z, column].astype(F32)
             for k in range(3):
                 total = total + self.ends[k, index].astype(F32)
@@ -806,8 +885,8 @@
     reduce = []
     for number, (name, cols, landing) in enumerate(PIECES):
         kind = PlaneReduce if name == W_Q else Reduce
-        part, *bufs = [s.P[name], s.R1[name], s.R2[name], s.RZ[name]]
-        core = s.RC[landing]
+        part, *bufs = [s.P[name], s.R1[name], s.R2[name], s.RZ[name], s.RM[name]]
+        core = s.RC[landing].at[:, :, : UNITS[name][0]]
         if cols is not None:
             part, *bufs = [ref.at[(*(slice(None),) * (len(ref.shape) - 1), cols)] for ref in (part, *bufs)]
             core = core.at[:, :, :, : cols.stop - cols.start]
@@ -821,7 +900,7 @@
     seen_out, seen_in = swap(s.AWAY, s.SEEN.at[:, y], s.SEEN.at[:, 1 - y], 1)
     cot_out, cot_in = swap(cotangent.at[other], s.INC.at[:, y], s.INC.at[:, 1 - y], 2)
     lay_out, lay_in = swap(s.TOK.at[:, 1 - y], layer_out.at[mine], layer_out.at[other], 3)
-    grad_out, grad_in = swap(s.INC.at[:, 1 - y], s.TGR, s.TGR, 4)
+    grad_out, grad_in = swap(s.INC.at[:, 1 - y], s.TOK.at[:, y], s.TOK.at[:, 1 - y], 4)
     tok_copy = pltpu.make_async_copy(tokens.at[mine], s.TOK.at[:, y], s.LOC.at[0])
     cot_copy = pltpu.make_async_copy(cotangent.at[mine], s.INC.at[:, y], s.LOC.at[1])
     out_copy = pltpu.make_async_copy(s.TOK.at[:, y], layer_out.at[mine], s.LOC.at[2])
@@ -853,8 +932,8 @@
             half = whole.shape[1] // 2
             unit = jnp.concatenate([whole[:, :half], whole[:, half:]], axis=0)
             s.G[name][z, own] = unit.astype(BF16)
-        s.G[W_R][z, own] = shard_R[0:48, :]
-        s.G[W_Q][z, own] = shard_R[48:96, :]
+        s.G[W_R][z, own] = shard_R[0:R_ROWS, :]
+        s.G[W_Q][z, own] = shard_R[R_ROWS:96, :]
         s.STAGE[...] = jnp.zeros_like(s.STAGE)
         for number, ref in enumerate((v0, v1, v2, v3, v4, v5, v6, v7)):
             s.STAGE[number : number + 1, 0:CHUNK] = ref[...].astype(F32)
@@ -997,17 +1076,16 @@
 
         lax.fori_loop(0, 4, one, 0)
 
-    def reduce_weight_grad():
-        def one(f, carry):
-            zz, xx = f // 2, f % 2
-            moved = s.ACT[:, lanes(384 * f, 384)].T
+    def reduce_weight_grad(xx):
+        def one(zz, carry):
+            moved = s.ACT[:, lanes(768 * zz + 384 * xx, 384)].T
             part = nn(moved, s.INC[...].reshape(512, 768))
             units = part.reshape(4, 96, 768).astype(BF16)
-            s.P[W_R][zz, pl.ds(4 * xx, 4)] = units[:, :48]
-            s.P[W_Q][zz, pl.ds(4 * xx, 4)] = units[:, 48:]
+            s.P[W_R][zz, pl.ds(4 * xx, 4)] = units[:, :R_ROWS]
+            s.P[W_Q][zz, pl.ds(4 * xx, 4)] = units[:, R_ROWS:]
             return carry
 
-        lax.fori_loop(0, 8, one, 0, unroll=2)
+        lax.fori_loop(0, 4, one, 0, unroll=2)
 
     def reduce_rows(zz):
         return jnp.concatenate([s.G[W_R][zz], s.G[W_Q][zz]], axis=1).reshape(768, 768)
@@ -1175,212 +1253,239 @@
     def take_grad():
         grad_in.wait_recv()
         for it in range(2):
-            s.ENT[rows_at(256 * it + 128 * (1 - y), 128), :] = s.TGR[it].astype(F32)
+            s.ENT[rows_at(256 * it + 128 * (1 - y), 128), :] = s.TOK[it, 1 - y].astype(F32)
         for copy in far_copies:
             copy.start()
 
+    def free_tokens():
+        lay_out.wait_send()
+        out_copy.wait()
+        lay_in.wait_recv()
+        pl.semaphore_signal(s.SPARE.at[4], inc=1, device_id=here.to_y, device_id_type=MESH)
+
+    def send_grad():
+        pl.semaphore_wait(s.SPARE.at[4], 1)
+        grad_out.start()
+
     def end():
-        for made in (seen_out, lay_out, grad_out):
+        for made in (seen_out, grad_out):
             made.wait_send()
-        out_copy.wait()
         for copy in near_copies + far_copies:
             copy.wait()
         for one in (*gather, *reduce):
             one.drain()
 
     start()
-    tok_out.start()
-    gather[VEC].begin_x()
+    gather[W_I].begin_x()
     gather[W_O].begin_x()
-    gather[VEC].begin_z()
-    gather[VEC].begin_y()
-    gather[W_O].begin_y()
-    seen_out.start()
+    gather[W_E].begin_y()
+    gather[W_Q].begin_x()
     gather[W_E].begin_x()
     gather[W_I].begin_y()
-    gather[W_Q].begin_x()
-    gather[W_I].begin_x()
     gather[W_I].begin_z()
+    gather[W_Q].begin_y()
+    gather[W_I].relay(0)
+    gather[W_O].begin_y()
+    tok_out.start()
+    gather[W_I].pass_on(2)
+    gather[VEC].begin_z()
     gather[W_I].pass_on(1)
-    gather[VEC].relay(0)
     gather[W_O].begin_z()
+    gather[VEC].begin_y()
+    gather[W_I].pass_on(3)
+    gather[W_I].own_to_core()
+    gather[W_E].begin_z()
+    gather[VEC].begin_x()
+    gather[VEC].pass_on(2)
+    seen_out.start()
+    gather[W_E].relay(0)
+    gather[VEC].pass_on(3)
+    gather[W_O].pass_on(1)
     gather[VEC].pass_on(1)
-    gather[W_E].begin_z()
-    gather[W_I].pass_on(3)
-    gather[VEC].pass_on(2)
-    gather[W_I].pass_on(2)
-    seen_in.wait_recv()
-    gather[VEC].pass_on(3)
-    gather[W_I].relay(0)
-    gather[VEC].relay(1)
-    gather[W_Q].own_along_z()
-    gather[W_E].begin_y()
-    gather[VEC].own_to_core()
-    gather[W_I].relay(1)
-    gather[W_I].relay(3)
-    gather[W_Q].begin_y()
-    gather[W_O].pass_on(1)
+    gather[W_O].pass_on(2)
+    gather[W_Q].relay()
     tok_copy.wait()
     tok_in.wait_recv()
     gather[W_I].relay(2)
+    gather[VEC].relay(0)
+    gather[W_O].pass_on(3)
     gather[VEC].relay(3)
+    gather[W_I].relay(3)
+    gather[W_I].relay(1)
+    gather[VEC].relay(1)
+    gather[VEC].own_to_core()
     gather[VEC].relay(2)
-    gather[W_O].pass_on(3)
-    gather[W_O].pass_on(2)
+    gather[W_I].sides_to_core()
+    gather[W_O].relay(0)
+    gather[W_E].pass_on(2)
     gather[W_R].begin_z()
-    gather[W_I].sides_to_core()
-    gather[W_E].relay(0)
-    gather[W_E].pass_on(3)
     gather[W_E].pass_on(1)
     gather[VEC].sides_to_core()
+    gather[W_E].pass_on(3)
+    gather[W_O].relay(1)
     gather[W_O].relay(3)
-    gather[W_E].pass_on(2)
+    gather[W_Q].pass_z(1)
+    gather[VEC].corner()
+    gather[VEC].from_core()
+    seen_in.wait_recv()
+    gather[W_R].begin_y()
+    vectors()
+    gather[W_O].relay(2)
     gather[W_I].corner()
-    gather[VEC].corner()
-    gather[W_I].own_to_core()
+    gather[W_O].sides_to_core()
+    gather[W_Q].corner()
+    gather[W_I].from_core()
+    gather[W_Q].pass_z(2)
+    gather[W_E].relay(1)
+    spread_rows(W_I, s.WI)
+    gather[W_O].own_to_core()
+    first_norm()
     gather[W_E].own_to_core()
+    gather[W_E].relay(2)
+    gather[W_R].begin_x()
+    gather[W_Q].to_core(1)
+    gather[W_R].pass_on(2)
+    project()
+    gather[W_O].corner()
     gather[W_E].relay(3)
-    gather[W_O].relay(2)
-    gather[VEC].from_core()
-    vectors()
-    gather[W_O].relay(1)
-    gather[W_O].relay(0)
-    gather[W_I].from_core()
-    gather[W_O].own_to_core()
-    gather[W_R].begin_y()
-    gather[W_O].sides_to_core()
-    spread_rows(W_I, s.WI)
-    first_norm()
-    gather[W_Q].relay()
-    gather[W_E].relay(1)
-    project()
     attend(0, 6)
-    gather[W_E].relay(2)
+    cot_out.start()
+    gather[W_Q].pass_z(3)
     gather[W_E].sides_to_core()
-    gather[W_R].begin_x()
-    gather[W_R].pass_on(2)
-    gather[W_O].corner()
+    gather[W_O].from_core()
+    gather[W_Q].own_along_z()
+    attend(6, 12)
+    gather[W_E].corner()
+    gather[W_R].pass_on(3)
+    spread_rows(W_O, s.WO)
+    second_norm()
+    gather[W_Q].to_core(2)
+    gather[W_R].relay(0)
+    gather[W_Q].to_core(3)
     gather[W_R].pass_on(1)
-    attend(6, 12)
-    gather[W_Q].corner()
-    gather[W_R].pass_on(3)
-    cot_out.start()
-    gather[W_E].corner()
-    gather[W_Q].to_core(0)
-    gather[W_O].from_core()
-    spread_rows(W_O, s.WO)
-    gather[W_Q].to_core(1)
-    second_norm()
-    gather[W_R].relay(0)
+    gather[W_R].own_to_core()
+    gather[W_R].relay(2)
     gather[W_E].from_core()
     spread_rows(W_E, s.WE)
     expand(0, 4)
-    gather[W_R].relay(2)
+    gather[W_Q].pass_z(0)
     expand(4, 8)
+    gather[W_R].relay(1)
     gather[W_R].relay(3)
-    gather[W_R].relay(1)
-    gather[W_Q].to_core(2)
     cot_copy.wait()
     cot_in.wait_recv()
+    gather[W_Q].to_core(0)
     gather[W_R].sides_to_core()
-    gather[W_R].own_to_core()
-    gather[W_Q].to_core(3)
     take_in()
+    reduce_weight_grad(1 - x)
+    reduce[D_R].core_send(None, 0, 2)
     gather[W_R].corner()
-    reduce_weight_grad()
-    reduce[D_R].core_send()
+    reduce_weight_grad(x)
+    reduce[D_R].core_add(0)
+    reduce[D_R].core_send(None, 2, 4)
+    reduce[D_Q].core_send(None, 2, 4)
     gather[W_Q].from_core()
+    reduce[D_R].core_add(1)
+    reduce[D_Q].core_send(None, 0, 2)
     gather[W_R].from_core()
     expanded_grad(0, 4)
-    reduce[D_R].core_add(0)
-    reduce[D_Q].core_send()
+    reduce[D_R].core_add(2)
     expanded_grad(4, 8)
-    reduce[D_R].core_add(1)
-    reduce[D_R].core_add(2)
+    weight_grad(W_E, s.SECT, s.GP, 0, 2)
+    reduce[D_Q].core_add(0)
     reduce[D_R].core_add(3)
     give_spare(0)
-    reduce[D_Q].core_add(0)
-    weight_grad(W_E, s.SECT, s.GP, 0, 2)
+    reduce[D_R].relay()
+    reduce[D_EA].core_send(s.SPARE.at[0])
+    weight_grad(W_E, s.SECT, s.GP, 2, 4)
+    reduce[D_EA].core_add(0)
+    finish_rows()
+    lay_out.start()
     reduce[D_Q].core_add(1)
-    reduce[D_EA].core_send(s.SPARE.at[0])
-    reduce[D_R].relay()
+    reduce[D_EA].core_add(1)
     reduce[D_Q].core_add(2)
-    finish_rows()
-    reduce[D_EA].core_add(0)
-    weight_grad(W_E, s.SECT, s.GP, 2, 4)
-    lay_out.start()
-    reduce[D_EA].core_add(1)
-    middle_back()
+    reduce[D_Q].pass_z(0)
     reduce[D_Q].core_add(3)
     give_spare(1)
     reduce[D_EB].core_send(s.SPARE.at[1])
+    middle_back()
+    reduce[D_EB].core_add(0)
+    reduce[D_EB].core_add(1)
     weight_grad(W_O, s.ATTT, s.XB, 0, 1)
     reduce[D_EA].core_add(2)
     attended_back()
     reduce[D_EA].relay()
-    reduce[D_EB].core_add(0)
-    reduce[D_R].sides()
+    reduce[D_O].core_send()
     attend_back(0, 6)
-    reduce[D_EB].core_add(1)
     attend_back(6, 12)
+    reduce[D_EB].core_add(2)
+    reduce[D_EB].relay()
     weight_grad(W_I, s.NRMT, s.PRJ, 0, 2)
-    reduce[D_EB].core_add(2)
+    reduce[D_O].core_add(0)
     weight_grad(W_I, s.NRMT, s.PRJ, 2, 3)
-    reduce[D_EB].relay()
     reduce[D_EA].core_add(3)
     give_spare(2)
     reduce[D_IA].core_send(s.SPARE.at[2])
+    reduce[D_Q].pass_z(2)
+    reduce[D_O].core_add(1)
+    reduce[D_Q].pass_z(1)
     reduce[D_EA].sides()
+    free_tokens()
+    reduce[D_IA].core_add(0)
     reduce[D_EB].core_add(3)
     give_spare(3)
-    reduce[D_IA].core_add(0)
+    reduce[D_R].sides()
+    entry_back_far()
+    reduce[D_O].core_add(2)
+    reduce[D_IA].core_add(1)
+    reduce[D_Q].pass_z(3)
     reduce[D_IB].core_send(s.SPARE.at[3])
-    reduce[D_O].core_send()
-    entry_back_far()
-    reduce[D_O].core_add(0)
-    reduce[D_IA].core_add(1)
     reduce[D_IA].core_add(2)
+    reduce[D_O].relay()
     entry_back_near()
+    reduce[D_IB].core_add(0)
+    reduce[D_R].pass_z()
+    reduce[D_EB].sides()
     reduce[D_IA].relay()
     deal_sums()
-    reduce[D_EB].sides()
-    reduce[D_IB].core_add(0)
+    reduce[D_V].core_send()
+    reduce[D_V].core_add(0)
+    reduce[D_EB].pass_z()
+    reduce[D_V].core_add(1)
+    reduce[D_O].core_add(3)
+    reduce[D_IB].core_add(1)
+    reduce[D_IB].core_add(2)
+    reduce[D_IA].core_add(3)
+    reduce[D_IB].core_add(3)
+    reduce[D_EA].pass_z()
+    reduce[D_V].core_add(2)
     reduce[D_Q].relay()
-    reduce[D_V].core_send()
+    reduce[D_O].sides()
+    reduce[D_IB].relay()
+    reduce[D_V].core_add(3)
+    reduce[D_IA].sides()
+    reduce[D_V].relay()
+    send_grad()
+    grad_R[0:R_ROWS, :] = reduce[D_R].finish()
+    reduce[D_IA].pass_z()
+    reduce[D_O].pass_z()
+    reduce[D_IB].sides()
+    reduce[D_V].sides()
+    place_grad(D_IA, grad_I)
     place_grad(D_EA, grad_E)
-    reduce[D_V].core_add(0)
-    reduce[D_V].core_add(1)
-    reduce[D_O].core_add(1)
-    reduce[D_O].core_add(2)
-    lay_in.wait_recv()
-    reduce[D_O].relay()
-    reduce[D_IA].core_add(3)
-    reduce[D_IB].core_add(1)
-    reduce[D_IA].sides()
-    reduce[D_IB].core_add(2)
-    reduce[D_V].core_add(2)
-    grad_R[0:48, :] = reduce[D_R].finish()
-    reduce[D_O].core_add(3)
-    reduce[D_IB].relay()
-    reduce[D_IB].core_add(3)
-    reduce[D_V].core_add(3)
+    reduce[D_V].pass_z()
+    reduce[D_Q].sides()
+    place_grad(D_O, grad_O)
+    reduce[D_IB].pass_z()
+    grad_V[...] = reduce[D_V].finish()
+    place_grad(D_IB, grad_I)
+    take_grad()
     place_grad(D_EB, grad_E)
-    reduce[D_V].relay()
-    reduce[D_Q].sides()
-    grad_out.start()
-    reduce[D_O].sides()
-    reduce[D_IB].sides()
-    grad_R[48:96, :] = reduce[D_Q].finish()
-    place_grad(D_O, grad_O)
-    reduce[D_V].sides()
-    place_grad(D_IB, grad_I)
-    place_grad(D_IA, grad_I)
-    grad_V[...] = reduce[D_V].finish()
-    take_grad()
+    grad_R[R_ROWS:96, :] = reduce[D_Q].finish()
     end()
 
 
-UNITS = ((48, 1152), (48, 384), (48, 1536), (48, 768), (48, 768), (8, 128))
+UNITS = ((48, 1152), (48, 384), (48, 1536), (R_ROWS, 768), (Q_ROWS, 768), (8, 128))
 
 
 PIECES = (
@@ -1401,7 +1506,7 @@
         SWS=dma((5,)),
         SWR=dma((5,)),
         LOC=dma((7,)),
-        SPARE=pltpu.SemaphoreType.REGULAR((4,)),
+        SPARE=pltpu.SemaphoreType.REGULAR((5,)),
         TOK=vmem((2, 2, 128, 768), BF16),
         INC=vmem((2, 2, 128, 768), BF16),
         SEEN=vmem((2, 2, 8, 128), jnp.int32),
@@ -1425,9 +1530,8 @@
         ATN=vmem((24, 256, 256), BF16),
         ACT=vmem((512, 3072), BF16),
         GP=vmem((512, 3072), BF16),
-        TGR=vmem((2, 128, 768), BF16),
-    )
-    many = dict(G=[], GS=[], GQ=[], P=[], RC=[], R1=[], R2=[], RZ=[], RS=[], RQ=[])
+    )
+    many = dict(G=[], GS=[], GQ=[], P=[], RC=[], R1=[], R2=[], RZ=[], RM=[], RS=[], RQ=[])
     for name in TENSORS:
         kind = F32 if name == VEC else BF16
         unit = UNITS[name]
@@ -1438,10 +1542,12 @@
         if name in (W_R, W_Q, VEC):
             many["P"].append(vmem((4, 8, *unit), kind))
         if name not in (W_I, W_E):
-            many["RC"].append(vmem((4, 4, *unit), kind))
+            room = (max(unit[0], 48), unit[1]) if name == W_R else unit
+            many["RC"].append(vmem((4, 4, *room), kind))
         many["R1"].append(vmem(unit if plane else (4, *unit), kind))
         many["R2"].append(vmem((2, *unit) if plane else (4, 2, *unit), kind))
         many["RZ"].append(vmem((3, 4, *unit) if plane else (3, *unit), kind))
+        many["RM"].append(vmem((4, *unit) if plane else unit, kind))
     for _ in SUMS:
         many["RS"].append(dma((SEMS,)))
         many["RQ"].append(dma((SEMS,)))

time: 150 us -> 148 us (0.987)
  Pallas kernels: 149 us -> 147 us
    pallas_call x1, Pallas kernels: 145 us -> 142 us  [fused_body(): pl.pallas_call(fused_kernel, name='layer', out_shape=results, in_specs=[s...]
where the time goes in v4:
time: 148 us; the launch traced here: 147 us
  Pallas kernels  147 us (99%)
    pallas_call x1, Pallas kernels, fused_body(): pl.pallas_call(fused_kernel, name='layer', out_shape=results, in_specs=[s...  142 us
    pallas_call x1, Pallas kernels, fused_body(): pl.pallas_call(hand_over, name='hand_over', out_shape=[jax.ShapeDtypeStru...  4.39 us

profile of v4, /device:TPU:0, one launch (start us, length us, event | category | flops | bytes accessed | tf_op | source)
XLA Modules:
  0.0 147.5 jit_solution(13765126219244358152)
XLA Ops:
  0.7 142.2 %layer.1 = (bf16[4,128,768]{2,1,0:T(8,128)(2,1)}, f32[4,128,768]{2,1,0:T(8,128)}, f32[24,2304]{1,0:T(8,128)}, f32[24,768]{1,0:T(8,128)}, f32[24,3072]{1,0:T(8,12...) custom-call(s32[4]{0:T(128)} %lengths.1, bf16[4,128,768]{2,1,0:T(8,128)(2,1)} %bitcast.26, bf16[4,128,768]{2,1,0:T(8,128)(2,1)} %bitcast.27, ...), custom_call_target="tpu_custom_call" | custom-call | tf_op jit(solution)/shard_map/layer/pallas_call | solution.py:1629
  142.9 4.4 %hand_over.1 = (bf16[4,128,768]{2,1,0:T(8,128)(2,1)}, f32[4,128,768]{2,1,0:T(8,128)}, f32[24,2304]{1,0:T(8,128)}, f32[24,768]{1,0:T(8,128)}, f32[24,3072]{1,0:T(...) custom-call(bf16[4,128,768]{2,1,0:T(8,128)(2,1)} %get-tuple-element., ...), custom_call_target="tpu_custom_call" | custom-call | tf_op jit(solution)/shard_map/hand_over/pallas_call | solution.py:1652

commit v5 on v4

--- a/solution.py
+++ b/solution.py
@@ -1581,10 +1581,13 @@
     given, vectors_in, results, rows = refs[:6], refs[6], refs[7:13], refs[13:22]
     holds, sems = refs[22:28], refs[28]
     steps = []
-    for src, hold, dst in zip(given, holds, results):
-        parts = src.shape[0] if len(src.shape) == 3 else 1
-        for part in range(parts):
-            where = part if parts > 1 else slice(None)
+    for which in (1, 0, 4, 5, 2, 3):
+        src, hold, dst = given[which], holds[which], results[which]
+        if len(src.shape) == 3:
+            places = [(part, slice(first, first + 64)) for part in range(4) for first in (0, 64)]
+        else:
+            places = [slice(None)]
+        for where in places:
             number = len(steps)
             steps.append((
                 pltpu.make_async_copy(src.at[where], hold.at[where], sems.at[0, number]),
@@ -1655,7 +1658,7 @@
         out_shape=[jax.ShapeDtypeStruct(part.shape, part.dtype) for part in parts] + [row] * VECTORS + [long_row],
         in_specs=[hbm] * 6 + [vmem],
         out_specs=[hbm] * 6 + [vmem] * 9,
-        scratch_shapes=[pltpu.VMEM(part.shape, part.dtype) for part in parts] + [pltpu.SemaphoreType.DMA((2, 12))],
+        scratch_shapes=[pltpu.VMEM(part.shape, part.dtype) for part in parts] + [pltpu.SemaphoreType.DMA((2, 20))],
     )(*parts, grad_V)
     dealt = [row.reshape(-1) for row in rows]
     return (

time: 148 us -> 148 us (level)
  no operation moved by 1% of the time
where the time goes in v5:
time: 148 us
  Pallas kernels  147 us (99%)
    pallas_call x1, Pallas kernels, fused_body(): pl.pallas_call(fused_kernel, name='layer', out_shape=results, in_specs=[s...  142 us
    pallas_call x1, Pallas kernels, fused_body(): pl.pallas_call(hand_over, name='hand_over', out_shape=[jax.ShapeDtypeStru...  4.52 us

profile of v5, /device:TPU:0, one launch (start us, length us, event | category | flops | bytes accessed | tf_op | source)
XLA Modules:
  0.0 147.6 jit_solution(14697954722821869127)
XLA Ops:
  0.7 142.2 %layer.1 = (bf16[4,128,768]{2,1,0:T(8,128)(2,1)}, f32[4,128,768]{2,1,0:T(8,128)}, f32[24,2304]{1,0:T(8,128)}, f32[24,768]{1,0:T(8,128)}, f32[24,3072]{1,0:T(8,12...) custom-call(s32[4]{0:T(128)} %lengths.1, bf16[4,128,768]{2,1,0:T(8,128)(2,1)} %bitcast.26, bf16[4,128,768]{2,1,0:T(8,128)(2,1)} %bitcast.27, ...), custom_call_target="tpu_custom_call" | custom-call | tf_op jit(solution)/shard_map/layer/pallas_call | solution.py:1632
  142.9 4.5 %hand_over.1 = (bf16[4,128,768]{2,1,0:T(8,128)(2,1)}, f32[4,128,768]{2,1,0:T(8,128)}, f32[24,2304]{1,0:T(8,128)}, f32[24,768]{1,0:T(8,128)}, f32[24,3072]{1,0:T(...) custom-call(bf16[4,128,768]{2,1,0:T(8,128)(2,1)} %get-tuple-element., ...), custom_call_target="tpu_custom_call" | custom-call | tf_op jit(solution)/shard_map/hand_over/pallas_call | solution.py:1655
